TPU v7x, 32 devices: a whole 2x2x4 slice. The times are simulated.
32 devices in a mesh: dp: 8 (over y, x, core), feat: 4 (over z).
Axes of the slice: x: 2, y: 2, z: 4, core: 2. Of those that a mesh axis runs over, the one named last changes fastest.
Arguments:
- samples: bfloat16 [6144, 256], P('dp'), may hold values from -6 to 6
- targets: bfloat16 [6144], P('dp'), may hold values from -6 to 6
- counts: int32 [8], replicated, may hold values from 1 to 768, 3072 in all
- bucket_ids: int32 [3, 256], replicated, may hold values from 0 to 4095
- sign_bits: int32 [3, 256], replicated, may hold values from 0 to 1
Outputs:
- gram: float32 [4096, 4096], P('dp', 'feat')
- zty: float32 [4096], P('feat')
Inputs may be any that keep to these rules, and one draw needn't show every extreme that they name: The counts sum to 3072, and some index of dp has exactly 768 live rows.
All inputs are finite; a program needn't handle non-finite values.
Results may differ from a plain program's by a relative error of at most 0.0048.
Values may be sent and summed in bfloat16 or wider, within the bound.
No kernel may reach another device: no remote copies, remote signals or barrier semaphores. Data moves between devices by JAX's collectives and lax.ppermute only.
A program may use at most 64 MiB of HBM per device.

v0:
```python
import math

import jax
import jax.numpy as jnp
from jax import lax
from jax.sharding import PartitionSpec as P

DIN = 256
SK = 4096
BAL_DEV = 384


def inverse_terms(spectra_pair, freq_ids, column_ids):
    turns = freq_ids[:, None] * column_ids[None, :] % SK
    angles = turns.astype(jnp.float32) * (2.0 * math.pi / SK)
    cosine = jnp.cos(angles).astype(jnp.bfloat16)
    sine = jnp.sin(angles).astype(jnp.bfloat16)
    first_term = jnp.einsum(
        "fc,rf->cr", cosine, spectra_pair[0], preferred_element_type=jnp.float32
    )
    second_term = jnp.einsum("fc,rf->cr", sine, spectra_pair[1], preferred_element_type=jnp.float32)
    return first_term - second_term


def complex_times(real_a, imag_a, real_b, imag_b):
    return (real_a * real_b - imag_a * imag_b, real_a * imag_b + imag_a * real_b)


def body(samples, targets, counts, bucket_ids, sign_bits):
    device_row = lax.axis_index("dp")
    dp_count = lax.axis_size("dp")
    local_count = counts[device_row]
    row_ends = jnp.cumsum(counts)
    first_row = row_ends[device_row] - local_count
    global_pos = jnp.arange(dp_count * BAL_DEV, dtype=jnp.int32)
    local_pos = global_pos - first_row
    usable = (local_pos >= 0) & (local_pos < local_count)
    clipped = jnp.clip(local_pos, 0, samples.shape[0] - 1)
    send_mask = usable.astype(jnp.bfloat16)
    sent_rows = (jnp.take(samples, clipped, axis=0) * send_mask[:, None]).reshape(
        dp_count, BAL_DEV, samples.shape[1]
    )
    sent_targets = (jnp.take(targets, clipped, axis=0) * send_mask).reshape(dp_count, BAL_DEV)
    got_rows, got_targets = (
        lax.all_to_all(sent_rows, "dp", split_axis=0, concat_axis=0, tiled=True),
        lax.all_to_all(sent_targets, "dp", split_axis=0, concat_axis=0, tiled=True),
    )
    own_rows = jnp.sum(got_rows, axis=0)
    own_targets = jnp.sum(got_targets, axis=0)
    live_mask = jnp.ones((BAL_DEV,), jnp.float32)
    values = own_rows.astype(jnp.float32)
    normed = (
        values
        * lax.rsqrt(jnp.mean(values * values, axis=-1, keepdims=True) + 1e-06)
        * DIN ** (-0.5)
    )
    normed = normed * live_mask[:, None]
    freq_panel = SK // lax.axis_size("feat")
    own_ids = lax.axis_index("feat") * freq_panel + jnp.arange(freq_panel, dtype=jnp.int32)
    turns = bucket_ids[:, :, None] * own_ids[None, None, :] % SK
    angles = turns.astype(jnp.float32) * (2.0 * math.pi / SK)
    signed = (2 * sign_bits - 1).astype(jnp.float32)[:, :, None]
    table = jnp.stack([signed * jnp.cos(angles), -signed * jnp.sin(angles)], axis=1)
    table = jnp.transpose(table, (2, 0, 1, 3)).reshape(DIN, 6 * freq_panel)
    spectrum_all = jnp.dot(
        normed, table, precision=lax.Precision.HIGHEST, preferred_element_type=jnp.float32
    )
    spectrum_all = spectrum_all.reshape(normed.shape[0], 3, 2, freq_panel)
    real_mix, imag_mix = complex_times(
        spectrum_all[:, 0, 0], spectrum_all[:, 0, 1], spectrum_all[:, 1, 0], spectrum_all[:, 1, 1]
    )
    real_mix, imag_mix = complex_times(
        real_mix, imag_mix, spectrum_all[:, 2, 0], spectrum_all[:, 2, 1]
    )
    spectra_pair = jnp.stack([real_mix.astype(jnp.bfloat16), imag_mix.astype(jnp.bfloat16)], axis=0)
    portion = lax.all_gather(spectra_pair, "feat", axis=2, tiled=True)
    freq_ids = jnp.arange(portion.shape[2], dtype=jnp.int32)
    summed = inverse_terms(portion, freq_ids, own_ids)
    features = (summed * SK ** (-0.5)).astype(jnp.bfloat16)
    partial_gram = lax.dot_general(
        lax.all_gather(features, "feat", axis=0, tiled=True),
        features,
        (((1,), (1,)), ((), ())),
        preferred_element_type=jnp.float32,
    )
    gram_local = lax.psum_scatter(partial_gram, "dp", scatter_dimension=0, tiled=True)
    target_part = lax.dot_general(
        features, own_targets, (((1,), (0,)), ((), ())), preferred_element_type=jnp.float32
    )
    target_sum = lax.psum(target_part, "dp")
    total_rows = BAL_DEV * lax.axis_size("dp")
    return (gram_local / total_rows, target_sum * total_rows ** (-0.5))


def solution(mesh):
    placed = (P("dp", None), P("dp"), P(), P(), P())
    return jax.shard_map(
        body, mesh=mesh, in_specs=placed, out_specs=(P("dp", "feat"), P("feat")), check_vma=False
    )
```

profile of v0, /device:TPU:0, one launch (start us, length us, event | category | flops | bytes accessed | tf_op | source)
XLA Modules:
  0.0 524.6 jit_solution(6853592128375638644)
XLA Ops:
  7.2 0.0 copy-start
  7.2 1.3 dynamic_slice.7
  8.5 0.8 reduce-window.4
  9.3 0.6 constant_dynamic-slice_fusion
  11.1 0.6 fusion.32
  11.8 0.0 copy-done
  11.8 11.1 %gather_fusion = bf16[3072,256]{1,0:T(8,128)(2,1)S(1)} fusion(bf16[768,256]{1,0:T(8,128)(2,1)S(1)} %copy-done, s32[3072]{0:T(1024)S(1)} %broadcast_clamp_fusion), kind=kCustom, calls=%fused_computation | custom fusion | bytes 3158016 | tf_op jit(solution)/shard_map/jit(_take)/gather | solution.py:40
  22.8 0.0 copy-start.3
  22.8 2.3 select_multiply_fusion
  25.1 5.2 all-to-all-start
  30.3 0.0 all-gather.3.cloned.1.call-start
  30.4 14.9 %cosine_multiply_fusion = (f32[3,1,256,1024]{2,3,1,0:T(8,128)S(1)}, f32[3,1,256,1024]{2,3,1,0:T(8,128)}) fusion(s32[1024]{0:T(1024)S(1)} %iota_add_fusion, s32[3,256]{1,0:T(4,128)} %param.8, f32[3,256]{1,0:T(4,128)S(1)} %add_convert_fusion.1, f32[3,256]{1,0:T(4,128)S(1)} %fusion.49), kind=kLoop, calls=%fused_computation.30 | loop fusion | flops 12582912 | bytes 6304768 | tf_op jit(solution)/shard_map/mul | solution.py:63
  45.3 6.1 %all-to-all-done = bf16[8,384,256]{2,1,0:T(8,128)(2,1)} async-done(((bf16[8,384,256]{2,1,0:T(8,128)(2,1)}), bf16[8,384,256]{2,1,0:T(8,128)(2,1)}, u32[]{:S(2)}, u32[]{:S(2)}) %all-to-all-start) | async-done | bytes 1572896 | tf_op jit(solution)/shard_map/all_to_all | solution.py:45
  51.4 2.4 reduce_sum.33
  53.8 1.1 fusion.18
  54.9 10.6 %fusion.10 = f32[384,3,2,1024]{3,0,2,1:T(8,128)S(1)} fusion(f32[3,1,256,1024]{2,3,1,0:T(8,128)} %get-tuple-element.6, f32[3,1,256,1024]{2,3,1,0:T(8,128)S(1)} %get-tuple-element.5, bf16[384,256]{1,0:T(8,128)(2,1)} %reduce_sum.33, f32[384]{0:T(512)S(1)} %add_rsqrt_fusion), kind=kOutput, calls=%fused_computation.16 | convolution fusion | flops 7249625088 | bytes 15926784 | tf_op jit(solution)/shard_map/dot_general | solution.py:65
  65.5 1.6 fusion.16
  67.0 0.8 fusion.17
  67.8 1.3 pad_maximum_fusion
  69.1 0.0 all-gather.3.cloned.1.call-update
  69.1 0.0 all-gather.5.cloned.1.call-start
  69.1 115.3 %all-gather.3.cloned.1.call-done = bf16[2,384,4096]{2,1,0:T(8,128)(2,1)} async-done(((bf16[2,384,1024]{2,1,0:T(8,128)(2,1)}), bf16[2,384,4096]{2,1,0:T(8,128)(2,1)}) %all-gather.3.cloned.1.call-update) | async-done | bytes 6291472 | tf_op jit(solution)/shard_map/all_gather | solution.py:76
  184.5 2.2 slice_bitcast_fusion.12
  186.7 0.0 slice-start.1
  186.7 74.1 %fusion.6 = f32[1024,384]{1,0:T(8,128)S(1)} fusion(s32[1024]{0:T(1024)S(1)} %iota_add_fusion, bf16[384,4096]{1,0:T(8,128)(2,1)S(1)} %slice_bitcast_fusion.12), kind=kOutput, calls=%fused_computation.13 | convolution fusion | flops 3284140032 | bytes 4722688 | tf_op jit(solution)/shard_map/fc,rf->cr/dot_general | solution.py:18
  260.9 0.0 slice-done
  260.9 0.0 slice-done.1
  260.9 0.3 slice_bitcast_fusion.13
  261.3 64.2 %multiply_convert_fusion = bf16[1024,384]{1,0:T(8,128)(2,1)} fusion(f32[1024,384]{1,0:T(8,128)S(1)} %fusion.6, s32[1024]{0:T(1024)S(1)} %iota_add_fusion, bf16[384,4096]{1,0:T(8,128)(2,1)S(1)} %slice_bitcast_fusion.13), kind=kOutput, calls=%fused_computation.32 | convolution fusion | flops 3285319680 | bytes 5509120 | tf_op jit(solution)/shard_map/fc,rf->cr/dot_general | solution.py:21
  325.5 0.0 all-gather.5.cloned.1.call-update
  325.5 0.0 reduce-scatter.2.cloned.1.call-start
  325.6 61.8 %all-gather.5.cloned.1.call-done = bf16[4096,384]{1,0:T(8,128)(2,1)} async-done(((bf16[1024,384]{1,0:T(8,128)(2,1)}), bf16[4096,384]{1,0:T(8,128)(2,1)}) %all-gather.5.cloned.1.call-update) | async-done | bytes 3145744 | tf_op jit(solution)/shard_map/all_gather | solution.py:81
  387.4 12.4 %fusion.50 = f32[4096,1024]{1,0:T(8,128)} fusion(bf16[4096,384]{1,0:T(8,128)(2,1)} %all-gather.5.cloned.1.call-done, bf16[1024,384]{1,0:T(8,128)(2,1)} %multiply_convert_fusion), kind=kOutput, calls=%fused_computation.85 | convolution fusion | flops 3221225472 | bytes 20709376 | tf_op jit(solution)/shard_map/dot_general | solution.py:80
  399.7 0.0 reduce-scatter.2.cloned.1.call-update
  399.7 0.7 copy-done.1
  400.4 19.3 %gather_fusion.1 = bf16[3072]{0:T(1024)(128)(2,1)S(1)} fusion(bf16[768]{0:T(1024)(128)(2,1)S(1)} %copy-done.1, s32[3072]{0:T(1024)S(1)} %broadcast_clamp_fusion), kind=kCustom, calls=%fused_computation.1 | custom fusion | bytes 24576 | tf_op jit(solution)/shard_map/jit(_take)/gather | solution.py:43
  419.8 0.6 fusion.38
  420.4 0.5 broadcast.363
  420.9 0.7 reduce.3
  421.5 0.1 reshape.382
  421.6 8.2 %all_to_all.11 = bf16[8,2,192]{2,1,0:T(2,128)(2,1)S(1)} all-to-all(bf16[8,2,192]{2,1,0:T(2,128)(2,1)S(1)} %reshape.382), channel_id=1, replica_groups=mesh['dp'=8,'feat'=4] {'dp'}, dimensions={0} | all-to-all | bytes 12288 | tf_op jit(solution)/shard_map/all_to_all | solution.py:46
  429.8 0.1 reshape.383
  429.9 0.0 copy-done.2
  429.9 0.3 fusion.51
  430.2 12.4 %psum.7 = f32[1024]{0:T(1024)S(1)} all-reduce(f32[1024]{0:T(1024)S(1)} %bitcast.50), channel_id=1, replica_groups=mesh['dp'=8,'feat'=4] {'dp'}, use_global_device_ids=true, to_apply=%region_5.6 | all-reduce | flops 1024 | bytes 8192 | tf_op jit(solution)/shard_map/psum | solution.py:90
  442.6 0.6 broadcast_multiply_fusion.1
  443.2 71.4 %reduce-scatter.2.cloned.1.call-done = f32[512,1024]{1,0:T(8,128)} async-done(((f32[4096,1024]{1,0:T(8,128)}), f32[512,1024]{1,0:T(8,128)}) %reduce-scatter.2.cloned.1.call-update) | async-done | bytes 2097168 | tf_op jit(solution)/shard_map/reduce_scatter | solution.py:86
  514.6 3.3 broadcast_multiply_fusion
  (14 shorter events, 0.1 us)
Async XLA Ops:
  7.2 4.6 copy-start
  22.8 7.5 %copy-start.3 = (s32[3,256]{1,0:T(4,128)S(1)}, s32[3,256]{1,0:T(4,128)}, u32[]{:S(2)}) copy-start(s32[3,256]{1,0:T(4,128)} %param.9) | copy-start | bytes 9220
  25.1 26.3 %all-to-all-start = ((bf16[8,384,256]{2,1,0:T(8,128)(2,1)}), bf16[8,384,256]{2,1,0:T(8,128)(2,1)}, u32[]{:S(2)}, u32[]{:S(2)}) async-start(bf16[8,384,256]{2,1,0:T(8,128)(2,1)} %select_multiply_fusion), calls=%async_computation | async-start | bytes 3145728 | tf_op jit(solution)/shard_map/all_to_all | solution.py:45
  30.3 154.2 %all-gather.3.cloned.1.call-start = ((), (), s32[]{:S(2)}) async-start(), calls=%async_computation.3 | async-start | bytes 7864320 | tf_op jit(solution)/shard_map/all_gather | solution.py:76
  69.1 318.3 %all-gather.5.cloned.1.call-start = ((), (), s32[]{:S(2)}) async-start(), calls=%async_computation.4 | async-start | bytes 3932160 | tf_op jit(solution)/shard_map/all_gather | solution.py:81
  184.5 76.4 %slice-start = ((s8[6291456]{0:T(1024)(128)(4,1)}), s8[4194304]{0:T(1024)(128)(4,1)S(1)}, s32[]{:S(2)}) async-start(s8[6291456]{0:T(1024)(128)(4,1)} %bitcast.46), calls=%async_computation.6 | async-start | bytes 8388608
  186.7 74.2 %slice-start.1 = ((s8[6291456]{0:T(1024)(128)(4,1)}), s8[2097152]{0:T(1024)(128)(4,1)S(1)}, s32[]{:S(2)}) async-start(s8[6291456]{0:T(1024)(128)(4,1)} %bitcast.46), calls=%async_computation.7 | async-start | bytes 4194304
  325.5 189.1 %reduce-scatter.2.cloned.1.call-start = ((), (), s32[]{:S(2)}) async-start(), calls=%async_computation.5 | async-start | bytes 18874368 | tf_op jit(solution)/shard_map/reduce_scatter | solution.py:86
  399.7 0.7 copy-start.1
  400.4 29.5 %copy-start.2 = (bf16[1024,384]{1,0:T(8,128)(2,1)S(1)}, bf16[1024,384]{1,0:T(8,128)(2,1)}, u32[]{:S(2)}) copy-start(bf16[1024,384]{1,0:T(8,128)(2,1)} %multiply_convert_fusion) | copy-start | bytes 2359300
Sparse Core Ops, SparseCore 0:
  69.2 115.2 all-gather.2
  325.6 61.6 all-gather.4
  399.9 114.6 reduce-scatter.1
where the time goes:
time: 522 us; the launch traced here: 525 us
  waiting for transfers between devices  255 us (49%)
  matrix products  162 us (31%)
  local copies, waits for them, and re-layouts  36.3 us (7%)
  other arithmetic  30.9 us (6%)
  blocking collectives  20.5 us (4%)
  between operations  15.4 us (3%)
  starting transfers between devices  5.29 us (1%)
    all_gather x1, waiting for transfers between devices, body(): portion = lax.all_gather(spectra_pair, 'feat', axis=2, tiled=True)  115 us
    dot_general x1, matrix products, inverse_terms(): jnp.einsum('fc,rf->cr', cosine, spectra_pair[0], preferred_element_type=j...  74.1 us
    reduce_scatter x1, waiting for transfers between devices, body(): lax.psum_scatter(partial_gram, 'dp', scatter_dimension=0, tiled=True)  71.4 us
    dot_general x1, matrix products, inverse_terms(): jnp.einsum('fc,rf->cr', sine, spectra_pair[1], preferred_element_type=jnp...  64.2 us
    all_gather x1, waiting for transfers between devices, body(): lax.all_gather(features, 'feat', axis=0, tiled=True)  61.8 us
    gather x2, local copies, waits for them, and re-layouts, body(): jnp.take(targets, clipped, axis=0) * send_mask  19.4 us
    mul x1, other arithmetic, body(): signed * jnp.cos(angles)  14.9 us
    psum x1, blocking collectives, body(): target_sum = lax.psum(target_part, 'dp')  12.4 us
  transfers between devices with their start and end apart: 4, of which 4 were waited for; matrix products, arithmetic and copies ran while one was open for 7% of the time, Pallas kernels for 0%

commit v1 on v0

v1 whole, which is shorter than its diff:
```python
import functools
import math

import jax
import jax.numpy as jnp
import numpy as np
from jax import lax
from jax.experimental import pallas as pl
from jax.experimental.pallas import tpu as pltpu
from jax.sharding import PartitionSpec as P

SK = 4096
RADIX = 16
WIDE = SK // RADIX
HALF = WIDE // 2
TILE = 256
TAIL = 16
VMEM_BYTES = 60 * 1024 * 1024


def split_bf16(values):
    high = values.astype(jnp.bfloat16)
    return high, (values - high.astype(np.float32)).astype(jnp.bfloat16)


def short_dft():
    index = np.arange(WIDE)[:, None] * np.arange(HALF)[None, :] % WIDE
    angle = index * (2.0 * np.pi / WIDE)
    terms = []
    for table in (np.cos(angle), -np.sin(angle)):
        rest = table.astype(np.float32)
        for _ in range(3):
            part = rest.astype(jnp.bfloat16)
            terms.append(part)
            rest = rest - part.astype(np.float32)
    return np.concatenate(terms, axis=1)


def inverse_tables():
    scale = SK ** (-0.5)
    column = np.arange(WIDE)[None, :]

    def trig(freq):
        angle = (freq[:, None] * column % SK) * (2.0 * np.pi / SK)
        return 2.0 * scale * np.cos(angle), 2.0 * scale * np.sin(angle)

    narrow = np.arange(HALF)
    cos_a, sin_a = trig(RADIX * narrow)
    cos_b, sin_b = trig(RADIX // 2 + RADIX * narrow)
    imag_a = -sin_a
    cos_a[0] = scale
    imag_a[0] = scale * (1.0 - 2.0 * (np.arange(WIDE) % 2))
    ends = np.concatenate(
        [np.concatenate([cos_a, imag_a], axis=0), np.concatenate([cos_b, -sin_b], axis=0)], axis=1
    )
    groups = []
    for group in range(1, RADIX // 2):
        cosine, sine = trig(group + RADIX * np.arange(WIDE))
        groups.append(
            np.concatenate(
                [np.concatenate([cosine, sine], axis=1), np.concatenate([-sine, cosine], axis=1)],
                axis=0,
            )
        )
    return ends.astype(jnp.bfloat16), np.stack(groups).astype(jnp.bfloat16)


def table_kernel(bucket_ref, phase_ref, dft_ref, out_ref, base_ref):
    group = pl.program_id(0)
    sketches, features_in = 3, bucket_ref.shape[0]

    @pl.when(group == 0)
    def _():
        lane = lax.broadcasted_iota(jnp.int32, (features_in, WIDE), 1)
        for k in range(sketches):
            chosen = jnp.where(bucket_ref[:, k : k + 1] == lane, 1.0, 0.0).astype(jnp.bfloat16)
            full = jnp.dot(chosen, dft_ref[...], preferred_element_type=jnp.float32)
            for part in range(2):
                at = 3 * part * HALF
                base_ref[2 * k + part] = (
                    full[:, at : at + HALF]
                    + full[:, at + HALF : at + 2 * HALF]
                    + full[:, at + 2 * HALF : at + 3 * HALF]
                )

    first_lane = (lax.broadcasted_iota(jnp.int32, (features_in, HALF), 1) == 0) & (group == 0)
    for k in range(sketches):
        base_re, base_im = base_ref[2 * k], base_ref[2 * k + 1]
        for side in range(2):
            at = 6 * side + 2 * k
            turn_re, turn_im = phase_ref[0, :, at : at + 1], phase_ref[0, :, at + 1 : at + 2]
            real = turn_re * base_re - turn_im * base_im
            imag = turn_re * base_im + turn_im * base_re
            if side == 0:
                imag = jnp.where(first_lane, phase_ref[0, :, 12 + k : 13 + k], imag)
            for part, values in enumerate((real, imag)):
                start = (2 * k + part) * WIDE + side * HALF
                high = values.astype(jnp.bfloat16)
                low = (values - high.astype(jnp.float32)).astype(jnp.bfloat16)
                out_ref[0, :features_in, start : start + HALF] = high
                out_ref[0, features_in:, start : start + HALF] = low


def forward_tables(bucket_ids, sign_bits):
    groups = RADIX // 2
    features_in = bucket_ids.shape[1]
    first = np.arange(groups)
    second = np.where(first == 0, RADIX // 2, first + RADIX * HALF)
    offsets = jnp.asarray(np.stack([first, second], axis=1), jnp.int32)
    buckets = bucket_ids.T
    signs = (2 * sign_bits - 1).astype(jnp.float32).T
    turns = buckets[None, :, None, :] * offsets[:, None, :, None] % SK
    angles = turns.astype(jnp.float32) * (2.0 * math.pi / SK)
    phases = jnp.stack([signs[None, :, None] * jnp.cos(angles), -signs[None, :, None] * jnp.sin(angles)], -1)
    phases = phases.reshape(groups, features_in, 12)
    middle = signs * (1 - 2 * (buckets % 2)).astype(jnp.float32)
    phases = jnp.concatenate([phases, jnp.broadcast_to(middle[None], (groups, features_in, 3))], -1)
    short = jnp.pad(buckets % WIDE, ((0, 0), (0, 5)))
    dft = jnp.asarray(short_dft())
    return pl.pallas_call(
        table_kernel,
        grid=(groups,),
        out_shape=jax.ShapeDtypeStruct((groups, 2 * features_in, 6 * WIDE), jnp.bfloat16),
        in_specs=[
            pl.BlockSpec(short.shape, lambda g: (0, 0)),
            pl.BlockSpec((1, features_in, 15), lambda g: (g, 0, 0)),
            pl.BlockSpec(dft.shape, lambda g: (0, 0)),
        ],
        out_specs=pl.BlockSpec((1, 2 * features_in, 6 * WIDE), lambda g: (g, 0, 0)),
        scratch_shapes=[pltpu.VMEM((6, features_in, HALF), jnp.float32)],
        compiler_params=pltpu.CompilerParams(vmem_limit_bytes=VMEM_BYTES // 2),
        cost_estimate=pl.CostEstimate(flops=2 * 10**9, bytes_accessed=14 * 10**6, transcendentals=0),
    )(short, phases, dft)


def combine(load):
    root = math.sqrt(0.5)
    big, small = math.cos(math.pi / 8), math.sin(math.pi / 8)
    r4, i4 = load(8), load(9)
    q0, q8 = load(0), load(1)
    a, b = q0 + q8, q0 - q8
    quarter = (a + r4, b - i4, a - r4, b + i4)
    r2, i2, r6, i6 = load(4), load(5), load(12), load(13)
    u, v = r2 - r6, i2 + i6
    other = (r2 + r6, root * (u - v), i6 - i2, -root * (u + v))
    even = [quarter[c] + other[c] for c in range(4)] + [quarter[c] - other[c] for c in range(4)]
    r1, i1, r7, i7 = load(2), load(3), load(14), load(15)
    r3, i3, r5, i5 = load(6), load(7), load(10), load(11)
    p1, q1, t1, s1 = r1 + r7, r1 - r7, i1 - i7, i1 + i7
    p3, q3, t3, s3 = r3 + r5, r3 - r5, i3 - i5, i3 + i5
    w, y = root * (p1 - p3), root * (t1 + t3)
    a1, b1 = q1 * big + q3 * small, s1 * small + s3 * big
    c1, d1 = q1 * small - q3 * big, s1 * big - s3 * small
    odd = [p1 + p3, a1 - b1, w - y, c1 - d1, t3 - t1, -(c1 + d1), -(w + y), -(a1 + b1)]
    return [even[c] + odd[c] for c in range(8)] + [even[c] - odd[c] for c in range(8)]


def main_kernel(place_ref, shift_ref, *refs):
    count = shift_ref.shape[0] - 1
    blocks = refs[:count]
    table_ref, ends_ref, groups_ref, own_ref, send_ref = refs[count : count + 5]
    stack, table, loose, rows2, cube, spectra, products, sums, kept, block_sem, table_sem = refs[
        count + 5 :
    ]
    device, panel, pair_panel = place_ref[0], place_ref[1], place_ref[2]
    n_groups = RADIX // 2
    slots = stack.shape[1] - TAIL
    width = stack.shape[2]
    rows = rows2.shape[0]
    pair_slots = own_ref.shape[0] // WIDE * 2
    panel_slots = own_ref.shape[1] // WIDE
    junk = pair_slots + panel_slots

    block_copies = [pltpu.make_async_copy(blocks[i], stack.at[i], block_sem.at[i]) for i in range(count)]
    table_copies = [
        pltpu.make_async_copy(table_ref.at[g], table.at[g], table_sem.at[g]) for g in range(n_groups)
    ]
    for copy in block_copies + table_copies:
        copy.start()
    for copy in block_copies:
        copy.wait()

    span = loose.shape[0]
    lane = lax.broadcasted_iota(jnp.int32, (8, span), 1)
    marks = jnp.zeros((8, span), jnp.float32)
    for j in range(count):
        at = lax.bitwise_xor(device, j)
        block = stack[at, :slots, :].astype(jnp.float32)
        block = jnp.concatenate([block, jnp.zeros((8, width), jnp.float32)], axis=0)
        spill = lax.rem(shift_ref[j], 8)
        block = pltpu.roll(block, spill, 0)
        start = pl.multiple_of(shift_ref[j] - spill, 8)
        head = jnp.where(
            lax.broadcasted_iota(jnp.int32, (8, width), 0) < spill, loose[pl.ds(start, 8), :], block[:8]
        )
        loose[pl.ds(start, 8), :] = head
        loose[pl.ds(start + 8, slots), :] = block[8:]
        tail = stack[at, slots:, :].astype(jnp.float32)
        pieces = [tail[i : i + 1, :] for i in range(-(-slots // width))]
        line = jnp.concatenate(pieces, axis=1)
        line = jnp.concatenate([line, jnp.zeros((1, span - line.shape[1]), jnp.float32)], axis=1)
        line = pltpu.roll(jnp.broadcast_to(line, (8, span)), shift_ref[j], 1)
        marks = jnp.where((lane >= shift_ref[j]) & (lane < shift_ref[j + 1]), line, marks)
    marks = marks[:, :rows].astype(jnp.bfloat16)

    for t in range(rows // TILE):
        values = loose[t * TILE : (t + 1) * TILE, :]
        mean = jnp.sum(values * values, axis=1, keepdims=True) * (1.0 / width)
        factor = lax.rsqrt(mean + 1e-06) * width ** (-0.5)
        cube[t * TILE : (t + 1) * TILE, :] = jnp.broadcast_to(factor * factor * factor, (TILE, 128))
        low = values.astype(jnp.bfloat16)
        rows2[t * TILE : (t + 1) * TILE, :width] = low
        rows2[t * TILE : (t + 1) * TILE, width:] = low
    for copy in table_copies:
        copy.wait()

    def tile_step(t, _):
        base = pl.multiple_of(t * TILE, TILE)
        here = pl.ds(base, TILE)

        def forward(group):
            spectra[group % 2] = jnp.dot(
                rows2[here, :], table[group], preferred_element_type=jnp.float32
            )

        def multiply(group):
            source = spectra.at[group % 2]
            target = products.at[group % 2]
            step = 32
            for r in range(0, TILE, step):
                third = cube[pl.ds(base + r, step), :]
                for side in range(2):
                    part = [
                        source[r : r + step, i * WIDE + side * HALF : i * WIDE + (side + 1) * HALF]
                        for i in range(6)
                    ]
                    a_re, a_im, b_re, b_im, c_re, c_im = part
                    a_re, a_im = a_re * third, a_im * third
                    if group == 0 and side == 0:
                        real = a_re * b_re
                        both = a_im * b_im
                        m_re, m_im = real - both, a_re * b_im + a_im * b_re
                        first = lax.broadcasted_iota(jnp.int32, real.shape, 1) == 0
                        out_re = jnp.where(first, real * c_re, m_re * c_re - m_im * c_im)
                        out_im = jnp.where(first, both * c_im, m_re * c_im + m_im * c_re)
                    else:
                        m_re, m_im = a_re * b_re - a_im * b_im, a_re * b_im + a_im * b_re
                        out_re = m_re * c_re - m_im * c_im
                        out_im = m_re * c_im + m_im * c_re
                    if group == 0:
                        re_at, im_at = 2 * side * HALF, (2 * side + 1) * HALF
                    else:
                        re_at, im_at = side * HALF, WIDE + side * HALF
                    target[r : r + step, re_at : re_at + HALF] = out_re.astype(jnp.bfloat16)
                    target[r : r + step, im_at : im_at + HALF] = out_im.astype(jnp.bfloat16)

        def inverse(group):
            source = products.at[group % 2]
            if group == 0:
                for side in range(2):
                    at = slice(side * WIDE, (side + 1) * WIDE)
                    sums[:, at] = jnp.dot(
                        source[:, at], ends_ref[:, at], preferred_element_type=jnp.float32
                    )
            else:
                sums[:, 2 * group * WIDE : 2 * (group + 1) * WIDE] = jnp.dot(
                    source[...], groups_ref[group - 1], preferred_element_type=jnp.float32
                )

        forward(0)
        for group in range(n_groups):
            if group + 1 < n_groups:
                forward(group + 1)
            multiply(group)
            inverse(group)

        step = 16
        where_pair, where_panel = [], []
        for c in range(RADIX):
            low = c - pair_panel * pair_slots
            where_pair.append(jnp.where((low >= 0) & (low < pair_slots), low, junk))
            low = c - panel * panel_slots
            where_panel.append(jnp.where((low >= 0) & (low < panel_slots), low + pair_slots, junk))
        for r in range(0, TILE, step):
            for side in range(2):
                def load(i):
                    at = i * WIDE + side * HALF
                    return sums[r : r + step, at : at + HALF]

                outs = combine(load)
                at = slice(side * HALF, (side + 1) * HALF)
                for c in range(RADIX):
                    value = outs[c].astype(jnp.bfloat16)
                    kept[where_pair[c], pl.ds(base + r, step), at] = value
                    kept[where_panel[c], pl.ds(base + r, step), at] = value
        return 0

    lax.fori_loop(0, rows // TILE, tile_step, 0)

    odd = lax.rem(device, 2)
    each = pair_slots // 2
    for i in range(each):
        for who, target in ((1 - odd, send_ref), (odd, own_ref)):
            left = kept[who * each + i].T
            for j in range(panel_slots):
                target[i * WIDE : (i + 1) * WIDE, j * WIDE : (j + 1) * WIDE] = jnp.dot(
                    left, kept[pair_slots + j], preferred_element_type=jnp.float32
                )
    for j in range(panel_slots):
        line = jnp.dot(marks, kept[pair_slots + j], preferred_element_type=jnp.float32)
        send_ref[each * WIDE : each * WIDE + 8, j * WIDE : (j + 1) * WIDE] = line
        own_ref[each * WIDE : each * WIDE + 8, j * WIDE : (j + 1) * WIDE] = line


def body(samples, targets, counts, bucket_ids, sign_bits):
    device = lax.axis_index("dp")
    n_dp, n_feat = lax.axis_size("dp"), lax.axis_size("feat")
    core = device % 2
    slots, width = samples.shape
    half = slots // 2
    total = half * n_dp
    rows = total // 2
    ends = jnp.cumsum(counts)
    starts = ends - counts
    first_part = (ends + 1) // 2 - (starts + 1) // 2
    edges = jnp.concatenate([jnp.zeros((1,), jnp.int32), ends])
    shift = jnp.where(core == 0, (edges + 1) // 2, edges // 2).astype(jnp.int32)
    cut = first_part[device]

    def message(values, marks):
        marks = jnp.pad(marks, (0, TAIL * width - half)).reshape(TAIL, width)
        return jnp.concatenate([values, marks], axis=0)

    low = message(samples[:half], targets[:half])
    high = message(
        lax.dynamic_slice_in_dim(samples, cut, half, 0), lax.dynamic_slice_in_dim(targets, cut, half, 0)
    )
    own = jnp.where(core == 0, low, high)
    other = jnp.where(core == 0, high, low)

    def swap(block, bit):
        return lax.ppermute(block, "dp", [(i, i ^ bit) for i in range(n_dp)])

    blocks = [own, swap(other, 1)]
    for delta in range(2, n_dp):
        bits = [1 << i for i in range(1, n_dp.bit_length()) if delta >> i & 1]
        bit = bits[0] if delta % 2 else bits[-1]
        blocks.append(swap(blocks[delta ^ bit], bit))

    table = forward_tables(bucket_ids, sign_bits)
    ends_table, group_table = inverse_tables()
    ends_table, group_table = jnp.asarray(ends_table), jnp.asarray(group_table)
    own_columns, panel_columns = SK // n_dp, SK // n_feat
    place = jnp.stack([device, lax.axis_index("feat"), device // 2]).astype(jnp.int32)
    out = jax.ShapeDtypeStruct((own_columns + 8, panel_columns), jnp.float32)
    kept_slots = 2 * own_columns // WIDE + panel_columns // WIDE + 1
    span = -(-(rows + half + 8) // 128) * 128
    n_groups = RADIX // 2
    mine, send = pl.pallas_call(
        main_kernel,
        out_shape=(out, out),
        in_specs=[pl.BlockSpec(memory_space=pltpu.SMEM)] * 2
        + [pl.BlockSpec(memory_space=pl.ANY)] * (n_dp + 1)
        + [pl.BlockSpec(memory_space=pltpu.VMEM)] * 2,
        out_specs=(pl.BlockSpec(memory_space=pltpu.VMEM),) * 2,
        scratch_shapes=[
            pltpu.VMEM((n_dp, half + TAIL, width), jnp.bfloat16),
            pltpu.VMEM((n_groups, 2 * width, 6 * WIDE), jnp.bfloat16),
            pltpu.VMEM((span, width), jnp.float32),
            pltpu.VMEM((rows, 2 * width), jnp.bfloat16),
            pltpu.VMEM((rows, 128), jnp.float32),
            pltpu.VMEM((2, TILE, 6 * WIDE), jnp.float32),
            pltpu.VMEM((2, TILE, 2 * WIDE), jnp.bfloat16),
            pltpu.VMEM((TILE, SK), jnp.float32),
            pltpu.VMEM((kept_slots, rows, WIDE), jnp.bfloat16),
            pltpu.SemaphoreType.DMA((n_dp,)),
            pltpu.SemaphoreType.DMA((n_groups,)),
        ],
        compiler_params=pltpu.CompilerParams(vmem_limit_bytes=VMEM_BYTES),
        cost_estimate=pl.CostEstimate(flops=3 * 10**10, bytes_accessed=24 * 10**6, transcendentals=0),
    )(place, shift, *blocks, table, ends_table, group_table)
    summed = mine + swap(send, 1)
    return (summed[:own_columns] * (1.0 / total), summed[own_columns] * total ** (-0.5))


def solution(mesh):
    placed = (P("dp", None), P("dp"), P(), P(), P())
    return jax.shard_map(
        body, mesh=mesh, in_specs=placed, out_specs=(P("dp", "feat"), P("feat")), check_vma=False
    )
```

time: 522 us -> 92.4 us (0.18)
  waiting for transfers between devices: 255 us -> 10.8 us
  matrix products: 162 us -> 0 us
  Pallas kernels: 0 us -> 53.5 us
  local copies, waits for them, and re-layouts: 36.3 us -> 10.2 us
  other arithmetic: 30.9 us -> 8.09 us
  blocking collectives: 20.5 us -> 0 us
  between operations: 15.4 us -> 2.83 us
    all_gather x2 -> x0, waiting for transfers between devices: 177 us -> none  [the longest x1 115 us: body(): portion = lax.all_gather(spectra_pair, 'feat', axis=2, tiled=True)]
    dot_general x5 -> x0, matrix products: 162 us -> none  [the longest x1 74.1 us: inverse_terms(): jnp.einsum('fc,rf->cr', cosine, spectra_pair[0], preferred_element_type=j...]
    reduce_scatter x1 -> x0, waiting for transfers between devices: 71.4 us -> none  [body(): lax.psum_scatter(partial_gram, 'dp', scatter_dimension=0, tiled=True)]
    pallas_call x0 -> x2, Pallas kernels: none -> 53.5 us  [the longest x1 47.8 us: body(): pl.pallas_call(main_kernel, out_shape=(out, out), in_specs=[pl.BlockSpec(...]
    gather x3 -> x0, local copies, waits for them, and re-layouts: 30.4 us -> none  [the longest x2 19.4 us: body(): jnp.take(targets, clipped, axis=0) * send_mask]
    mul x5 -> x3, other arithmetic: 19 us -> 2.42 us  [the longest x1 1.53 us: body(): summed[:own_columns] * (1.0 / total)]
    psum x1 -> x0, blocking collectives: 12.4 us -> none  [body(): target_sum = lax.psum(target_part, 'dp')]
    ppermute x0 -> x8, waiting for transfers between devices: none -> 10.8 us  [swap(): return lax.ppermute(block, 'dp', [(i, i ^ bit) for i in range(n_dp)])]
  transfers between devices with their start and end apart: 4 -> 8, of which waited for: 4 -> 3; matrix products, arithmetic and copies ran while one was open for 7% -> 4% of each run, Pallas kernels for 0% -> 6%
where the time goes in v1:
time: 92.4 us; the launch traced here: 92.1 us
  Pallas kernels  53.5 us (58%)
  waiting for transfers between devices  10.8 us (12%)
  local copies, waits for them, and re-layouts  10.2 us (11%)
  other arithmetic  8.09 us (9%)
  starting transfers between devices  6.62 us (7%)
  between operations  2.83 us (3%)
    pallas_call x1, Pallas kernels, body(): pl.pallas_call(main_kernel, out_shape=(out, out), in_specs=[pl.BlockSpec(...  47.8 us
    ppermute x8, waiting for transfers between devices, swap(): return lax.ppermute(block, 'dp', [(i, i ^ bit) for i in range(n_dp)])  10.8 us
    unnamed x23, local copies, waits for them, and re-layouts  6.86 us
    ppermute x8, starting transfers between devices, swap(): return lax.ppermute(block, 'dp', [(i, i ^ bit) for i in range(n_dp)])  6.62 us
    pallas_call x1, Pallas kernels, forward_tables(): pl.pallas_call(table_kernel, grid=(groups,), out_shape=jax.ShapeDtypeStru...  5.76 us
    add x1, other arithmetic, body(): summed = mine + swap(send, 1)  2 us
    slice x2, local copies, waits for them, and re-layouts, body(): low = message(samples[:half], targets[:half])  1.91 us
  transfers between devices with their start and end apart: 8, of which 3 were waited for; matrix products, arithmetic and copies ran while one was open for 4% of the time, Pallas kernels for 6%

profile of v1, /device:TPU:0, one launch (start us, length us, event | category | flops | bytes accessed | tf_op | source)
XLA Modules:
  0.0 92.1 jit_solution(331894904539454536)
XLA Ops:
  0.6 0.0 copy-start.3
  0.7 0.8 reduce-window.9
  1.5 0.7 fusion.7
  2.2 0.6 dynamic_slice.9
  4.7 0.8 fusion.9
  5.6 1.1 %fusion.8 = (bf16[384,256]{1,0:T(8,128)(2,1)S(1)}, bf16[384,256]{1,0:T(8,128)(2,1)S(1)}) fusion(bf16[768,256]{1,0:T(8,128)(2,1)} %param.9, s32[]{:T(128)S(6)} %select_n.91), kind=kLoop, calls=%fused_computation.50 | loop fusion | bytes 786436 | tf_op jit(solution)/shard_map/slice | solution.py:334
  6.7 0.0 copy-start.1
  6.7 0.1 broadcast_select_fusion
  6.7 0.0 copy-start.2
  6.8 3.0 %collective-permute-start.3 = (bf16[400,256]{1,0:T(8,128)(2,1)S(1)}, bf16[400,256]{1,0:T(8,128)(2,1)S(1)}, u32[]{:S(2)}, u32[]{:S(2)}) collective-permute-start(bf16[400,256]{1,0:T(8,128)(2,1)S(1)} %get-tuple-element.7.refs_0_), channel_id=1, source_target_pairs={{0,16},{4,20},{8,24},{12,28},{16,0},{20,4},{24,8},{28,12},{1,17},{... | collective-permute-start | bytes 614408 | tf_op jit(solution)/shard_map/ppermute | solution.py:342
  9.8 1.5 %collective-permute-start.1 = (bf16[400,256]{1,0:T(8,128)(2,1)S(1)}, bf16[400,256]{1,0:T(8,128)(2,1)S(1)}, u32[]{:S(2)}, u32[]{:S(2)}) collective-permute-start(bf16[400,256]{1,0:T(8,128)(2,1)S(1)} %get-tuple-element.7.refs_0_), channel_id=1, source_target_pairs={{0,8},{4,12},{8,0},{12,4},{16,24},{20,28},{24,16},{28,20},{1,9},{5... | collective-permute-start | bytes 614408 | tf_op jit(solution)/shard_map/ppermute | solution.py:342
  11.3 0.0 collective-permute-start
  11.3 0.7 add_convert_fusion
  12.0 0.1 copy.33
  12.1 0.1 copy.34
  12.2 0.8 copy.32
  13.0 0.1 bitcast_negate_fusion
  13.1 0.1 copy.35
  13.2 0.1 copy.36
  13.3 0.1 copy.37
  13.4 0.3 cosine_multiply_fusion
  13.7 0.6 broadcast_select_fusion.2.shift_ref
  14.3 0.0 collective-permute-done.refs_1_
  14.3 0.6 collective-permute-start.4
  14.9 0.1 add_select_fusion.1
  14.9 0.2 collective-permute-start.2
  15.1 1.2 %collective-permute-done.1.refs_2_ = bf16[400,256]{1,0:T(8,128)(2,1)S(1)} collective-permute-done((bf16[400,256]{1,0:T(8,128)(2,1)S(1)}, bf16[400,256]{1,0:T(8,128)(2,1)S(1)}, u32[]{:S(2)}, u32[]{:S(2)}) %collective-permute-start.1) | collective-permute-done | bytes 204832 | tf_op jit(solution)/shard_map/ppermute | solution.py:342
  16.3 0.7 collective-permute-start.5
  17.1 5.2 %collective-permute-done.4.refs_5_ = bf16[400,256]{1,0:T(8,128)(2,1)S(1)} collective-permute-done((bf16[400,256]{1,0:T(8,128)(2,1)S(1)}, bf16[400,256]{1,0:T(8,128)(2,1)S(1)}, u32[]{:S(2)}, u32[]{:S(2)}) %collective-permute-start.4) | collective-permute-done | bytes 204832 | tf_op jit(solution)/shard_map/ppermute | solution.py:342
  22.3 0.5 collective-permute-start.6
  22.8 0.7 pad_add_fusion.place_ref
  23.5 0.4 copy.38.phase_ref
  23.8 5.8 %shard_map.104.refs_8_ = bf16[8,512,1536]{2,1,0:T(8,128)(2,1)S(1)} custom-call(s32[256,8]{1,0:T(8,128)S(1)} %pad.13.bucket_ref, f32[8,256,15]{2,1,0:T(8,128)S(1)} %copy.38.phase_ref, bf16[256,768]{1,0:T(8,128)(2,1)S(1)} %copy-done.1), custom_call_target="tpu_custom_call" | custom-call | flops 2000000000 | bytes 14000000 | tf_op jit(solution)/shard_map/pallas_call | solution.py:120
  29.7 4.5 %copy-done = bf16[8,512,1536]{2,1,0:T(8,128)(2,1)} copy-done((bf16[8,512,1536]{2,1,0:T(8,128)(2,1)}, bf16[8,512,1536]{2,1,0:T(8,128)(2,1)S(1)}, u32[]{:S(2)}) %copy-start) | copy-done | bytes 12582936
  34.2 0.0 collective-permute-done.3.refs_4_
  34.2 0.0 collective-permute-done.2.refs_3_
  34.2 0.0 collective-permute-done.5.refs_6_
  34.2 0.0 collective-permute-done.6.refs_7_
  34.2 0.6 copy-done.4
  34.9 0.1 copy-done.8
  35.0 0.1 copy-done.9
  35.0 0.7 copy-done.10
  35.7 47.8 %shard_map.105 = (f32[520,1024]{1,0:T(8,128)}, f32[520,1024]{1,0:T(8,128)}) custom-call(s32[3]{0:T(128)} %pad_add_fusion.place_ref, s32[9]{0:T(128)} %broadcast_select_fusion.2.shift_ref, bf16[400,256]{1,0:T(8,128)(2,1)} %copy-done.2, bf16[400,256]{1,0:T(8,128)(2,1)} %copy-done.6, bf16[400,256]{1,0:T(8,128)(2,1)} %copy-done.5, bf16[400,256]{1,0:T(8,128)(2,1)} %copy-done.8, ...), custom_call_target="tpu_custom_call" | custom-call | flops 30000001024 | bytes 24000000 | tf_op jit(solution)/shard_map/pallas_call | solution.py:359
  83.5 0.1 collective-permute-start.7
  83.6 4.4 %collective-permute-done.7 = f32[520,1024]{1,0:T(8,128)S(1)} collective-permute-done((f32[520,1024]{1,0:T(8,128)}, f32[520,1024]{1,0:T(8,128)S(1)}, u32[]{:S(2)}, u32[]{:S(2)}) %collective-permute-start.7) | collective-permute-done | bytes 2129952 | tf_op jit(solution)/shard_map/ppermute | solution.py:342
  88.0 2.0 %add.71 = f32[520,1024]{1,0:T(8,128)S(1)} add(f32[520,1024]{1,0:T(8,128)} %get-tuple-element.4, f32[520,1024]{1,0:T(8,128)S(1)} %collective-permute-done.7) | non-fusion elementwise | flops 532480 | bytes 6389760 | tf_op jit(solution)/shard_map/add | solution.py:382
  90.0 0.6 slice_multiply_fusion.1
  90.6 1.5 %slice_multiply_fusion = f32[512,1024]{1,0:T(8,128)} fusion(f32[520,1024]{1,0:T(8,128)S(1)} %add.71), kind=kLoop, calls=%fused_computation | loop fusion | flops 524288 | bytes 4194304 | tf_op jit(solution)/shard_map/mul | solution.py:383
  (22 shorter events, 0.1 us)
Async XLA Ops:
  0.6 12.7 %copy-start.3 = (s32[8,2]{0,1:T(2,128)S(1)}, s32[8,2]{0,1:T(2,128)}, u32[]{:S(2)}) copy-start(s32[8,2]{0,1:T(2,128)} %constant.131.clone) | copy-start | bytes 196
  6.7 17.2 %copy-start.1 = (bf16[256,768]{1,0:T(8,128)(2,1)S(1)}, bf16[256,768]{1,0:T(8,128)(2,1)}, u32[]{:S(2)}) copy-start(bf16[256,768]{1,0:T(8,128)(2,1)} %constant.132.clone.dft_ref) | copy-start | bytes 1179652
  6.7 22.9 %copy-start.2 = (bf16[400,256]{1,0:T(8,128)(2,1)}, bf16[400,256]{1,0:T(8,128)(2,1)S(1)}, u32[]{:S(2)}) copy-start(bf16[400,256]{1,0:T(8,128)(2,1)S(1)} %get-tuple-element.7.refs_0_) | copy-start | bytes 614404
  6.8 27.4 %collective-permute-start.3 = (bf16[400,256]{1,0:T(8,128)(2,1)S(1)}, bf16[400,256]{1,0:T(8,128)(2,1)S(1)}, u32[]{:S(2)}, u32[]{:S(2)}) collective-permute-start(bf16[400,256]{1,0:T(8,128)(2,1)S(1)} %get-tuple-element.7.refs_0_), channel_id=1, source_target_pairs={{0,16},{4,20},{8,24},{12,28},{16,0},{20,4},{24,8},{28,12},{1,17},{... | collective-permute-start | bytes 614408 | tf_op jit(solution)/shard_map/ppermute | solution.py:342
  9.8 6.5 %collective-permute-start.1 = (bf16[400,256]{1,0:T(8,128)(2,1)S(1)}, bf16[400,256]{1,0:T(8,128)(2,1)S(1)}, u32[]{:S(2)}, u32[]{:S(2)}) collective-permute-start(bf16[400,256]{1,0:T(8,128)(2,1)S(1)} %get-tuple-element.7.refs_0_), channel_id=1, source_target_pairs={{0,8},{4,12},{8,0},{12,4},{16,24},{20,28},{24,16},{28,20},{1,9},{5... | collective-permute-start | bytes 614408 | tf_op jit(solution)/shard_map/ppermute | solution.py:342
  11.3 3.0 %collective-permute-start = (bf16[400,256]{1,0:T(8,128)(2,1)S(1)}, bf16[400,256]{1,0:T(8,128)(2,1)S(1)}, u32[]{:S(2)}, u32[]{:S(2)}) collective-permute-start(bf16[400,256]{1,0:T(8,128)(2,1)S(1)} %get-tuple-element.6), channel_id=1, source_target_pairs={{0,4},{4,0},{8,12},{12,8},{16,20},{20,16},{24,28},{28,24},{1,5},{5... | collective-permute-start | bytes 614408 | tf_op jit(solution)/shard_map/ppermute | solution.py:342
  14.3 15.3 %copy-start.6 = (bf16[400,256]{1,0:T(8,128)(2,1)}, bf16[400,256]{1,0:T(8,128)(2,1)S(1)}, u32[]{:S(2)}) copy-start(bf16[400,256]{1,0:T(8,128)(2,1)S(1)} %collective-permute-done.refs_1_) | copy-start | bytes 614404
  14.3 7.9 %collective-permute-start.4 = (bf16[400,256]{1,0:T(8,128)(2,1)S(1)}, bf16[400,256]{1,0:T(8,128)(2,1)S(1)}, u32[]{:S(2)}, u32[]{:S(2)}) collective-permute-start(bf16[400,256]{1,0:T(8,128)(2,1)S(1)} %collective-permute-done.refs_1_), channel_id=1, source_target_pairs={{0,16},{4,20},{8,24},{12,28},{16,0},{20,4},{24,8},{28,12},{1,17},{... | collective-permute-start | bytes 614408 | tf_op jit(solution)/shard_map/ppermute | solution.py:342
  14.9 19.3 %collective-permute-start.2 = (bf16[400,256]{1,0:T(8,128)(2,1)S(1)}, bf16[400,256]{1,0:T(8,128)(2,1)S(1)}, u32[]{:S(2)}, u32[]{:S(2)}) collective-permute-start(bf16[400,256]{1,0:T(8,128)(2,1)S(1)} %collective-permute-done.refs_1_), channel_id=1, source_target_pairs={{0,8},{4,12},{8,0},{12,4},{16,24},{20,28},{24,16},{28,20},{1,9},{5... | collective-permute-start | bytes 614408 | tf_op jit(solution)/shard_map/ppermute | solution.py:342
  16.3 13.3 %copy-start.5 = (bf16[400,256]{1,0:T(8,128)(2,1)}, bf16[400,256]{1,0:T(8,128)(2,1)S(1)}, u32[]{:S(2)}) copy-start(bf16[400,256]{1,0:T(8,128)(2,1)S(1)} %collective-permute-done.1.refs_2_) | copy-start | bytes 614404
  16.3 17.9 %collective-permute-start.5 = (bf16[400,256]{1,0:T(8,128)(2,1)S(1)}, bf16[400,256]{1,0:T(8,128)(2,1)S(1)}, u32[]{:S(2)}, u32[]{:S(2)}) collective-permute-start(bf16[400,256]{1,0:T(8,128)(2,1)S(1)} %collective-permute-done.1.refs_2_), channel_id=1, source_target_pairs={{0,16},{4,20},{8,24},{12,28},{16,0},{20,4},{24,8},{28,12},{1,17},{... | collective-permute-start | bytes 614408 | tf_op jit(solution)/shard_map/ppermute | solution.py:342
  22.3 7.4 %copy-start.7 = (bf16[400,256]{1,0:T(8,128)(2,1)}, bf16[400,256]{1,0:T(8,128)(2,1)S(1)}, u32[]{:S(2)}) copy-start(bf16[400,256]{1,0:T(8,128)(2,1)S(1)} %collective-permute-done.4.refs_5_) | copy-start | bytes 614404
  22.3 12.0 %collective-permute-start.6 = (bf16[400,256]{1,0:T(8,128)(2,1)S(1)}, bf16[400,256]{1,0:T(8,128)(2,1)S(1)}, u32[]{:S(2)}, u32[]{:S(2)}) collective-permute-start(bf16[400,256]{1,0:T(8,128)(2,1)S(1)} %collective-permute-done.4.refs_5_), channel_id=1, source_target_pairs={{0,8},{4,12},{8,0},{12,4},{16,24},{20,28},{24,16},{28,20},{1,9},{5... | collective-permute-start | bytes 614408 | tf_op jit(solution)/shard_map/ppermute | solution.py:342
  29.7 4.5 %copy-start = (bf16[8,512,1536]{2,1,0:T(8,128)(2,1)}, bf16[8,512,1536]{2,1,0:T(8,128)(2,1)S(1)}, u32[]{:S(2)}) copy-start(bf16[8,512,1536]{2,1,0:T(8,128)(2,1)S(1)} %shard_map.104.refs_8_) | copy-start | bytes 37748740
  34.2 0.7 copy-start.4
  34.2 0.8 copy-start.8
  34.2 0.8 copy-start.9
  35.0 0.7 copy-start.10
  83.5 4.5 %collective-permute-start.7 = (f32[520,1024]{1,0:T(8,128)}, f32[520,1024]{1,0:T(8,128)S(1)}, u32[]{:S(2)}, u32[]{:S(2)}) collective-permute-start(f32[520,1024]{1,0:T(8,128)} %get-tuple-element.5), channel_id=1, source_target_pairs={{0,4},{4,0},{8,12},{12,8},{16,20},{20,16},{24,28},{28,24},{1,5},{5... | collective-permute-start | bytes 6389768 | tf_op jit(solution)/shard_map/ppermute | solution.py:342

commit v2 on v1

v2 whole, which is shorter than its diff:
```python
import functools
import math

import jax
import jax.numpy as jnp
import numpy as np
from jax import lax
from jax.experimental import pallas as pl
from jax.experimental.pallas import tpu as pltpu
from jax.sharding import PartitionSpec as P

SK = 4096
RADIX = 16
WIDE = SK // RADIX
HALF = WIDE // 2
TILE = 256
TAIL = 16
PAD = 16
VMEM_BYTES = 36 * 1024 * 1024


def split_bf16(values):
    high = values.astype(jnp.bfloat16)
    return high, (values - high.astype(np.float32)).astype(jnp.bfloat16)


def short_dft():
    index = np.arange(WIDE)[:, None] * np.arange(HALF)[None, :] % WIDE
    angle = index * (2.0 * np.pi / WIDE)
    terms = []
    for table in (np.cos(angle), -np.sin(angle)):
        rest = table.astype(np.float32)
        for _ in range(3):
            part = rest.astype(jnp.bfloat16)
            terms.append(part)
            rest = rest - part.astype(np.float32)
    return np.concatenate(terms, axis=1)


def inverse_tables():
    scale = SK ** (-0.5)
    column = np.arange(WIDE)[None, :]

    def trig(freq):
        angle = (freq[:, None] * column % SK) * (2.0 * np.pi / SK)
        return 2.0 * scale * np.cos(angle), 2.0 * scale * np.sin(angle)

    narrow = np.arange(HALF)
    cos_a, sin_a = trig(RADIX * narrow)
    cos_b, sin_b = trig(RADIX // 2 + RADIX * narrow)
    imag_a = -sin_a
    cos_a[0] = scale
    imag_a[0] = scale * (1.0 - 2.0 * (np.arange(WIDE) % 2))
    ends = np.concatenate(
        [np.concatenate([cos_a, imag_a], axis=0), np.concatenate([cos_b, -sin_b], axis=0)], axis=1
    )
    groups = []
    for group in range(1, RADIX // 2):
        cosine, sine = trig(group + RADIX * np.arange(WIDE))
        groups.append(
            np.concatenate(
                [np.concatenate([cosine, sine], axis=1), np.concatenate([-sine, cosine], axis=1)],
                axis=0,
            )
        )
    return ends.astype(jnp.bfloat16), np.stack(groups).astype(jnp.bfloat16)


def table_kernel(bucket_ref, phase_ref, dft_ref, out_ref, base_ref):
    group = pl.program_id(0)
    sketches, features_in = 3, bucket_ref.shape[0]

    @pl.when(group == 0)
    def _():
        lane = lax.broadcasted_iota(jnp.int32, (features_in, WIDE), 1)
        for k in range(sketches):
            chosen = jnp.where(bucket_ref[:, k : k + 1] == lane, 1.0, 0.0).astype(jnp.bfloat16)
            full = jnp.dot(chosen, dft_ref[...], preferred_element_type=jnp.float32)
            for part in range(2):
                at = 3 * part * HALF
                base_ref[2 * k + part] = (
                    full[:, at : at + HALF]
                    + full[:, at + HALF : at + 2 * HALF]
                    + full[:, at + 2 * HALF : at + 3 * HALF]
                )

    first_lane = (lax.broadcasted_iota(jnp.int32, (features_in, HALF), 1) == 0) & (group == 0)
    for k in range(sketches):
        base_re, base_im = base_ref[2 * k], base_ref[2 * k + 1]
        for side in range(2):
            at = 6 * side + 2 * k
            turn_re, turn_im = phase_ref[0, :, at : at + 1], phase_ref[0, :, at + 1 : at + 2]
            real = turn_re * base_re - turn_im * base_im
            imag = turn_re * base_im + turn_im * base_re
            if side == 0:
                imag = jnp.where(first_lane, phase_ref[0, :, 12 + k : 13 + k], imag)
            for part, values in enumerate((real, imag)):
                start = (2 * k + part) * WIDE + side * HALF
                high = values.astype(jnp.bfloat16)
                low = (values - high.astype(jnp.float32)).astype(jnp.bfloat16)
                out_ref[0, :features_in, start : start + HALF] = high
                out_ref[0, features_in:, start : start + HALF] = low


def forward_tables(bucket_ids, sign_bits):
    groups = RADIX // 2
    features_in = bucket_ids.shape[1]
    first = np.arange(groups)
    second = np.where(first == 0, RADIX // 2, first + RADIX * HALF)
    offsets = jnp.asarray(np.stack([first, second], axis=1), jnp.int32)
    buckets = bucket_ids.T
    signs = (2 * sign_bits - 1).astype(jnp.float32).T
    turns = buckets[None, :, None, :] * offsets[:, None, :, None] % SK
    angles = turns.astype(jnp.float32) * (2.0 * math.pi / SK)
    phases = jnp.stack([signs[None, :, None] * jnp.cos(angles), -signs[None, :, None] * jnp.sin(angles)], -1)
    phases = phases.reshape(groups, features_in, 12)
    middle = signs * (1 - 2 * (buckets % 2)).astype(jnp.float32)
    phases = jnp.concatenate([phases, jnp.broadcast_to(middle[None], (groups, features_in, 3))], -1)
    short = jnp.pad(buckets % WIDE, ((0, 0), (0, 5)))
    dft = jnp.asarray(short_dft())
    return pl.pallas_call(
        table_kernel,
        grid=(groups,),
        out_shape=jax.ShapeDtypeStruct((groups, 2 * features_in, 6 * WIDE), jnp.bfloat16),
        in_specs=[
            pl.BlockSpec(short.shape, lambda g: (0, 0)),
            pl.BlockSpec((1, features_in, 15), lambda g: (g, 0, 0)),
            pl.BlockSpec(dft.shape, lambda g: (0, 0)),
        ],
        out_specs=pl.BlockSpec((1, 2 * features_in, 6 * WIDE), lambda g: (g, 0, 0)),
        scratch_shapes=[pltpu.VMEM((6, features_in, HALF), jnp.float32)],
        compiler_params=pltpu.CompilerParams(vmem_limit_bytes=VMEM_BYTES // 2),
        cost_estimate=pl.CostEstimate(flops=2 * 10**9, bytes_accessed=14 * 10**6, transcendentals=0),
    )(short, phases, dft)


def combine(load):
    root = math.sqrt(0.5)
    big, small = math.cos(math.pi / 8), math.sin(math.pi / 8)
    r4, i4 = load(8), load(9)
    q0, q8 = load(0), load(1)
    a, b = q0 + q8, q0 - q8
    quarter = (a + r4, b - i4, a - r4, b + i4)
    r2, i2, r6, i6 = load(4), load(5), load(12), load(13)
    u, v = r2 - r6, i2 + i6
    other = (r2 + r6, root * (u - v), i6 - i2, -root * (u + v))
    even = [quarter[c] + other[c] for c in range(4)] + [quarter[c] - other[c] for c in range(4)]
    r1, i1, r7, i7 = load(2), load(3), load(14), load(15)
    r3, i3, r5, i5 = load(6), load(7), load(10), load(11)
    p1, q1, t1, s1 = r1 + r7, r1 - r7, i1 - i7, i1 + i7
    p3, q3, t3, s3 = r3 + r5, r3 - r5, i3 - i5, i3 + i5
    w, y = root * (p1 - p3), root * (t1 + t3)
    a1, b1 = q1 * big + q3 * small, s1 * small + s3 * big
    c1, d1 = q1 * small - q3 * big, s1 * big - s3 * small
    odd = [p1 + p3, a1 - b1, w - y, c1 - d1, t3 - t1, -(c1 + d1), -(w + y), -(a1 + b1)]
    return [even[c] + odd[c] for c in range(8)] + [even[c] - odd[c] for c in range(8)]


def window_start(first, slots):
    window = slots // 2 + PAD
    return pl.multiple_of(jnp.minimum(first // PAD * PAD, slots - window), PAD)


def prepare_kernel(place_ref, counts_ref, samples_ref, targets_ref, own_ref, other_ref):
    device = place_ref[0]
    core = lax.rem(device, 2)
    slots, width = samples_ref.shape
    window = slots // 2 + PAD
    start = jnp.int32(0)
    for j in range(counts_ref.shape[0]):
        start = start + jnp.where(j < device, counts_ref[j], 0)
    cut = (start + counts_ref[device] + 1) // 2 - (start + 1) // 2
    late = window_start(cut, slots)
    lines = [targets_ref[:, i * width : (i + 1) * width] for i in range(slots // width)]
    lines.append(jnp.zeros((TAIL - len(lines), width), jnp.bfloat16))
    tail = jnp.concatenate(lines, axis=0)
    for target, is_late in ((own_ref, core), (other_ref, 1 - core)):
        begin = pl.multiple_of(late * is_late, PAD)
        target[:window, :] = samples_ref[pl.ds(begin, window), :]
        target[window:, :] = tail


def gather_rows(device, counts_ref, ends_ref, blocks, slots, loose, width):
    core = lax.rem(device, 2)
    window = slots // 2 + PAD
    span = loose.shape[0]
    lane = lax.broadcasted_iota(jnp.int32, (8, span), 1)
    marks = jnp.zeros((8, span), jnp.float32)
    total = jnp.int32(0)
    for j in range(counts_ref.shape[0]):
        total = total + counts_ref[j]
        ends_ref[j] = total
    at = jnp.int32(0)
    for delta, block_ref in enumerate(blocks):
        source = lax.bitwise_xor(device, delta)
        end = ends_ref[source]
        start = end - counts_ref[source]
        cut = (end + 1) // 2 - (start + 1) // 2
        share = jnp.where(core == 0, cut, end // 2 - start // 2)
        first = cut * core
        skip = first - window_start(cut, slots) * core
        base = at - skip + PAD
        spill = lax.rem(base, 8)
        begin = pl.multiple_of(base - spill, 8)
        block = block_ref[:window, :].astype(jnp.float32)
        block = jnp.concatenate([block, jnp.zeros((8, width), jnp.float32)], axis=0)
        block = pltpu.roll(block, spill, 0)
        edge = PAD + 8
        keep = lax.broadcasted_iota(jnp.int32, (edge, width), 0) < spill + skip
        loose[pl.ds(begin, edge), :] = jnp.where(keep, loose[pl.ds(begin, edge), :], block[:edge])
        loose[pl.ds(begin + edge, window + 8 - edge), :] = block[edge:]
        tail = block_ref[window:, :].astype(jnp.float32)
        line = jnp.concatenate([tail[i : i + 1, :] for i in range(slots // width)], axis=1)
        line = jnp.concatenate([line, jnp.zeros((1, span - slots), jnp.float32)], axis=1)
        line = pltpu.roll(jnp.broadcast_to(line, (8, span)), lax.rem(at - first + span, span), 1)
        marks = jnp.where((lane >= at) & (lane < at + share), line, marks)
        at = at + share
    return marks


def main_kernel(place_ref, counts_ref, *refs):
    count = counts_ref.shape[0]
    blocks = refs[:count]
    table, ends_table, groups_table, own_ref, send_ref = refs[count : count + 5]
    ends_ref, loose, rows2, cube, spectra, products, sums_a, sums_b, kept = refs[count + 5 :]
    sums = (sums_a, sums_b)
    device, panel, pair_panel = place_ref[0], place_ref[1], place_ref[2]
    n_groups = RADIX // 2
    width = rows2.shape[1] // 2
    slots = 2 * (blocks[0].shape[0] - TAIL - PAD)
    rows = rows2.shape[0]
    pair_slots = own_ref.shape[0] // WIDE * 2
    panel_slots = own_ref.shape[1] // WIDE
    junk = pair_slots + panel_slots

    marks = gather_rows(device, counts_ref, ends_ref, blocks, slots, loose, width)
    marks = marks[:, :rows].astype(jnp.bfloat16)
    for t in range(rows // TILE):
        values = loose[PAD + t * TILE : PAD + (t + 1) * TILE, :]
        mean = jnp.sum(values * values, axis=1, keepdims=True) * (1.0 / width)
        factor = lax.rsqrt(mean + 1e-06) * width ** (-0.5)
        cube[t * TILE : (t + 1) * TILE, :] = jnp.broadcast_to(factor * factor * factor, (TILE, 128))
        low = values.astype(jnp.bfloat16)
        rows2[t * TILE : (t + 1) * TILE, :width] = low
        rows2[t * TILE : (t + 1) * TILE, width:] = low

    where_pair, where_panel = [], []
    for c in range(RADIX):
        low = c - pair_panel * pair_slots
        where_pair.append(jnp.where((low >= 0) & (low < pair_slots), low, junk))
        low = c - panel * panel_slots
        where_panel.append(jnp.where((low >= 0) & (low < panel_slots), low + pair_slots, junk))

    def forward(base, step):
        spectra[step % 2] = jnp.dot(
            rows2[pl.ds(base, TILE), :], table[step % n_groups], preferred_element_type=jnp.float32
        )

    def multiply(base, step):
        group = step % n_groups
        source = spectra.at[step % 2]
        target = products.at[step % 2]
        chunk = 32
        for r in range(0, TILE, chunk):
            third = cube[pl.ds(base + r, chunk), :]
            for side in range(2):
                a_re, a_im, b_re, b_im, c_re, c_im = [
                    source[r : r + chunk, i * WIDE + side * HALF : i * WIDE + (side + 1) * HALF]
                    for i in range(6)
                ]
                a_re, a_im = a_re * third, a_im * third
                if group == 0 and side == 0:
                    real = a_re * b_re
                    both = a_im * b_im
                    m_re, m_im = real - both, a_re * b_im + a_im * b_re
                    first = lax.broadcasted_iota(jnp.int32, real.shape, 1) == 0
                    out_re = jnp.where(first, real * c_re, m_re * c_re - m_im * c_im)
                    out_im = jnp.where(first, both * c_im, m_re * c_im + m_im * c_re)
                else:
                    m_re, m_im = a_re * b_re - a_im * b_im, a_re * b_im + a_im * b_re
                    out_re = m_re * c_re - m_im * c_im
                    out_im = m_re * c_im + m_im * c_re
                if group == 0:
                    re_at, im_at = 2 * side * HALF, (2 * side + 1) * HALF
                else:
                    re_at, im_at = side * HALF, WIDE + side * HALF
                target[r : r + chunk, re_at : re_at + HALF] = out_re.astype(jnp.bfloat16)
                target[r : r + chunk, im_at : im_at + HALF] = out_im.astype(jnp.bfloat16)

    def inverse(step):
        group = step % n_groups
        source = products.at[step % 2]
        into = sums[step // n_groups]
        if group == 0:
            for side in range(2):
                at = slice(side * WIDE, (side + 1) * WIDE)
                into[:, at] = jnp.dot(source[:, at], ends_table[:, at], preferred_element_type=jnp.float32)
        else:
            into[:, 2 * group * WIDE : 2 * (group + 1) * WIDE] = jnp.dot(
                source[...], groups_table[group - 1], preferred_element_type=jnp.float32
            )

    def finish(source, base, part, parts):
        chunk = 16
        size = TILE // parts
        for r in range(part * size, (part + 1) * size, chunk):
            for side in range(2):
                outs = combine(
                    lambda i: source[r : r + chunk, i * WIDE + side * HALF : i * WIDE + (side + 1) * HALF]
                )
                at = slice(side * HALF, (side + 1) * HALF)
                for c in range(RADIX):
                    value = outs[c].astype(jnp.bfloat16)
                    kept[where_pair[c], pl.ds(base + r, chunk), at] = value
                    kept[where_panel[c], pl.ds(base + r, chunk), at] = value

    steps = 2 * n_groups

    def pair_step(t, _):
        bases = [pl.multiple_of(2 * t * TILE, TILE), pl.multiple_of((2 * t + 1) * TILE, TILE)]
        before = [pl.multiple_of(jnp.maximum(2 * t - 1, 1) * TILE, TILE), bases[0]]
        forward(bases[0], 0)
        for step in range(steps):
            if step + 1 < steps:
                forward(bases[(step + 1) // n_groups], step + 1)
            multiply(bases[step // n_groups], step)
            inverse(step)
            which = step // n_groups
            finish(sums[1 - which], before[which], step % n_groups, n_groups)
        return 0

    lax.fori_loop(0, rows // (2 * TILE), pair_step, 0)
    for part in range(n_groups):
        finish(sums[1], rows - TILE, part, n_groups)

    odd = lax.rem(device, 2)
    each = pair_slots // 2
    for i in range(each):
        for who, target in ((1 - odd, send_ref), (odd, own_ref)):
            left = kept[who * each + i].T
            for j in range(panel_slots):
                target[i * WIDE : (i + 1) * WIDE, j * WIDE : (j + 1) * WIDE] = jnp.dot(
                    left, kept[pair_slots + j], preferred_element_type=jnp.float32
                ).astype(target.dtype)
    for j in range(panel_slots):
        line = jnp.dot(marks, kept[pair_slots + j], preferred_element_type=jnp.float32)
        at = slice(j * WIDE, (j + 1) * WIDE)
        own_ref[each * WIDE : each * WIDE + 8, at] = line
        send_ref[each * WIDE :, at] = jnp.concatenate([line, line], axis=0).astype(send_ref.dtype)


def body(samples, targets, counts, bucket_ids, sign_bits):
    device = lax.axis_index("dp")
    n_dp, n_feat = lax.axis_size("dp"), lax.axis_size("feat")
    slots, width = samples.shape
    half = slots // 2
    total = half * n_dp
    rows = total // 2
    place = jnp.stack([device, lax.axis_index("feat"), device // 2]).astype(jnp.int32)
    scalars = [pl.BlockSpec(memory_space=pltpu.SMEM)] * 2
    vector = pl.BlockSpec(memory_space=pltpu.VMEM)

    message = jax.ShapeDtypeStruct((half + PAD + TAIL, width), jnp.bfloat16)
    own, other = pl.pallas_call(
        prepare_kernel,
        out_shape=(message, message),
        in_specs=scalars + [vector] * 2,
        out_specs=(vector, vector),
    )(place, counts, samples, targets.reshape(1, slots))

    def swap(block, bit):
        return lax.ppermute(block, "dp", [(i, i ^ bit) for i in range(n_dp)])

    blocks = [own, swap(other, 1)]
    for delta in range(2, n_dp):
        bits = [1 << i for i in range(1, n_dp.bit_length()) if delta >> i & 1]
        bit = bits[0] if delta % 2 else bits[-1]
        blocks.append(swap(blocks[delta ^ bit], bit))

    table = forward_tables(bucket_ids, sign_bits)
    ends_table, group_table = inverse_tables()
    ends_table, group_table = jnp.asarray(ends_table), jnp.asarray(group_table)
    own_columns, panel_columns = SK // n_dp, SK // n_feat
    kept_slots = 2 * own_columns // WIDE + panel_columns // WIDE + 1
    span = -(-(rows + half + 2 * PAD + 8) // 128) * 128
    mine, send = pl.pallas_call(
        main_kernel,
        out_shape=(
            jax.ShapeDtypeStruct((own_columns + 8, panel_columns), jnp.float32),
            jax.ShapeDtypeStruct((own_columns + 16, panel_columns), jnp.bfloat16),
        ),
        in_specs=scalars + [vector] * (n_dp + 3),
        out_specs=(vector, vector),
        scratch_shapes=[
            pltpu.SMEM((n_dp,), jnp.int32),
            pltpu.VMEM((span, width), jnp.float32),
            pltpu.VMEM((rows, 2 * width), jnp.bfloat16),
            pltpu.VMEM((rows, 128), jnp.float32),
            pltpu.VMEM((2, TILE, 6 * WIDE), jnp.float32),
            pltpu.VMEM((2, TILE, 2 * WIDE), jnp.bfloat16),
            pltpu.VMEM((TILE, SK), jnp.float32),
            pltpu.VMEM((TILE, SK), jnp.float32),
            pltpu.VMEM((kept_slots, rows, WIDE), jnp.bfloat16),
        ],
        compiler_params=pltpu.CompilerParams(vmem_limit_bytes=VMEM_BYTES),
        cost_estimate=pl.CostEstimate(flops=3 * 10**10, bytes_accessed=24 * 10**6, transcendentals=0),
    )(place, counts, *blocks, table, ends_table, group_table)
    theirs = swap(send, 1)
    gram = (mine[:own_columns] + theirs[:own_columns].astype(jnp.float32)) * (1.0 / total)
    zty = (mine[own_columns] + theirs[own_columns].astype(jnp.float32)) * total ** (-0.5)
    return gram, zty


def solution(mesh):
    placed = (P("dp", None), P("dp"), P(), P(), P())
    return jax.shard_map(
        body, mesh=mesh, in_specs=placed, out_specs=(P("dp", "feat"), P("feat")), check_vma=False
    )
```

time: 92.4 us -> 80.5 us (0.87)
  other arithmetic: 8.09 us -> 4.71 us
  local copies, waits for them, and re-layouts: 10.2 us -> 7.53 us
  Pallas kernels: 53.5 us -> 51.4 us
  between operations: 2.83 us -> 0.84 us
  waiting for transfers between devices: 10.8 us -> 9.72 us
    pallas_call x1 -> x2, Pallas kernels: 47.8 us -> 45.6 us  [the longest x1 43.8 us: body(): pl.pallas_call(main_kernel, out_shape=(jax.ShapeDtypeStruct((own_columns...]
    add x1 -> x0, other arithmetic: 2 us -> none  [body(): summed = mine + swap(send, 1)]
    slice x2 -> x0, local copies, waits for them, and re-layouts: 1.91 us -> none  [body(): low = message(samples[:half], targets[:half])]
    unnamed x23 -> x15, local copies, waits for them, and re-layouts: 6.86 us -> 5.39 us
    reshape x2 -> x1, local copies, waits for them, and re-layouts: 0.02 us -> 1.31 us  [body(): targets.reshape(1, slots)]
    ppermute x8, waiting for transfers between devices: 10.8 us -> 9.72 us  [swap(): return lax.ppermute(block, 'dp', [(i, i ^ bit) for i in range(n_dp)])]
  transfers between devices with their start and end apart: 8 -> 8, of which waited for: 3 -> 3; matrix products, arithmetic and copies ran while one was open for 4% -> 4% of each run, Pallas kernels for 6% -> 7%
where the time goes in v2:
time: 80.5 us; the launch traced here: 80.2 us
  Pallas kernels  51.4 us (64%)
  waiting for transfers between devices  9.72 us (12%)
  local copies, waits for them, and re-layouts  7.53 us (9%)
  starting transfers between devices  6.07 us (8%)
  other arithmetic  4.71 us (6%)
  between operations  0.84 us (1%)
    pallas_call x1, Pallas kernels, body(): pl.pallas_call(main_kernel, out_shape=(jax.ShapeDtypeStruct((own_columns...  43.8 us
    ppermute x8, waiting for transfers between devices, swap(): return lax.ppermute(block, 'dp', [(i, i ^ bit) for i in range(n_dp)])  9.72 us
    ppermute x8, starting transfers between devices, swap(): return lax.ppermute(block, 'dp', [(i, i ^ bit) for i in range(n_dp)])  6.07 us
    pallas_call x1, Pallas kernels, forward_tables(): pl.pallas_call(table_kernel, grid=(groups,), out_shape=jax.ShapeDtypeStru...  5.76 us
    unnamed x15, local copies, waits for them, and re-layouts  5.39 us
    pallas_call x1, Pallas kernels, body(): pl.pallas_call(prepare_kernel, out_shape=(message, message), in_specs=sca...  1.83 us
    mul x1, other arithmetic, body(): (mine[:own_columns] + theirs[:own_columns].astype(jnp.float32)) * (1.0 /...  1.66 us
  transfers between devices with their start and end apart: 8, of which 3 were waited for; matrix products, arithmetic and copies ran while one was open for 4% of the time, Pallas kernels for 7%

profile of v2, /device:TPU:0, one launch (start us, length us, event | category | flops | bytes accessed | tf_op | source)
XLA Modules:
  0.0 80.2 jit_solution(5213409532171277344)
XLA Ops:
  0.6 0.0 copy-start.1
  0.7 1.3 %reshape.80.targets_ref = bf16[1,768]{1,0:T(2,128)(2,1)} reshape(bf16[768]{0:T(1024)(128)(2,1)} %param.10) | data formatting | bytes 3072 | tf_op jit(solution)/shard_map/reshape | solution.py:369
  2.0 0.6 pad_add_fusion.place_ref
  2.6 1.8 %shard_map.104 = (bf16[416,256]{1,0:T(8,128)(2,1)}, bf16[416,256]{1,0:T(8,128)(2,1)}) custom-call(s32[3]{0:T(128)} %pad_add_fusion.place_ref, s32[8]{0:T(128)} %counts_ref.3, bf16[768,256]{1,0:T(8,128)(2,1)} %samples_ref.1, bf16[1,768]{1,0:T(2,128)(2,1)} %reshape.80.targets_ref), custom_call_target="tpu_custom_call" | custom-call | tf_op jit(solution)/shard_map/pallas_call | solution.py:364
  4.4 3.0 %collective-permute-start.3 = (bf16[416,256]{1,0:T(8,128)(2,1)}, bf16[416,256]{1,0:T(8,128)(2,1)S(1)}, u32[]{:S(2)}, u32[]{:S(2)}) collective-permute-start(bf16[416,256]{1,0:T(8,128)(2,1)} %get-tuple-element.6.refs_0_), channel_id=1, source_target_pairs={{0,16},{4,20},{8,24},{12,28},{16,0},{20,4},{24,8},{28,12},{1,17},{... | collective-permute-start | bytes 638984 | tf_op jit(solution)/shard_map/ppermute | solution.py:372
  7.4 1.5 %collective-permute-start.1 = (bf16[416,256]{1,0:T(8,128)(2,1)}, bf16[416,256]{1,0:T(8,128)(2,1)S(1)}, u32[]{:S(2)}, u32[]{:S(2)}) collective-permute-start(bf16[416,256]{1,0:T(8,128)(2,1)} %get-tuple-element.6.refs_0_), channel_id=1, source_target_pairs={{0,8},{4,12},{8,0},{12,4},{16,24},{20,28},{24,16},{28,20},{1,9},{5... | collective-permute-start | bytes 638984 | tf_op jit(solution)/shard_map/ppermute | solution.py:372
  8.9 0.0 collective-permute-start
  8.9 0.7 add_convert_fusion
  9.6 0.1 copy.33
  9.7 0.1 copy.34
  9.8 0.8 %copy.32 = s32[3,256]{0,1:T(8,128)S(1)} copy(s32[3,256]{1,0:T(4,128)} %param.12) | data formatting | bytes 6144 | tf_op args[3]
  10.6 0.1 bitcast_negate_fusion
  10.7 0.1 copy.35
  10.8 0.1 copy.36
  10.9 1.0 %cosine_multiply_fusion = (f32[8,256,2,3,1]{1,0,4,3,2:T(8,128)S(1)}, f32[8,256,2,3,1]{1,0,4,3,2:T(8,128)S(1)}) fusion(s32[8,2]{0,1:T(2,128)} %constant.80.clone, s32[256,3]{0,1:T(4,128)S(1)} %copy.35, f32[256,3]{0,1:T(4,128)S(1)} %copy.34, f32[256,3]{0,1:T(4,128)S(1)} %copy.36), kind=kLoop, calls=%fused_computation.21 | loop fusion | flops 196608 | bytes 107584 | tf_op jit(solution)/shard_map/mul | solution.py:115
  11.9 0.1 copy.37
  12.0 0.0 collective-permute-done.refs_1_
  12.0 0.6 collective-permute-start.4
  12.5 0.1 add_select_fusion.1
  12.6 0.1 collective-permute-start.2
  12.7 1.6 %collective-permute-done.1.refs_2_ = bf16[416,256]{1,0:T(8,128)(2,1)S(1)} collective-permute-done((bf16[416,256]{1,0:T(8,128)(2,1)}, bf16[416,256]{1,0:T(8,128)(2,1)S(1)}, u32[]{:S(2)}, u32[]{:S(2)}) %collective-permute-start.1) | collective-permute-done | bytes 213024 | tf_op jit(solution)/shard_map/ppermute | solution.py:372
  14.3 0.4 collective-permute-start.5
  14.7 5.4 %collective-permute-done.4.refs_5_ = bf16[416,256]{1,0:T(8,128)(2,1)S(1)} collective-permute-done((bf16[416,256]{1,0:T(8,128)(2,1)S(1)}, bf16[416,256]{1,0:T(8,128)(2,1)S(1)}, u32[]{:S(2)}, u32[]{:S(2)}) %collective-permute-start.4) | collective-permute-done | bytes 213024 | tf_op jit(solution)/shard_map/ppermute | solution.py:372
  20.1 0.5 collective-permute-start.6
  20.6 0.4 copy.38.phase_ref
  21.0 0.0 copy-done.1
  21.0 0.0 copy-start.2
  21.0 0.0 copy-start.3
  21.1 0.0 copy-start.4
  21.1 0.0 copy-start.5
  21.1 0.0 copy-start.6
  21.1 5.8 %shard_map.105.refs_8_ = bf16[8,512,1536]{2,1,0:T(8,128)(2,1)S(1)} custom-call(s32[256,8]{1,0:T(8,128)S(1)} %pad.4.bucket_ref, f32[8,256,15]{2,1,0:T(8,128)S(1)} %copy.38.phase_ref, bf16[256,768]{1,0:T(8,128)(2,1)S(1)} %copy-done.1), custom_call_target="tpu_custom_call" | custom-call | flops 2000000000 | bytes 14000000 | tf_op jit(solution)/shard_map/pallas_call | solution.py:121
  26.9 0.0 copy-start
  26.9 4.5 %copy-done = bf16[8,512,1536]{2,1,0:T(8,128)(2,1)} copy-done((bf16[8,512,1536]{2,1,0:T(8,128)(2,1)}, bf16[8,512,1536]{2,1,0:T(8,128)(2,1)S(1)}, u32[]{:S(2)}) %copy-start) | copy-done | bytes 12582936
  31.4 0.0 collective-permute-done.3.refs_4_
  31.4 0.0 collective-permute-done.2.refs_3_
  31.4 0.0 collective-permute-done.5.refs_6_
  31.4 0.0 collective-permute-done.6.refs_7_
  31.4 0.0 copy-done.2
  31.4 0.0 copy-done.3
  31.4 0.0 copy-done.4
  31.4 0.0 copy-done.5
  31.5 0.0 copy-done.6
  31.5 43.8 %shard_map.106 = (f32[520,1024]{1,0:T(8,128)S(1)}, bf16[528,1024]{1,0:T(8,128)(2,1)S(1)}) custom-call(s32[3]{0:T(128)S(1)} %copy-done.2, s32[8]{0:T(128)S(1)} %copy-done.3, bf16[416,256]{1,0:T(8,128)(2,1)S(1)} %copy-done.4, bf16[416,256]{1,0:T(8,128)(2,1)S(1)} %collective-permute-done.refs_1_, bf16[416,256]{1,0:T(8,128)(2,1)S(1)} %collective-permute-done.1.refs_2_, ...), custom_call_target="tpu_custom_call" | custom-call | flops 30000001024 | bytes 24000000 | tf_op jit(solution)/shard_map/pallas_call | solution.py:386
  75.2 0.0 collective-permute-start.7
  75.2 2.7 %collective-permute-done.7 = bf16[528,1024]{1,0:T(8,128)(2,1)S(1)} collective-permute-done((bf16[528,1024]{1,0:T(8,128)(2,1)S(1)}, bf16[528,1024]{1,0:T(8,128)(2,1)S(1)}, u32[]{:S(2)}, u32[]{:S(2)}) %collective-permute-start.7) | collective-permute-done | bytes 1081376 | tf_op jit(solution)/shard_map/ppermute | solution.py:372
  78.0 0.6 fusion.8
  78.6 1.7 %add_multiply_fusion = f32[512,1024]{1,0:T(8,128)} fusion(f32[520,1024]{1,0:T(8,128)S(1)} %get-tuple-element.8, bf16[528,1024]{1,0:T(8,128)(2,1)S(1)} %collective-permute-done.7), kind=kLoop, calls=%fused_computation | loop fusion | flops 1572864 | bytes 5242880 | tf_op jit(solution)/shard_map/mul | solution.py:409
  (4 shorter events, 0.0 us)
Async XLA Ops:
  0.6 20.4 %copy-start.1 = (bf16[256,768]{1,0:T(8,128)(2,1)S(1)}, bf16[256,768]{1,0:T(8,128)(2,1)}, u32[]{:S(2)}) copy-start(bf16[256,768]{1,0:T(8,128)(2,1)} %constant.81.clone.dft_ref) | copy-start | bytes 1179652
  4.4 27.0 %collective-permute-start.3 = (bf16[416,256]{1,0:T(8,128)(2,1)}, bf16[416,256]{1,0:T(8,128)(2,1)S(1)}, u32[]{:S(2)}, u32[]{:S(2)}) collective-permute-start(bf16[416,256]{1,0:T(8,128)(2,1)} %get-tuple-element.6.refs_0_), channel_id=1, source_target_pairs={{0,16},{4,20},{8,24},{12,28},{16,0},{20,4},{24,8},{28,12},{1,17},{... | collective-permute-start | bytes 638984 | tf_op jit(solution)/shard_map/ppermute | solution.py:372
  7.4 6.9 %collective-permute-start.1 = (bf16[416,256]{1,0:T(8,128)(2,1)}, bf16[416,256]{1,0:T(8,128)(2,1)S(1)}, u32[]{:S(2)}, u32[]{:S(2)}) collective-permute-start(bf16[416,256]{1,0:T(8,128)(2,1)} %get-tuple-element.6.refs_0_), channel_id=1, source_target_pairs={{0,8},{4,12},{8,0},{12,4},{16,24},{20,28},{24,16},{28,20},{1,9},{5... | collective-permute-start | bytes 638984 | tf_op jit(solution)/shard_map/ppermute | solution.py:372
  8.9 3.1 %collective-permute-start = (bf16[416,256]{1,0:T(8,128)(2,1)}, bf16[416,256]{1,0:T(8,128)(2,1)S(1)}, u32[]{:S(2)}, u32[]{:S(2)}) collective-permute-start(bf16[416,256]{1,0:T(8,128)(2,1)} %get-tuple-element.7), channel_id=1, source_target_pairs={{0,4},{4,0},{8,12},{12,8},{16,20},{20,16},{24,28},{28,24},{1,5},{5... | collective-permute-start | bytes 638984 | tf_op jit(solution)/shard_map/ppermute | solution.py:372
  12.0 8.1 %collective-permute-start.4 = (bf16[416,256]{1,0:T(8,128)(2,1)S(1)}, bf16[416,256]{1,0:T(8,128)(2,1)S(1)}, u32[]{:S(2)}, u32[]{:S(2)}) collective-permute-start(bf16[416,256]{1,0:T(8,128)(2,1)S(1)} %collective-permute-done.refs_1_), channel_id=1, source_target_pairs={{0,16},{4,20},{8,24},{12,28},{16,0},{20,4},{24,8},{28,12},{1,17},{... | collective-permute-start | bytes 638984 | tf_op jit(solution)/shard_map/ppermute | solution.py:372
  12.6 18.8 %collective-permute-start.2 = (bf16[416,256]{1,0:T(8,128)(2,1)S(1)}, bf16[416,256]{1,0:T(8,128)(2,1)S(1)}, u32[]{:S(2)}, u32[]{:S(2)}) collective-permute-start(bf16[416,256]{1,0:T(8,128)(2,1)S(1)} %collective-permute-done.refs_1_), channel_id=1, source_target_pairs={{0,8},{4,12},{8,0},{12,4},{16,24},{20,28},{24,16},{28,20},{1,9},{5... | collective-permute-start | bytes 638984 | tf_op jit(solution)/shard_map/ppermute | solution.py:372
  14.3 17.1 %collective-permute-start.5 = (bf16[416,256]{1,0:T(8,128)(2,1)S(1)}, bf16[416,256]{1,0:T(8,128)(2,1)S(1)}, u32[]{:S(2)}, u32[]{:S(2)}) collective-permute-start(bf16[416,256]{1,0:T(8,128)(2,1)S(1)} %collective-permute-done.1.refs_2_), channel_id=1, source_target_pairs={{0,16},{4,20},{8,24},{12,28},{16,0},{20,4},{24,8},{28,12},{1,17},{... | collective-permute-start | bytes 638984 | tf_op jit(solution)/shard_map/ppermute | solution.py:372
  20.1 11.3 %collective-permute-start.6 = (bf16[416,256]{1,0:T(8,128)(2,1)S(1)}, bf16[416,256]{1,0:T(8,128)(2,1)S(1)}, u32[]{:S(2)}, u32[]{:S(2)}) collective-permute-start(bf16[416,256]{1,0:T(8,128)(2,1)S(1)} %collective-permute-done.4.refs_5_), channel_id=1, source_target_pairs={{0,8},{4,12},{8,0},{12,4},{16,24},{20,28},{24,16},{28,20},{1,9},{5... | collective-permute-start | bytes 638984 | tf_op jit(solution)/shard_map/ppermute | solution.py:372
  21.0 10.4 %copy-start.2 = (s32[3]{0:T(128)S(1)}, s32[3]{0:T(128)}, u32[]{:S(2)}) copy-start(s32[3]{0:T(128)} %pad_add_fusion.place_ref) | copy-start | bytes 40
  21.0 10.4 %copy-start.3 = (s32[8]{0:T(128)S(1)}, s32[8]{0:T(128)}, u32[]{:S(2)}) copy-start(s32[8]{0:T(128)} %counts_ref.3) | copy-start | bytes 100
  21.1 10.4 %copy-start.4 = (bf16[416,256]{1,0:T(8,128)(2,1)S(1)}, bf16[416,256]{1,0:T(8,128)(2,1)}, u32[]{:S(2)}) copy-start(bf16[416,256]{1,0:T(8,128)(2,1)} %get-tuple-element.6.refs_0_) | copy-start | bytes 638980
  21.1 10.4 %copy-start.5 = (bf16[7,512,512]{2,1,0:T(8,128)(2,1)S(1)}, bf16[7,512,512]{2,1,0:T(8,128)(2,1)}, u32[]{:S(2)}) copy-start(bf16[7,512,512]{2,1,0:T(8,128)(2,1)} %constant.83.clone.refs_10_) | copy-start | bytes 11010052
  21.1 10.4 %copy-start.6 = (bf16[256,512]{1,0:T(8,128)(2,1)S(1)}, bf16[256,512]{1,0:T(8,128)(2,1)}, u32[]{:S(2)}) copy-start(bf16[256,512]{1,0:T(8,128)(2,1)} %constant.82.clone.refs_9_) | copy-start | bytes 786436
  26.9 4.5 %copy-start = (bf16[8,512,1536]{2,1,0:T(8,128)(2,1)}, bf16[8,512,1536]{2,1,0:T(8,128)(2,1)S(1)}, u32[]{:S(2)}) copy-start(bf16[8,512,1536]{2,1,0:T(8,128)(2,1)S(1)} %shard_map.105.refs_8_) | copy-start | bytes 37748740
  75.2 2.7 %collective-permute-start.7 = (bf16[528,1024]{1,0:T(8,128)(2,1)S(1)}, bf16[528,1024]{1,0:T(8,128)(2,1)S(1)}, u32[]{:S(2)}, u32[]{:S(2)}) collective-permute-start(bf16[528,1024]{1,0:T(8,128)(2,1)S(1)} %get-tuple-element.9), channel_id=1, source_target_pairs={{0,4},{4,0},{8,12},{12,8},{16,20},{20,16},{24,28},{28,24},{1,5},{5... | collective-permute-start | bytes 3244040 | tf_op jit(solution)/shard_map/ppermute | solution.py:372

commit v3 on v2

--- a/solution.py
+++ b/solution.py
@@ -16,7 +16,7 @@
 TILE = 256
 TAIL = 16
 PAD = 16
-VMEM_BYTES = 36 * 1024 * 1024
+VMEM_BYTES = 25 * 1024 * 1024
 
 
 def split_bf16(values):
@@ -161,8 +161,8 @@
     return pl.multiple_of(jnp.minimum(first // PAD * PAD, slots - window), PAD)
 
 
-def prepare_kernel(place_ref, counts_ref, samples_ref, targets_ref, own_ref, other_ref):
-    device = place_ref[0]
+def prepare_kernel(counts_ref, samples_ref, targets_ref, own_ref, other_ref):
+    device = lax.axis_index("dp")
     core = lax.rem(device, 2)
     slots, width = samples_ref.shape
     window = slots // 2 + PAD
@@ -218,13 +218,14 @@
     return marks
 
 
-def main_kernel(place_ref, counts_ref, *refs):
+def main_kernel(counts_ref, *refs):
     count = counts_ref.shape[0]
     blocks = refs[:count]
     table, ends_table, groups_table, own_ref, send_ref = refs[count : count + 5]
     ends_ref, loose, rows2, cube, spectra, products, sums_a, sums_b, kept = refs[count + 5 :]
     sums = (sums_a, sums_b)
-    device, panel, pair_panel = place_ref[0], place_ref[1], place_ref[2]
+    device, panel = lax.axis_index("dp"), lax.axis_index("feat")
+    pair_panel = device // 2
     n_groups = RADIX // 2
     width = rows2.shape[1] // 2
     slots = 2 * (blocks[0].shape[0] - TAIL - PAD)
@@ -350,14 +351,12 @@
 
 
 def body(samples, targets, counts, bucket_ids, sign_bits):
-    device = lax.axis_index("dp")
     n_dp, n_feat = lax.axis_size("dp"), lax.axis_size("feat")
     slots, width = samples.shape
     half = slots // 2
     total = half * n_dp
     rows = total // 2
-    place = jnp.stack([device, lax.axis_index("feat"), device // 2]).astype(jnp.int32)
-    scalars = [pl.BlockSpec(memory_space=pltpu.SMEM)] * 2
+    scalars = [pl.BlockSpec(memory_space=pltpu.SMEM)]
     vector = pl.BlockSpec(memory_space=pltpu.VMEM)
 
     message = jax.ShapeDtypeStruct((half + PAD + TAIL, width), jnp.bfloat16)
@@ -366,7 +365,7 @@
         out_shape=(message, message),
         in_specs=scalars + [vector] * 2,
         out_specs=(vector, vector),
-    )(place, counts, samples, targets.reshape(1, slots))
+    )(counts, samples, targets.reshape(1, slots))
 
     def swap(block, bit):
         return lax.ppermute(block, "dp", [(i, i ^ bit) for i in range(n_dp)])
@@ -404,7 +403,7 @@
         ],
         compiler_params=pltpu.CompilerParams(vmem_limit_bytes=VMEM_BYTES),
         cost_estimate=pl.CostEstimate(flops=3 * 10**10, bytes_accessed=24 * 10**6, transcendentals=0),
-    )(place, counts, *blocks, table, ends_table, group_table)
+    )(counts, *blocks, table, ends_table, group_table)
     theirs = swap(send, 1)
     gram = (mine[:own_columns] + theirs[:own_columns].astype(jnp.float32)) * (1.0 / total)
     zty = (mine[own_columns] + theirs[own_columns].astype(jnp.float32)) * total ** (-0.5)

time: 80.5 us -> 73.1 us (0.908)
  local copies, waits for them, and re-layouts: 7.53 us -> 3 us
  Pallas kernels: 51.4 us -> 49.1 us
    unnamed x15 -> x11, local copies, waits for them, and re-layouts: 5.39 us -> 0.86 us
    pallas_call x1, Pallas kernels: 43.8 us -> 41.5 us  [body(): pl.pallas_call(main_kernel, out_shape=(jax.ShapeDtypeStruct((own_columns...]
  transfers between devices with their start and end apart: 8 -> 8, of which waited for: 3 -> 3; matrix products, arithmetic and copies ran while one was open for 4% -> 5% of each run, Pallas kernels for 7% -> 8%
where the time goes in v3:
time: 73.1 us; the launch traced here: 72.8 us
  Pallas kernels  49.1 us (67%)
  waiting for transfers between devices  9.72 us (13%)
  starting transfers between devices  6.07 us (8%)
  other arithmetic  4.1 us (6%)
  local copies, waits for them, and re-layouts  3 us (4%)
  between operations  0.82 us (1%)
    pallas_call x1, Pallas kernels, body(): pl.pallas_call(main_kernel, out_shape=(jax.ShapeDtypeStruct((own_columns...  41.5 us
    ppermute x8, waiting for transfers between devices, swap(): return lax.ppermute(block, 'dp', [(i, i ^ bit) for i in range(n_dp)])  9.72 us
    ppermute x8, starting transfers between devices, swap(): return lax.ppermute(block, 'dp', [(i, i ^ bit) for i in range(n_dp)])  6.07 us
    pallas_call x1, Pallas kernels, forward_tables(): pl.pallas_call(table_kernel, grid=(groups,), out_shape=jax.ShapeDtypeStru...  5.76 us
    pallas_call x1, Pallas kernels, body(): pl.pallas_call(prepare_kernel, out_shape=(message, message), in_specs=sca...  1.82 us
    mul x1, other arithmetic, body(): (mine[:own_columns] + theirs[:own_columns].astype(jnp.float32)) * (1.0 /...  1.69 us
  transfers between devices with their start and end apart: 8, of which 3 were waited for; matrix products, arithmetic and copies ran while one was open for 5% of the time, Pallas kernels for 8%

profile of v3, /device:TPU:0, one launch (start us, length us, event | category | flops | bytes accessed | tf_op | source)
XLA Modules:
  0.0 72.8 jit_solution(10466735249246238388)
XLA Ops:
  0.6 0.0 copy-start
  0.6 1.3 %reshape.80.targets_ref = bf16[1,768]{1,0:T(2,128)(2,1)} reshape(bf16[768]{0:T(1024)(128)(2,1)} %param.10) | data formatting | bytes 3072 | tf_op jit(solution)/shard_map/reshape | solution.py:368
  2.0 1.8 %shard_map.104 = (bf16[416,256]{1,0:T(8,128)(2,1)}, bf16[416,256]{1,0:T(8,128)(2,1)}) custom-call(s32[8]{0:T(128)} %counts_ref.3, bf16[768,256]{1,0:T(8,128)(2,1)} %samples_ref.1, bf16[1,768]{1,0:T(2,128)(2,1)} %reshape.80.targets_ref), custom_call_target="tpu_custom_call" | custom-call | tf_op jit(solution)/shard_map/pallas_call | solution.py:363
  3.8 3.0 %collective-permute-start.3 = (bf16[416,256]{1,0:T(8,128)(2,1)}, bf16[416,256]{1,0:T(8,128)(2,1)S(1)}, u32[]{:S(2)}, u32[]{:S(2)}) collective-permute-start(bf16[416,256]{1,0:T(8,128)(2,1)} %get-tuple-element.6.refs_0_), channel_id=1, source_target_pairs={{0,16},{4,20},{8,24},{12,28},{16,0},{20,4},{24,8},{28,12},{1,17},{... | collective-permute-start | bytes 638984 | tf_op jit(solution)/shard_map/ppermute | solution.py:371
  6.7 1.5 %collective-permute-start.1 = (bf16[416,256]{1,0:T(8,128)(2,1)}, bf16[416,256]{1,0:T(8,128)(2,1)S(1)}, u32[]{:S(2)}, u32[]{:S(2)}) collective-permute-start(bf16[416,256]{1,0:T(8,128)(2,1)} %get-tuple-element.6.refs_0_), channel_id=1, source_target_pairs={{0,8},{4,12},{8,0},{12,4},{16,24},{20,28},{24,16},{28,20},{1,9},{5... | collective-permute-start | bytes 638984 | tf_op jit(solution)/shard_map/ppermute | solution.py:371
  8.2 0.0 collective-permute-start
  8.2 0.7 add_convert_fusion
  8.9 0.1 copy.33
  9.1 0.1 copy.34
  9.1 0.8 %copy.32 = s32[3,256]{0,1:T(8,128)S(1)} copy(s32[3,256]{1,0:T(4,128)} %param.12) | data formatting | bytes 6144 | tf_op args[3]
  10.0 0.1 bitcast_negate_fusion
  10.1 0.1 copy.35
  10.1 0.1 copy.36
  10.2 1.0 %cosine_multiply_fusion = (f32[8,256,2,3,1]{1,0,4,3,2:T(8,128)S(1)}, f32[8,256,2,3,1]{1,0,4,3,2:T(8,128)S(1)}) fusion(s32[8,2]{0,1:T(2,128)} %constant.61.clone, s32[256,3]{0,1:T(4,128)S(1)} %copy.35, f32[256,3]{0,1:T(4,128)S(1)} %copy.34, f32[256,3]{0,1:T(4,128)S(1)} %copy.36), kind=kLoop, calls=%fused_computation.21 | loop fusion | flops 196608 | bytes 107584 | tf_op jit(solution)/shard_map/mul | solution.py:115
  11.2 0.1 copy.37
  11.3 0.0 collective-permute-done.refs_1_
  11.3 0.6 collective-permute-start.4
  11.9 0.1 add_select_fusion.1
  11.9 0.1 collective-permute-start.2
  12.0 1.6 %collective-permute-done.1.refs_2_ = bf16[416,256]{1,0:T(8,128)(2,1)S(1)} collective-permute-done((bf16[416,256]{1,0:T(8,128)(2,1)}, bf16[416,256]{1,0:T(8,128)(2,1)S(1)}, u32[]{:S(2)}, u32[]{:S(2)}) %collective-permute-start.1) | collective-permute-done | bytes 213024 | tf_op jit(solution)/shard_map/ppermute | solution.py:371
  13.7 0.4 collective-permute-start.5
  14.1 5.4 %collective-permute-done.4.refs_5_ = bf16[416,256]{1,0:T(8,128)(2,1)S(1)} collective-permute-done((bf16[416,256]{1,0:T(8,128)(2,1)S(1)}, bf16[416,256]{1,0:T(8,128)(2,1)S(1)}, u32[]{:S(2)}, u32[]{:S(2)}) %collective-permute-start.4) | collective-permute-done | bytes 213024 | tf_op jit(solution)/shard_map/ppermute | solution.py:371
  19.4 0.5 collective-permute-start.6
  20.0 0.4 copy.38.phase_ref
  20.4 0.0 copy-done
  20.4 0.0 copy-start.1
  20.4 0.0 copy-start.2
  20.4 0.0 copy-start.3
  20.4 0.0 copy-start.4
  20.4 5.8 %shard_map.105.refs_8_ = bf16[8,512,1536]{2,1,0:T(8,128)(2,1)S(1)} custom-call(s32[256,8]{1,0:T(8,128)S(1)} %pad.4.bucket_ref, f32[8,256,15]{2,1,0:T(8,128)S(1)} %copy.38.phase_ref, bf16[256,768]{1,0:T(8,128)(2,1)S(1)} %copy-done), custom_call_target="tpu_custom_call" | custom-call | flops 2000000000 | bytes 14000000 | tf_op jit(solution)/shard_map/pallas_call | solution.py:121
  26.2 0.0 collective-permute-done.3.refs_4_
  26.2 0.0 collective-permute-done.2.refs_3_
  26.2 0.0 collective-permute-done.5.refs_6_
  26.2 0.0 collective-permute-done.6.refs_7_
  26.2 0.0 copy-done.1
  26.2 0.0 copy-done.2
  26.3 0.0 copy-done.3
  26.3 0.0 copy-done.4
  26.3 41.5 %shard_map.106 = (f32[520,1024]{1,0:T(8,128)S(1)}, bf16[528,1024]{1,0:T(8,128)(2,1)S(1)}) custom-call(s32[8]{0:T(128)S(1)} %copy-done.1, bf16[416,256]{1,0:T(8,128)(2,1)S(1)} %copy-done.2, bf16[416,256]{1,0:T(8,128)(2,1)S(1)} %collective-permute-done.refs_1_, bf16[416,256]{1,0:T(8,128)(2,1)S(1)} %collective-permute-done.1.refs_2_, ...), custom_call_target="tpu_custom_call" | custom-call | flops 30000001024 | bytes 24000000 | tf_op jit(solution)/shard_map/pallas_call | solution.py:385
  67.8 0.0 collective-permute-start.7
  67.8 2.7 %collective-permute-done.7 = bf16[528,1024]{1,0:T(8,128)(2,1)S(1)} collective-permute-done((bf16[528,1024]{1,0:T(8,128)(2,1)S(1)}, bf16[528,1024]{1,0:T(8,128)(2,1)S(1)}, u32[]{:S(2)}, u32[]{:S(2)}) %collective-permute-start.7) | collective-permute-done | bytes 1081376 | tf_op jit(solution)/shard_map/ppermute | solution.py:371
  70.5 0.6 fusion.8
  71.1 1.7 %add_multiply_fusion = f32[512,1024]{1,0:T(8,128)} fusion(f32[520,1024]{1,0:T(8,128)S(1)} %get-tuple-element.8, bf16[528,1024]{1,0:T(8,128)(2,1)S(1)} %collective-permute-done.7), kind=kLoop, calls=%fused_computation | loop fusion | flops 1572864 | bytes 5242880 | tf_op jit(solution)/shard_map/mul | solution.py:408
  (4 shorter events, 0.0 us)
Async XLA Ops:
  0.6 19.7 %copy-start = (bf16[256,768]{1,0:T(8,128)(2,1)S(1)}, bf16[256,768]{1,0:T(8,128)(2,1)}, u32[]{:S(2)}) copy-start(bf16[256,768]{1,0:T(8,128)(2,1)} %constant.62.clone.dft_ref) | copy-start | bytes 1179652
  3.8 22.4 %collective-permute-start.3 = (bf16[416,256]{1,0:T(8,128)(2,1)}, bf16[416,256]{1,0:T(8,128)(2,1)S(1)}, u32[]{:S(2)}, u32[]{:S(2)}) collective-permute-start(bf16[416,256]{1,0:T(8,128)(2,1)} %get-tuple-element.6.refs_0_), channel_id=1, source_target_pairs={{0,16},{4,20},{8,24},{12,28},{16,0},{20,4},{24,8},{28,12},{1,17},{... | collective-permute-start | bytes 638984 | tf_op jit(solution)/shard_map/ppermute | solution.py:371
  6.7 6.9 %collective-permute-start.1 = (bf16[416,256]{1,0:T(8,128)(2,1)}, bf16[416,256]{1,0:T(8,128)(2,1)S(1)}, u32[]{:S(2)}, u32[]{:S(2)}) collective-permute-start(bf16[416,256]{1,0:T(8,128)(2,1)} %get-tuple-element.6.refs_0_), channel_id=1, source_target_pairs={{0,8},{4,12},{8,0},{12,4},{16,24},{20,28},{24,16},{28,20},{1,9},{5... | collective-permute-start | bytes 638984 | tf_op jit(solution)/shard_map/ppermute | solution.py:371
  8.2 3.1 %collective-permute-start = (bf16[416,256]{1,0:T(8,128)(2,1)}, bf16[416,256]{1,0:T(8,128)(2,1)S(1)}, u32[]{:S(2)}, u32[]{:S(2)}) collective-permute-start(bf16[416,256]{1,0:T(8,128)(2,1)} %get-tuple-element.7), channel_id=1, source_target_pairs={{0,4},{4,0},{8,12},{12,8},{16,20},{20,16},{24,28},{28,24},{1,5},{5... | collective-permute-start | bytes 638984 | tf_op jit(solution)/shard_map/ppermute | solution.py:371
  11.3 8.1 %collective-permute-start.4 = (bf16[416,256]{1,0:T(8,128)(2,1)S(1)}, bf16[416,256]{1,0:T(8,128)(2,1)S(1)}, u32[]{:S(2)}, u32[]{:S(2)}) collective-permute-start(bf16[416,256]{1,0:T(8,128)(2,1)S(1)} %collective-permute-done.refs_1_), channel_id=1, source_target_pairs={{0,16},{4,20},{8,24},{12,28},{16,0},{20,4},{24,8},{28,12},{1,17},{... | collective-permute-start | bytes 638984 | tf_op jit(solution)/shard_map/ppermute | solution.py:371
  11.9 14.3 %collective-permute-start.2 = (bf16[416,256]{1,0:T(8,128)(2,1)S(1)}, bf16[416,256]{1,0:T(8,128)(2,1)S(1)}, u32[]{:S(2)}, u32[]{:S(2)}) collective-permute-start(bf16[416,256]{1,0:T(8,128)(2,1)S(1)} %collective-permute-done.refs_1_), channel_id=1, source_target_pairs={{0,8},{4,12},{8,0},{12,4},{16,24},{20,28},{24,16},{28,20},{1,9},{5... | collective-permute-start | bytes 638984 | tf_op jit(solution)/shard_map/ppermute | solution.py:371
  13.7 12.6 %collective-permute-start.5 = (bf16[416,256]{1,0:T(8,128)(2,1)S(1)}, bf16[416,256]{1,0:T(8,128)(2,1)S(1)}, u32[]{:S(2)}, u32[]{:S(2)}) collective-permute-start(bf16[416,256]{1,0:T(8,128)(2,1)S(1)} %collective-permute-done.1.refs_2_), channel_id=1, source_target_pairs={{0,16},{4,20},{8,24},{12,28},{16,0},{20,4},{24,8},{28,12},{1,17},{... | collective-permute-start | bytes 638984 | tf_op jit(solution)/shard_map/ppermute | solution.py:371
  19.4 6.8 %collective-permute-start.6 = (bf16[416,256]{1,0:T(8,128)(2,1)S(1)}, bf16[416,256]{1,0:T(8,128)(2,1)S(1)}, u32[]{:S(2)}, u32[]{:S(2)}) collective-permute-start(bf16[416,256]{1,0:T(8,128)(2,1)S(1)} %collective-permute-done.4.refs_5_), channel_id=1, source_target_pairs={{0,8},{4,12},{8,0},{12,4},{16,24},{20,28},{24,16},{28,20},{1,9},{5... | collective-permute-start | bytes 638984 | tf_op jit(solution)/shard_map/ppermute | solution.py:371
  20.4 5.9 %copy-start.1 = (s32[8]{0:T(128)S(1)}, s32[8]{0:T(128)}, u32[]{:S(2)}) copy-start(s32[8]{0:T(128)} %counts_ref.3) | copy-start | bytes 100
  20.4 5.9 %copy-start.2 = (bf16[416,256]{1,0:T(8,128)(2,1)S(1)}, bf16[416,256]{1,0:T(8,128)(2,1)}, u32[]{:S(2)}) copy-start(bf16[416,256]{1,0:T(8,128)(2,1)} %get-tuple-element.6.refs_0_) | copy-start | bytes 638980
  20.4 5.9 %copy-start.3 = (bf16[7,512,512]{2,1,0:T(8,128)(2,1)S(1)}, bf16[7,512,512]{2,1,0:T(8,128)(2,1)}, u32[]{:S(2)}) copy-start(bf16[7,512,512]{2,1,0:T(8,128)(2,1)} %constant.64.clone.refs_10_) | copy-start | bytes 11010052
  20.4 5.9 %copy-start.4 = (bf16[256,512]{1,0:T(8,128)(2,1)S(1)}, bf16[256,512]{1,0:T(8,128)(2,1)}, u32[]{:S(2)}) copy-start(bf16[256,512]{1,0:T(8,128)(2,1)} %constant.63.clone.refs_9_) | copy-start | bytes 786436
  67.8 2.7 %collective-permute-start.7 = (bf16[528,1024]{1,0:T(8,128)(2,1)S(1)}, bf16[528,1024]{1,0:T(8,128)(2,1)S(1)}, u32[]{:S(2)}, u32[]{:S(2)}) collective-permute-start(bf16[528,1024]{1,0:T(8,128)(2,1)S(1)} %get-tuple-element.9), channel_id=1, source_target_pairs={{0,4},{4,0},{8,12},{12,8},{16,20},{20,16},{24,28},{28,24},{1,5},{5... | collective-permute-start | bytes 3244040 | tf_op jit(solution)/shard_map/ppermute | solution.py:371

commit v4 on v3

--- a/solution.py
+++ b/solution.py
@@ -16,12 +16,8 @@
 TILE = 256
 TAIL = 16
 PAD = 16
+LOW = jnp.float8_e5m2
 VMEM_BYTES = 25 * 1024 * 1024
-
-
-def split_bf16(values):
-    high = values.astype(jnp.bfloat16)
-    return high, (values - high.astype(np.float32)).astype(jnp.bfloat16)
 
 
 def short_dft():
@@ -66,7 +62,7 @@
     return ends.astype(jnp.bfloat16), np.stack(groups).astype(jnp.bfloat16)
 
 
-def table_kernel(bucket_ref, phase_ref, dft_ref, out_ref, base_ref):
+def table_kernel(bucket_ref, phase_ref, dft_ref, high_ref, low_ref, base_ref):
     group = pl.program_id(0)
     sketches, features_in = 3, bucket_ref.shape[0]
 
@@ -97,9 +93,8 @@
             for part, values in enumerate((real, imag)):
                 start = (2 * k + part) * WIDE + side * HALF
                 high = values.astype(jnp.bfloat16)
-                low = (values - high.astype(jnp.float32)).astype(jnp.bfloat16)
-                out_ref[0, :features_in, start : start + HALF] = high
-                out_ref[0, features_in:, start : start + HALF] = low
+                high_ref[0, :, start : start + HALF] = high
+                low_ref[0, :, start : start + HALF] = (values - high.astype(jnp.float32)).astype(LOW)
 
 
 def forward_tables(bucket_ids, sign_bits):
@@ -121,13 +116,16 @@
     return pl.pallas_call(
         table_kernel,
         grid=(groups,),
-        out_shape=jax.ShapeDtypeStruct((groups, 2 * features_in, 6 * WIDE), jnp.bfloat16),
+        out_shape=(
+            jax.ShapeDtypeStruct((groups, features_in, 6 * WIDE), jnp.bfloat16),
+            jax.ShapeDtypeStruct((groups, features_in, 6 * WIDE), LOW),
+        ),
         in_specs=[
             pl.BlockSpec(short.shape, lambda g: (0, 0)),
             pl.BlockSpec((1, features_in, 15), lambda g: (g, 0, 0)),
             pl.BlockSpec(dft.shape, lambda g: (0, 0)),
         ],
-        out_specs=pl.BlockSpec((1, 2 * features_in, 6 * WIDE), lambda g: (g, 0, 0)),
+        out_specs=(pl.BlockSpec((1, features_in, 6 * WIDE), lambda g: (g, 0, 0)),) * 2,
         scratch_shapes=[pltpu.VMEM((6, features_in, HALF), jnp.float32)],
         compiler_params=pltpu.CompilerParams(vmem_limit_bytes=VMEM_BYTES // 2),
         cost_estimate=pl.CostEstimate(flops=2 * 10**9, bytes_accessed=14 * 10**6, transcendentals=0),
@@ -180,7 +178,7 @@
         target[window:, :] = tail
 
 
-def gather_rows(device, counts_ref, ends_ref, blocks, slots, loose, width):
+def gather_rows(device, counts_ref, ends_ref, blocks, slots, loose, width, with_marks):
     core = lax.rem(device, 2)
     window = slots // 2 + PAD
     span = loose.shape[0]
@@ -191,7 +189,7 @@
         total = total + counts_ref[j]
         ends_ref[j] = total
     at = jnp.int32(0)
-    for delta, block_ref in enumerate(blocks):
+    for delta, block_ref in blocks:
         source = lax.bitwise_xor(device, delta)
         end = ends_ref[source]
         start = end - counts_ref[source]
@@ -209,41 +207,47 @@
         keep = lax.broadcasted_iota(jnp.int32, (edge, width), 0) < spill + skip
         loose[pl.ds(begin, edge), :] = jnp.where(keep, loose[pl.ds(begin, edge), :], block[:edge])
         loose[pl.ds(begin + edge, window + 8 - edge), :] = block[edge:]
+        here, at = at, at + share
+        if not with_marks:
+            continue
         tail = block_ref[window:, :].astype(jnp.float32)
         line = jnp.concatenate([tail[i : i + 1, :] for i in range(slots // width)], axis=1)
         line = jnp.concatenate([line, jnp.zeros((1, span - slots), jnp.float32)], axis=1)
-        line = pltpu.roll(jnp.broadcast_to(line, (8, span)), lax.rem(at - first + span, span), 1)
-        marks = jnp.where((lane >= at) & (lane < at + share), line, marks)
-        at = at + share
+        line = pltpu.roll(jnp.broadcast_to(line, (8, span)), lax.rem(here - first + span, span), 1)
+        marks = jnp.where((lane >= here) & (lane < at), line, marks)
     return marks
 
 
-def main_kernel(counts_ref, *refs):
-    count = counts_ref.shape[0]
-    blocks = refs[:count]
-    table, ends_table, groups_table, own_ref, send_ref = refs[count : count + 5]
-    ends_ref, loose, rows2, cube, spectra, products, sums_a, sums_b, kept = refs[count + 5 :]
+def main_kernel(deltas, first, final, counts_ref, *refs):
+    count = len(deltas)
+    blocks = list(zip(deltas, refs[:count]))
+    high_table, low_table, ends_table, groups_table = refs[count : count + 4]
+    if final:
+        early = refs[count + 4] if first else None
+        refs = refs[count + (5 if first else 4) :]
+        own_ref, send_ref, kept = refs[0], refs[1], refs[-1]
+        ends_ref, loose, rows2, rows_low, cube, spectra, products, sums_a, sums_b = refs[2:-1]
+    else:
+        kept, ends_ref, loose, rows2, rows_low, cube, spectra, products, sums_a, sums_b = refs[count + 4 :]
     sums = (sums_a, sums_b)
     device, panel = lax.axis_index("dp"), lax.axis_index("feat")
     pair_panel = device // 2
     n_groups = RADIX // 2
-    width = rows2.shape[1] // 2
-    slots = 2 * (blocks[0].shape[0] - TAIL - PAD)
+    width = rows2.shape[1]
+    slots = 2 * (blocks[0][1].shape[0] - TAIL - PAD)
     rows = rows2.shape[0]
-    pair_slots = own_ref.shape[0] // WIDE * 2
-    panel_slots = own_ref.shape[1] // WIDE
+    pair_slots = 2 * SK // WIDE // lax.axis_size("dp")
+    panel_slots = SK // WIDE // lax.axis_size("feat")
     junk = pair_slots + panel_slots
 
-    marks = gather_rows(device, counts_ref, ends_ref, blocks, slots, loose, width)
-    marks = marks[:, :rows].astype(jnp.bfloat16)
+    marks = gather_rows(device, counts_ref, ends_ref, blocks, slots, loose, width, final)
     for t in range(rows // TILE):
-        values = loose[PAD + t * TILE : PAD + (t + 1) * TILE, :]
+        values = loose[PAD + first + t * TILE : PAD + first + (t + 1) * TILE, :]
         mean = jnp.sum(values * values, axis=1, keepdims=True) * (1.0 / width)
         factor = lax.rsqrt(mean + 1e-06) * width ** (-0.5)
         cube[t * TILE : (t + 1) * TILE, :] = jnp.broadcast_to(factor * factor * factor, (TILE, 128))
-        low = values.astype(jnp.bfloat16)
-        rows2[t * TILE : (t + 1) * TILE, :width] = low
-        rows2[t * TILE : (t + 1) * TILE, width:] = low
+        rows2[t * TILE : (t + 1) * TILE, :] = values.astype(jnp.bfloat16)
+        rows_low[t * TILE : (t + 1) * TILE, :] = values.astype(LOW)
 
     where_pair, where_panel = [], []
     for c in range(RADIX):
@@ -253,9 +257,10 @@
         where_panel.append(jnp.where((low >= 0) & (low < panel_slots), low + pair_slots, junk))
 
     def forward(base, step):
+        group, here = step % n_groups, pl.ds(base, TILE)
         spectra[step % 2] = jnp.dot(
-            rows2[pl.ds(base, TILE), :], table[step % n_groups], preferred_element_type=jnp.float32
-        )
+            rows2[here, :], high_table[group], preferred_element_type=jnp.float32
+        ) + jnp.dot(rows_low[here, :], low_table[group], preferred_element_type=jnp.float32)
 
     def multiply(base, step):
         group = step % n_groups
@@ -334,17 +339,24 @@
     for part in range(n_groups):
         finish(sums[1], rows - TILE, part, n_groups)
 
+    if not final:
+        return
     odd = lax.rem(device, 2)
     each = pair_slots // 2
+    marks = marks[:, : first + rows].astype(jnp.bfloat16)
     for i in range(each):
         for who, target in ((1 - odd, send_ref), (odd, own_ref)):
             left = kept[who * each + i].T
+            left_early = early[who * each + i].T if first else None
             for j in range(panel_slots):
-                target[i * WIDE : (i + 1) * WIDE, j * WIDE : (j + 1) * WIDE] = jnp.dot(
-                    left, kept[pair_slots + j], preferred_element_type=jnp.float32
-                ).astype(target.dtype)
+                block = jnp.dot(left, kept[pair_slots + j], preferred_element_type=jnp.float32)
+                if first:
+                    block += jnp.dot(left_early, early[pair_slots + j], preferred_element_type=jnp.float32)
+                target[i * WIDE : (i + 1) * WIDE, j * WIDE : (j + 1) * WIDE] = block.astype(target.dtype)
     for j in range(panel_slots):
-        line = jnp.dot(marks, kept[pair_slots + j], preferred_element_type=jnp.float32)
+        line = jnp.dot(marks[:, first:], kept[pair_slots + j], preferred_element_type=jnp.float32)
+        if first:
+            line += jnp.dot(marks[:, :first], early[pair_slots + j], preferred_element_type=jnp.float32)
         at = slice(j * WIDE, (j + 1) * WIDE)
         own_ref[each * WIDE : each * WIDE + 8, at] = line
         send_ref[each * WIDE :, at] = jnp.concatenate([line, line], axis=0).astype(send_ref.dtype)
@@ -370,40 +382,64 @@
     def swap(block, bit):
         return lax.ppermute(block, "dp", [(i, i ^ bit) for i in range(n_dp)])
 
-    blocks = [own, swap(other, 1)]
-    for delta in range(2, n_dp):
+    high_table, low_table = forward_tables(bucket_ids, sign_bits)
+    blocks = {0: own, 1: swap(other, 1)}
+    near = [0, 1]
+    for i in range(1, (n_dp - 1).bit_length()):
+        for core in range(2):
+            blocks[(1 << i) + core] = swap(blocks[core], 1 << i)
+            near.append((1 << i) + core)
+    far = [delta for delta in range(n_dp) if delta not in blocks]
+    sure = max(0, total - slots * len(far) - len(near)) // 2 if far else 0
+    first = min(sure, rows // 3) // (2 * TILE) * 2 * TILE
+    if first:
+        high_table, sources = lax.optimization_barrier((high_table, dict(blocks)))
+        blocks.update(sources)
+    for delta in far:
         bits = [1 << i for i in range(1, n_dp.bit_length()) if delta >> i & 1]
         bit = bits[0] if delta % 2 else bits[-1]
-        blocks.append(swap(blocks[delta ^ bit], bit))
-
-    table = forward_tables(bucket_ids, sign_bits)
+        blocks[delta] = swap(blocks[delta ^ bit], bit)
+
     ends_table, group_table = inverse_tables()
-    ends_table, group_table = jnp.asarray(ends_table), jnp.asarray(group_table)
+    tables = (high_table, low_table, jnp.asarray(ends_table), jnp.asarray(group_table))
     own_columns, panel_columns = SK // n_dp, SK // n_feat
     kept_slots = 2 * own_columns // WIDE + panel_columns // WIDE + 1
     span = -(-(rows + half + 2 * PAD + 8) // 128) * 128
-    mine, send = pl.pallas_call(
-        main_kernel,
-        out_shape=(
-            jax.ShapeDtypeStruct((own_columns + 8, panel_columns), jnp.float32),
-            jax.ShapeDtypeStruct((own_columns + 16, panel_columns), jnp.bfloat16),
-        ),
-        in_specs=scalars + [vector] * (n_dp + 3),
-        out_specs=(vector, vector),
-        scratch_shapes=[
+
+    def transform(deltas, begin, end, final, more):
+        size = end - begin
+        kept = (kept_slots, size, WIDE)
+        out_shape = jax.ShapeDtypeStruct(kept, jnp.bfloat16)
+        if final:
+            out_shape = (
+                jax.ShapeDtypeStruct((own_columns + 8, panel_columns), jnp.float32),
+                jax.ShapeDtypeStruct((own_columns + 16, panel_columns), jnp.bfloat16),
+            )
+        scratch = [
             pltpu.SMEM((n_dp,), jnp.int32),
             pltpu.VMEM((span, width), jnp.float32),
-            pltpu.VMEM((rows, 2 * width), jnp.bfloat16),
-            pltpu.VMEM((rows, 128), jnp.float32),
+            pltpu.VMEM((size, width), jnp.bfloat16),
+            pltpu.VMEM((size, width), LOW),
+            pltpu.VMEM((size, 128), jnp.float32),
             pltpu.VMEM((2, TILE, 6 * WIDE), jnp.float32),
             pltpu.VMEM((2, TILE, 2 * WIDE), jnp.bfloat16),
             pltpu.VMEM((TILE, SK), jnp.float32),
             pltpu.VMEM((TILE, SK), jnp.float32),
-            pltpu.VMEM((kept_slots, rows, WIDE), jnp.bfloat16),
-        ],
-        compiler_params=pltpu.CompilerParams(vmem_limit_bytes=VMEM_BYTES),
-        cost_estimate=pl.CostEstimate(flops=3 * 10**10, bytes_accessed=24 * 10**6, transcendentals=0),
-    )(counts, *blocks, table, ends_table, group_table)
+        ]
+        return pl.pallas_call(
+            functools.partial(main_kernel, deltas, begin, final),
+            out_shape=out_shape,
+            in_specs=scalars + [vector] * (len(deltas) + 4 + len(more)),
+            out_specs=(vector, vector) if final else vector,
+            scratch_shapes=scratch + ([pltpu.VMEM(kept, jnp.bfloat16)] if final else []),
+            compiler_params=pltpu.CompilerParams(vmem_limit_bytes=VMEM_BYTES),
+            cost_estimate=pl.CostEstimate(
+                flops=2 * 10**7 * size, bytes_accessed=24 * 10**6, transcendentals=0
+            ),
+        )(counts, *[blocks[delta] for delta in deltas], *tables, *more)
+
+    early = (transform(near, 0, first, False, ()),) if first else ()
+    mine, send = transform(near + far, first, rows, True, early)
     theirs = swap(send, 1)
     gram = (mine[:own_columns] + theirs[:own_columns].astype(jnp.float32)) * (1.0 / total)
     zty = (mine[own_columns] + theirs[own_columns].astype(jnp.float32)) * total ** (-0.5)

time: 73.1 us -> 69.2 us (0.947)
  waiting for transfers between devices: 9.72 us -> 3.69 us
  starting transfers between devices: 6.07 us -> 7.71 us
    ppermute x8, waiting for transfers between devices: 9.72 us -> 3.69 us  [swap(): return lax.ppermute(block, 'dp', [(i, i ^ bit) for i in range(n_dp)])]
    ppermute x8, starting transfers between devices: 6.07 us -> 7.71 us  [swap(): return lax.ppermute(block, 'dp', [(i, i ^ bit) for i in range(n_dp)])]
    pallas_call x2 -> x3, Pallas kernels: 47.3 us -> 47.8 us  [the longest x2 42 us: transform(): pl.pallas_call(functools.partial(main_kernel, deltas, begin, final), out_...]
  transfers between devices with their start and end apart: 8 -> 8, of which waited for: 3 -> 3; matrix products, arithmetic and copies ran while one was open for 5% -> 5% of each run, Pallas kernels for 8% -> 28%
where the time goes in v4:
time: 69.2 us; the launch traced here: 68.9 us
  Pallas kernels  49.6 us (72%)
  starting transfers between devices  7.71 us (11%)
  other arithmetic  4.1 us (6%)
  waiting for transfers between devices  3.69 us (5%)
  local copies, waits for them, and re-layouts  3.01 us (4%)
  between operations  0.81 us (1%)
    pallas_call x2, Pallas kernels, transform(): pl.pallas_call(functools.partial(main_kernel, deltas, begin, final), out_...  42 us
    ppermute x8, starting transfers between devices, swap(): return lax.ppermute(block, 'dp', [(i, i ^ bit) for i in range(n_dp)])  7.71 us
    pallas_call x1, Pallas kernels, forward_tables(): pl.pallas_call(table_kernel, grid=(groups,), out_shape=(jax.ShapeDtypeStr...  5.82 us
    ppermute x8, waiting for transfers between devices, swap(): return lax.ppermute(block, 'dp', [(i, i ^ bit) for i in range(n_dp)])  3.69 us
    pallas_call x1, Pallas kernels, body(): pl.pallas_call(prepare_kernel, out_shape=(message, message), in_specs=sca...  1.83 us
    mul x1, other arithmetic, body(): (mine[:own_columns] + theirs[:own_columns].astype(jnp.float32)) * (1.0 /...  1.69 us
  transfers between devices with their start and end apart: 8, of which 3 were waited for; matrix products, arithmetic and copies ran while one was open for 5% of the time, Pallas kernels for 28%

profile of v4, /device:TPU:0, one launch (start us, length us, event | category | flops | bytes accessed | tf_op | source)
XLA Modules:
  0.0 68.9 jit_solution(5657042623744612687)
XLA Ops:
  0.6 0.0 copy-start.3
  0.6 1.3 %reshape.81.targets_ref = bf16[1,768]{1,0:T(2,128)(2,1)} reshape(bf16[768]{0:T(1024)(128)(2,1)} %param.10) | data formatting | bytes 3072 | tf_op jit(solution)/shard_map/reshape | solution.py:380
  2.0 1.8 %shard_map.105 = (bf16[416,256]{1,0:T(8,128)(2,1)}, bf16[416,256]{1,0:T(8,128)(2,1)}) custom-call(s32[8]{0:T(128)} %counts_ref.5, bf16[768,256]{1,0:T(8,128)(2,1)} %samples_ref.1, bf16[1,768]{1,0:T(2,128)(2,1)} %reshape.81.targets_ref), custom_call_target="tpu_custom_call" | custom-call | tf_op jit(solution)/shard_map/pallas_call | solution.py:375
  3.8 3.0 %collective-permute-start.3 = (bf16[416,256]{1,0:T(8,128)(2,1)}, bf16[416,256]{1,0:T(8,128)(2,1)S(1)}, u32[]{:S(2)}, u32[]{:S(2)}) collective-permute-start(bf16[416,256]{1,0:T(8,128)(2,1)} %get-tuple-element.18.refs_0_), channel_id=1, source_target_pairs={{0,16},{4,20},{8,24},{12,28},{16,0},{20,4},{24,8},{28,12},{1,17},{... | collective-permute-start | bytes 638984 | tf_op jit(solution)/shard_map/ppermute | solution.py:383
  6.8 1.5 %collective-permute-start.1 = (bf16[416,256]{1,0:T(8,128)(2,1)}, bf16[416,256]{1,0:T(8,128)(2,1)S(1)}, u32[]{:S(2)}, u32[]{:S(2)}) collective-permute-start(bf16[416,256]{1,0:T(8,128)(2,1)} %get-tuple-element.18.refs_0_), channel_id=1, source_target_pairs={{0,8},{4,12},{8,0},{12,4},{16,24},{20,28},{24,16},{28,20},{1,9},{5... | collective-permute-start | bytes 638984 | tf_op jit(solution)/shard_map/ppermute | solution.py:383
  8.2 0.0 collective-permute-start
  8.2 0.7 %add_convert_fusion = f32[3,256]{1,0:T(4,128)S(1)} fusion(s32[3,256]{1,0:T(4,128)} %param.13), kind=kLoop, calls=%fused_computation.25 | loop fusion | flops 2304 | bytes 6144 | tf_op jit(solution)/shard_map/convert_element_type | solution.py:107
  8.9 0.1 copy.33
  9.1 0.1 copy.34
  9.2 0.8 %copy.32 = s32[3,256]{0,1:T(8,128)S(1)} copy(s32[3,256]{1,0:T(4,128)} %param.12) | data formatting | bytes 6144 | tf_op args[3]
  10.0 0.1 bitcast_negate_fusion
  10.1 0.1 copy.35
  10.2 0.1 copy.36
  10.2 0.1 copy.37
  10.3 1.0 %cosine_multiply_fusion = (f32[8,256,2,3,1]{1,0,4,3,2:T(8,128)S(1)}, f32[8,256,2,3,1]{1,0,4,3,2:T(8,128)S(1)}) fusion(s32[8,2]{0,1:T(2,128)} %constant.61.clone, s32[256,3]{0,1:T(4,128)S(1)} %copy.35, f32[256,3]{0,1:T(4,128)S(1)} %copy.34, f32[256,3]{0,1:T(4,128)S(1)} %copy.36), kind=kLoop, calls=%fused_computation.21 | loop fusion | flops 196608 | bytes 107584 | tf_op jit(solution)/shard_map/mul | solution.py:110
  11.3 0.1 add_select_fusion.1
  11.4 0.0 collective-permute-done.refs_1_
  11.4 0.6 collective-permute-start.4
  12.0 0.1 collective-permute-start.2
  12.1 0.4 copy.38.phase_ref
  12.5 0.0 copy-done.3
  12.5 0.0 copy-start
  12.5 0.0 copy-start.1
  12.5 0.0 copy-start.2
  12.5 0.0 copy-start.4
  12.5 5.8 %shard_map.104 = (bf16[8,256,1536]{2,1,0:T(8,128)(2,1)S(1)}, f8e5m2[8,256,1536]{2,1,0:T(32,128)(4,1)S(1)}) custom-call(s32[256,8]{1,0:T(8,128)S(1)} %pad.4.bucket_ref, f32[8,256,15]{2,1,0:T(8,128)S(1)} %copy.38.phase_ref, bf16[256,768]{1,0:T(8,128)(2,1)S(1)} %copy-done.3), custom_call_target="tpu_custom_call" | custom-call | flops 2000000000 | bytes 14000000 | tf_op jit(solution)/shard_map/pallas_call | solution.py:116
  18.4 0.0 collective-permute-done.3.refs_4_
  18.4 0.0 collective-permute-done.1.refs_2_
  18.4 0.7 %collective-permute-done.4.refs_5_ = bf16[416,256]{1,0:T(8,128)(2,1)S(1)} collective-permute-done((bf16[416,256]{1,0:T(8,128)(2,1)S(1)}, bf16[416,256]{1,0:T(8,128)(2,1)S(1)}, u32[]{:S(2)}, u32[]{:S(2)}) %collective-permute-start.4) | collective-permute-done | bytes 213024 | tf_op jit(solution)/shard_map/ppermute | solution.py:383
  19.1 0.2 collective-permute-done.2.refs_3_
  19.3 1.5 %collective-permute-start.5 = (bf16[416,256]{1,0:T(8,128)(2,1)S(1)}, bf16[416,256]{1,0:T(8,128)(2,1)S(1)}, u32[]{:S(2)}, u32[]{:S(2)}) collective-permute-start(bf16[416,256]{1,0:T(8,128)(2,1)S(1)} %collective-permute-done.1.refs_2_), channel_id=1, source_target_pairs={{0,16},{4,20},{8,24},{12,28},{16,0},{20,4},{24,8},{28,12},{1,17},{... | collective-permute-start | bytes 638984 | tf_op jit(solution)/shard_map/ppermute | solution.py:383
  20.9 1.0 %collective-permute-start.6 = (bf16[416,256]{1,0:T(8,128)(2,1)S(1)}, bf16[416,256]{1,0:T(8,128)(2,1)S(1)}, u32[]{:S(2)}, u32[]{:S(2)}) collective-permute-start(bf16[416,256]{1,0:T(8,128)(2,1)S(1)} %collective-permute-done.4.refs_5_), channel_id=1, source_target_pairs={{0,8},{4,12},{8,0},{12,4},{16,24},{20,28},{24,16},{28,20},{1,9},{5... | collective-permute-start | bytes 638984 | tf_op jit(solution)/shard_map/ppermute | solution.py:383
  21.9 0.0 copy-done
  21.9 0.0 copy-done.1
  21.9 0.0 copy-done.2
  21.9 0.0 copy-done.4
  21.9 13.3 %shard_map.106.refs_12_ = bf16[9,512,256]{2,1,0:T(8,128)(2,1)S(1)} custom-call(s32[8]{0:T(128)S(1)} %copy-done, bf16[416,256]{1,0:T(8,128)(2,1)S(1)} %copy-done.1, bf16[416,256]{1,0:T(8,128)(2,1)S(1)} %collective-permute-done.refs_1_, bf16[416,256]{1,0:T(8,128)(2,1)S(1)} %collective-permute-done.1.refs_2_, ...), custom_call_target="tpu_custom_call" | custom-call | flops 10240000000 | bytes 24000000 | tf_op jit(solution)/shard_map/pallas_call | solution.py:429
  35.3 0.0 collective-permute-done.5.refs_6_
  35.3 0.0 collective-permute-done.6.refs_7_
  35.3 28.6 %shard_map.107 = (f32[520,1024]{1,0:T(8,128)S(1)}, bf16[528,1024]{1,0:T(8,128)(2,1)S(1)}) custom-call(s32[8]{0:T(128)S(1)} %copy-done, bf16[416,256]{1,0:T(8,128)(2,1)S(1)} %copy-done.1, bf16[416,256]{1,0:T(8,128)(2,1)S(1)} %collective-permute-done.refs_1_, bf16[416,256]{1,0:T(8,128)(2,1)S(1)} %collective-permute-done.1.refs_2_, ...), custom_call_target="tpu_custom_call" | custom-call | flops 20480000000 | bytes 24000000 | tf_op jit(solution)/shard_map/pallas_call | solution.py:429
  63.9 0.0 collective-permute-start.7
  63.9 2.7 %collective-permute-done.7 = bf16[528,1024]{1,0:T(8,128)(2,1)S(1)} collective-permute-done((bf16[528,1024]{1,0:T(8,128)(2,1)S(1)}, bf16[528,1024]{1,0:T(8,128)(2,1)S(1)}, u32[]{:S(2)}, u32[]{:S(2)}) %collective-permute-start.7) | collective-permute-done | bytes 1081376 | tf_op jit(solution)/shard_map/ppermute | solution.py:383
  66.6 0.6 fusion.8
  67.2 1.7 %add_multiply_fusion = f32[512,1024]{1,0:T(8,128)} fusion(f32[520,1024]{1,0:T(8,128)S(1)} %get-tuple-element.26, bf16[528,1024]{1,0:T(8,128)(2,1)S(1)} %collective-permute-done.7), kind=kLoop, calls=%fused_computation | loop fusion | flops 1572864 | bytes 5242880 | tf_op jit(solution)/shard_map/mul | solution.py:444
  (4 shorter events, 0.0 us)
Async XLA Ops:
  0.6 11.8 %copy-start.3 = (bf16[256,768]{1,0:T(8,128)(2,1)S(1)}, bf16[256,768]{1,0:T(8,128)(2,1)}, u32[]{:S(2)}) copy-start(bf16[256,768]{1,0:T(8,128)(2,1)} %constant.62.clone.dft_ref) | copy-start | bytes 1179652
  3.8 14.6 %collective-permute-start.3 = (bf16[416,256]{1,0:T(8,128)(2,1)}, bf16[416,256]{1,0:T(8,128)(2,1)S(1)}, u32[]{:S(2)}, u32[]{:S(2)}) collective-permute-start(bf16[416,256]{1,0:T(8,128)(2,1)} %get-tuple-element.18.refs_0_), channel_id=1, source_target_pairs={{0,16},{4,20},{8,24},{12,28},{16,0},{20,4},{24,8},{28,12},{1,17},{... | collective-permute-start | bytes 638984 | tf_op jit(solution)/shard_map/ppermute | solution.py:383
  6.8 11.6 %collective-permute-start.1 = (bf16[416,256]{1,0:T(8,128)(2,1)}, bf16[416,256]{1,0:T(8,128)(2,1)S(1)}, u32[]{:S(2)}, u32[]{:S(2)}) collective-permute-start(bf16[416,256]{1,0:T(8,128)(2,1)} %get-tuple-element.18.refs_0_), channel_id=1, source_target_pairs={{0,8},{4,12},{8,0},{12,4},{16,24},{20,28},{24,16},{28,20},{1,9},{5... | collective-permute-start | bytes 638984 | tf_op jit(solution)/shard_map/ppermute | solution.py:383
  8.2 3.1 %collective-permute-start = (bf16[416,256]{1,0:T(8,128)(2,1)}, bf16[416,256]{1,0:T(8,128)(2,1)S(1)}, u32[]{:S(2)}, u32[]{:S(2)}) collective-permute-start(bf16[416,256]{1,0:T(8,128)(2,1)} %get-tuple-element.17), channel_id=1, source_target_pairs={{0,4},{4,0},{8,12},{12,8},{16,20},{20,16},{24,28},{28,24},{1,5},{5... | collective-permute-start | bytes 638984 | tf_op jit(solution)/shard_map/ppermute | solution.py:383
  11.4 7.7 %collective-permute-start.4 = (bf16[416,256]{1,0:T(8,128)(2,1)S(1)}, bf16[416,256]{1,0:T(8,128)(2,1)S(1)}, u32[]{:S(2)}, u32[]{:S(2)}) collective-permute-start(bf16[416,256]{1,0:T(8,128)(2,1)S(1)} %collective-permute-done.refs_1_), channel_id=1, source_target_pairs={{0,16},{4,20},{8,24},{12,28},{16,0},{20,4},{24,8},{28,12},{1,17},{... | collective-permute-start | bytes 638984 | tf_op jit(solution)/shard_map/ppermute | solution.py:383
  12.0 7.4 %collective-permute-start.2 = (bf16[416,256]{1,0:T(8,128)(2,1)S(1)}, bf16[416,256]{1,0:T(8,128)(2,1)S(1)}, u32[]{:S(2)}, u32[]{:S(2)}) collective-permute-start(bf16[416,256]{1,0:T(8,128)(2,1)S(1)} %collective-permute-done.refs_1_), channel_id=1, source_target_pairs={{0,8},{4,12},{8,0},{12,4},{16,24},{20,28},{24,16},{28,20},{1,9},{5... | collective-permute-start | bytes 638984 | tf_op jit(solution)/shard_map/ppermute | solution.py:383
  12.5 9.4 %copy-start = (s32[8]{0:T(128)S(1)}, s32[8]{0:T(128)}, u32[]{:S(2)}) copy-start(s32[8]{0:T(128)} %counts_ref.5) | copy-start | bytes 100
  12.5 9.4 %copy-start.1 = (bf16[416,256]{1,0:T(8,128)(2,1)S(1)}, bf16[416,256]{1,0:T(8,128)(2,1)}, u32[]{:S(2)}) copy-start(bf16[416,256]{1,0:T(8,128)(2,1)} %get-tuple-element.18.refs_0_) | copy-start | bytes 638980
  12.5 9.4 %copy-start.2 = (bf16[7,512,512]{2,1,0:T(8,128)(2,1)S(1)}, bf16[7,512,512]{2,1,0:T(8,128)(2,1)}, u32[]{:S(2)}) copy-start(bf16[7,512,512]{2,1,0:T(8,128)(2,1)} %constant.64.clone.refs_9_.refs_11_) | copy-start | bytes 11010052
  12.5 9.4 %copy-start.4 = (bf16[256,512]{1,0:T(8,128)(2,1)S(1)}, bf16[256,512]{1,0:T(8,128)(2,1)}, u32[]{:S(2)}) copy-start(bf16[256,512]{1,0:T(8,128)(2,1)} %constant.63.clone.refs_8_.refs_10_) | copy-start | bytes 786436
  19.3 15.9 %collective-permute-start.5 = (bf16[416,256]{1,0:T(8,128)(2,1)S(1)}, bf16[416,256]{1,0:T(8,128)(2,1)S(1)}, u32[]{:S(2)}, u32[]{:S(2)}) collective-permute-start(bf16[416,256]{1,0:T(8,128)(2,1)S(1)} %collective-permute-done.1.refs_2_), channel_id=1, source_target_pairs={{0,16},{4,20},{8,24},{12,28},{16,0},{20,4},{24,8},{28,12},{1,17},{... | collective-permute-start | bytes 638984 | tf_op jit(solution)/shard_map/ppermute | solution.py:383
  20.9 14.4 %collective-permute-start.6 = (bf16[416,256]{1,0:T(8,128)(2,1)S(1)}, bf16[416,256]{1,0:T(8,128)(2,1)S(1)}, u32[]{:S(2)}, u32[]{:S(2)}) collective-permute-start(bf16[416,256]{1,0:T(8,128)(2,1)S(1)} %collective-permute-done.4.refs_5_), channel_id=1, source_target_pairs={{0,8},{4,12},{8,0},{12,4},{16,24},{20,28},{24,16},{28,20},{1,9},{5... | collective-permute-start | bytes 638984 | tf_op jit(solution)/shard_map/ppermute | solution.py:383
  63.9 2.7 %collective-permute-start.7 = (bf16[528,1024]{1,0:T(8,128)(2,1)S(1)}, bf16[528,1024]{1,0:T(8,128)(2,1)S(1)}, u32[]{:S(2)}, u32[]{:S(2)}) collective-permute-start(bf16[528,1024]{1,0:T(8,128)(2,1)S(1)} %get-tuple-element.27), channel_id=1, source_target_pairs={{0,4},{4,0},{8,12},{12,8},{16,20},{20,16},{24,28},{28,24},{1,5},{5... | collective-permute-start | bytes 3244040 | tf_op jit(solution)/shard_map/ppermute | solution.py:383

commit v5 on v4

--- a/solution.py
+++ b/solution.py
@@ -20,17 +20,31 @@
 VMEM_BYTES = 25 * 1024 * 1024
 
 
-def short_dft():
-    index = np.arange(WIDE)[:, None] * np.arange(HALF)[None, :] % WIDE
-    angle = index * (2.0 * np.pi / WIDE)
+def three_terms(tables):
     terms = []
-    for table in (np.cos(angle), -np.sin(angle)):
+    for table in tables:
         rest = table.astype(np.float32)
         for _ in range(3):
             part = rest.astype(jnp.bfloat16)
             terms.append(part)
             rest = rest - part.astype(np.float32)
     return np.concatenate(terms, axis=1)
+
+
+def turn_tables():
+    groups = RADIX // 2
+    first = np.arange(groups)
+    second = np.where(first == 0, RADIX // 2, first + RADIX * HALF)
+    starts = np.zeros(HALF, np.int64)
+    starts[: 2 * groups] = np.concatenate([first, second])
+    low, high = np.arange(WIDE)[:, None], np.arange(HALF)[:, None]
+    angles = [
+        low * np.arange(HALF)[None, :] % WIDE * (2.0 * np.pi / WIDE),
+        low * starts[None, :] % SK * (2.0 * np.pi / SK),
+        high * starts[None, :] % RADIX * (2.0 * np.pi / RADIX),
+    ]
+    pairs = [three_terms([np.cos(angle), -np.sin(angle)]) for angle in angles]
+    return np.concatenate(pairs[:2], axis=1), pairs[2]
 
 
 def inverse_tables():
@@ -62,74 +76,64 @@
     return ends.astype(jnp.bfloat16), np.stack(groups).astype(jnp.bfloat16)
 
 
-def table_kernel(bucket_ref, phase_ref, dft_ref, high_ref, low_ref, base_ref):
-    group = pl.program_id(0)
-    sketches, features_in = 3, bucket_ref.shape[0]
-
-    @pl.when(group == 0)
-    def _():
+def table_kernel(bucket_ref, sign_ref, low_turns_ref, high_turns_ref, high_ref, low_ref):
+    sketches, features_in = bucket_ref.shape
+    groups = RADIX // 2
+    blank = jnp.zeros((8 - 2 * sketches, features_in), jnp.float32)
+    columns = jnp.concatenate(
+        [bucket_ref[...].astype(jnp.float32), sign_ref[...].astype(jnp.float32), blank], axis=0
+    ).T
+
+    def three(full, at):
+        return full[:, at : at + HALF] + full[:, at + HALF : at + 2 * HALF] + full[:, at + 2 * HALF : at + 3 * HALF]
+
+    chunk = 64
+    for k in range(sketches):
+        bucket = columns[:, k : k + 1].astype(jnp.int32)
+        sign = 2.0 * columns[:, sketches + k : sketches + k + 1] - 1.0
         lane = lax.broadcasted_iota(jnp.int32, (features_in, WIDE), 1)
-        for k in range(sketches):
-            chosen = jnp.where(bucket_ref[:, k : k + 1] == lane, 1.0, 0.0).astype(jnp.bfloat16)
-            full = jnp.dot(chosen, dft_ref[...], preferred_element_type=jnp.float32)
-            for part in range(2):
-                at = 3 * part * HALF
-                base_ref[2 * k + part] = (
-                    full[:, at : at + HALF]
-                    + full[:, at + HALF : at + 2 * HALF]
-                    + full[:, at + 2 * HALF : at + 3 * HALF]
-                )
-
-    first_lane = (lax.broadcasted_iota(jnp.int32, (features_in, HALF), 1) == 0) & (group == 0)
-    for k in range(sketches):
-        base_re, base_im = base_ref[2 * k], base_ref[2 * k + 1]
-        for side in range(2):
-            at = 6 * side + 2 * k
-            turn_re, turn_im = phase_ref[0, :, at : at + 1], phase_ref[0, :, at + 1 : at + 2]
-            real = turn_re * base_re - turn_im * base_im
-            imag = turn_re * base_im + turn_im * base_re
-            if side == 0:
-                imag = jnp.where(first_lane, phase_ref[0, :, 12 + k : 13 + k], imag)
-            for part, values in enumerate((real, imag)):
-                start = (2 * k + part) * WIDE + side * HALF
-                high = values.astype(jnp.bfloat16)
-                high_ref[0, :, start : start + HALF] = high
-                low_ref[0, :, start : start + HALF] = (values - high.astype(jnp.float32)).astype(LOW)
+        chosen = jnp.where(bucket % WIDE == lane, 1.0, 0.0).astype(jnp.bfloat16)
+        full = jnp.dot(chosen, low_turns_ref[...], preferred_element_type=jnp.float32)
+        base_re, base_im, fine_re, fine_im = [three(full, 3 * i * HALF) for i in range(4)]
+        lane = lax.broadcasted_iota(jnp.int32, (features_in, HALF), 1)
+        chosen = jnp.where(bucket // WIDE == lane, 1.0, 0.0).astype(jnp.bfloat16)
+        full = jnp.dot(chosen, high_turns_ref[...], preferred_element_type=jnp.float32)
+        wide_re, wide_im = three(full, 0), three(full, 3 * HALF)
+        turns_re = (fine_re * wide_re - fine_im * wide_im) * sign
+        turns_im = (fine_re * wide_im + fine_im * wide_re) * sign
+        middle = sign * (1 - 2 * (bucket % 2)).astype(jnp.float32)
+        for r in range(0, features_in, chunk):
+            rows = slice(r, r + chunk)
+            first_lane = lax.broadcasted_iota(jnp.int32, (chunk, HALF), 1) == 0
+            for group in range(groups):
+                for side in range(2):
+                    at = side * groups + group
+                    turn_re, turn_im = turns_re[rows, at : at + 1], turns_im[rows, at : at + 1]
+                    real = turn_re * base_re[rows] - turn_im * base_im[rows]
+                    imag = turn_re * base_im[rows] + turn_im * base_re[rows]
+                    if group == 0 and side == 0:
+                        imag = jnp.where(first_lane, middle[rows], imag)
+                    for part, values in enumerate((real, imag)):
+                        start = (2 * k + part) * WIDE + side * HALF
+                        high = values.astype(jnp.bfloat16)
+                        high_ref[group, rows, start : start + HALF] = high
+                        low_ref[group, rows, start : start + HALF] = (
+                            values - high.astype(jnp.float32)
+                        ).astype(LOW)
 
 
 def forward_tables(bucket_ids, sign_bits):
-    groups = RADIX // 2
-    features_in = bucket_ids.shape[1]
-    first = np.arange(groups)
-    second = np.where(first == 0, RADIX // 2, first + RADIX * HALF)
-    offsets = jnp.asarray(np.stack([first, second], axis=1), jnp.int32)
-    buckets = bucket_ids.T
-    signs = (2 * sign_bits - 1).astype(jnp.float32).T
-    turns = buckets[None, :, None, :] * offsets[:, None, :, None] % SK
-    angles = turns.astype(jnp.float32) * (2.0 * math.pi / SK)
-    phases = jnp.stack([signs[None, :, None] * jnp.cos(angles), -signs[None, :, None] * jnp.sin(angles)], -1)
-    phases = phases.reshape(groups, features_in, 12)
-    middle = signs * (1 - 2 * (buckets % 2)).astype(jnp.float32)
-    phases = jnp.concatenate([phases, jnp.broadcast_to(middle[None], (groups, features_in, 3))], -1)
-    short = jnp.pad(buckets % WIDE, ((0, 0), (0, 5)))
-    dft = jnp.asarray(short_dft())
+    shape = (RADIX // 2, bucket_ids.shape[1], 6 * WIDE)
+    low_turns, high_turns = turn_tables()
+    vector = pl.BlockSpec(memory_space=pltpu.VMEM)
     return pl.pallas_call(
         table_kernel,
-        grid=(groups,),
-        out_shape=(
-            jax.ShapeDtypeStruct((groups, features_in, 6 * WIDE), jnp.bfloat16),
-            jax.ShapeDtypeStruct((groups, features_in, 6 * WIDE), LOW),
-        ),
-        in_specs=[
-            pl.BlockSpec(short.shape, lambda g: (0, 0)),
-            pl.BlockSpec((1, features_in, 15), lambda g: (g, 0, 0)),
-            pl.BlockSpec(dft.shape, lambda g: (0, 0)),
-        ],
-        out_specs=(pl.BlockSpec((1, features_in, 6 * WIDE), lambda g: (g, 0, 0)),) * 2,
-        scratch_shapes=[pltpu.VMEM((6, features_in, HALF), jnp.float32)],
+        out_shape=(jax.ShapeDtypeStruct(shape, jnp.bfloat16), jax.ShapeDtypeStruct(shape, LOW)),
+        in_specs=[vector] * 4,
+        out_specs=(vector, vector),
         compiler_params=pltpu.CompilerParams(vmem_limit_bytes=VMEM_BYTES // 2),
         cost_estimate=pl.CostEstimate(flops=2 * 10**9, bytes_accessed=14 * 10**6, transcendentals=0),
-    )(short, phases, dft)
+    )(bucket_ids, sign_bits, jnp.asarray(low_turns), jnp.asarray(high_turns))
 
 
 def combine(load):
@@ -387,7 +391,7 @@
     near = [0, 1]
     for i in range(1, (n_dp - 1).bit_length()):
         for core in range(2):
-            blocks[(1 << i) + core] = swap(blocks[core], 1 << i)
+            blocks[(1 << i) + core] = swap(other if core else own, (1 << i) + core)
             near.append((1 << i) + core)
     far = [delta for delta in range(n_dp) if delta not in blocks]
     sure = max(0, total - slots * len(far) - len(near)) // 2 if far else 0

time: 69.2 us -> 69.9 us (1.010)
  other arithmetic: 4.1 us -> 2.29 us
  local copies, waits for them, and re-layouts: 3.01 us -> 4.71 us
  Pallas kernels: 49.6 us -> 50.9 us
  waiting for transfers between devices: 3.69 us -> 2.74 us
    unnamed x11 -> x16, local copies, waits for them, and re-layouts: 0.86 us -> 3.45 us
    pallas_call x1, Pallas kernels: 5.82 us -> 6.88 us  [forward_tables(): pl.pallas_call(table_kernel, out_shape=(jax.ShapeDtypeStruct(shape, jnp.b...]
    mul x1 -> x0, other arithmetic: 0.97 us -> none  [forward_tables(): signs[None, :, None] * jnp.cos(angles)]
    ppermute x8, waiting for transfers between devices: 3.69 us -> 2.74 us  [swap(): return lax.ppermute(block, 'dp', [(i, i ^ bit) for i in range(n_dp)])]
  transfers between devices with their start and end apart: 8 -> 8, of which waited for: 3 -> 1; matrix products, arithmetic and copies ran while one was open for 5% -> 0% of each run, Pallas kernels for 28% -> 29%
where the time goes in v5:
time: 69.9 us; the launch traced here: 69.6 us
  Pallas kernels  50.9 us (73%)
  starting transfers between devices  8.3 us (12%)
  local copies, waits for them, and re-layouts  4.71 us (7%)
  waiting for transfers between devices  2.74 us (4%)
  other arithmetic  2.29 us (3%)
  between operations  0.72 us (1%)
    pallas_call x2, Pallas kernels, transform(): pl.pallas_call(functools.partial(main_kernel, deltas, begin, final), out_...  42.1 us
    ppermute x8, starting transfers between devices, swap(): return lax.ppermute(block, 'dp', [(i, i ^ bit) for i in range(n_dp)])  8.3 us
    pallas_call x1, Pallas kernels, forward_tables(): pl.pallas_call(table_kernel, out_shape=(jax.ShapeDtypeStruct(shape, jnp.b...  6.88 us
    unnamed x16, local copies, waits for them, and re-layouts  3.45 us
    ppermute x8, waiting for transfers between devices, swap(): return lax.ppermute(block, 'dp', [(i, i ^ bit) for i in range(n_dp)])  2.74 us
    pallas_call x1, Pallas kernels, body(): pl.pallas_call(prepare_kernel, out_shape=(message, message), in_specs=sca...  1.83 us
    mul x1, other arithmetic, body(): (mine[:own_columns] + theirs[:own_columns].astype(jnp.float32)) * (1.0 /...  1.69 us
  transfers between devices with their start and end apart: 8, of which 1 were waited for; matrix products, arithmetic and copies ran while one was open for 0% of the time, Pallas kernels for 29%

profile of v5, /device:TPU:0, one launch (start us, length us, event | category | flops | bytes accessed | tf_op | source)
XLA Modules:
  0.0 69.6 jit_solution(316765068485728052)
XLA Ops:
  0.6 1.3 %reshape.11.targets_ref = bf16[1,768]{1,0:T(2,128)(2,1)} reshape(bf16[768]{0:T(1024)(128)(2,1)} %param.10) | data formatting | bytes 3072 | tf_op jit(solution)/shard_map/reshape | solution.py:384
  1.9 1.8 %shard_map.105 = (bf16[416,256]{1,0:T(8,128)(2,1)}, bf16[416,256]{1,0:T(8,128)(2,1)}) custom-call(s32[8]{0:T(128)} %counts_ref.5, bf16[768,256]{1,0:T(8,128)(2,1)} %samples_ref.1, bf16[1,768]{1,0:T(2,128)(2,1)} %reshape.11.targets_ref), custom_call_target="tpu_custom_call" | custom-call | tf_op jit(solution)/shard_map/pallas_call | solution.py:379
  3.7 3.0 %collective-permute-start.3 = (bf16[416,256]{1,0:T(8,128)(2,1)}, bf16[416,256]{1,0:T(8,128)(2,1)S(1)}, u32[]{:S(2)}, u32[]{:S(2)}) collective-permute-start(bf16[416,256]{1,0:T(8,128)(2,1)} %get-tuple-element.18.refs_0_), channel_id=1, source_target_pairs={{0,16},{4,20},{8,24},{12,28},{16,0},{20,4},{24,8},{28,12},{1,17},{... | collective-permute-start | bytes 638984 | tf_op jit(solution)/shard_map/ppermute | solution.py:387
  6.7 1.5 %collective-permute-start.1 = (bf16[416,256]{1,0:T(8,128)(2,1)}, bf16[416,256]{1,0:T(8,128)(2,1)S(1)}, u32[]{:S(2)}, u32[]{:S(2)}) collective-permute-start(bf16[416,256]{1,0:T(8,128)(2,1)} %get-tuple-element.18.refs_0_), channel_id=1, source_target_pairs={{0,8},{4,12},{8,0},{12,4},{16,24},{20,28},{24,16},{28,20},{1,9},{5... | collective-permute-start | bytes 638984 | tf_op jit(solution)/shard_map/ppermute | solution.py:387
  8.2 0.0 copy-start
  8.2 0.0 copy-start.1
  8.2 0.0 collective-permute-start.4
  8.2 0.3 collective-permute-start.2
  8.4 0.4 collective-permute-start
  8.8 0.0 copy-start.2
  8.8 0.7 copy-done.2
  9.5 0.0 copy-start.3
  9.5 0.7 copy-done.3
  10.2 0.0 copy-start.5
  10.2 1.1 %copy-done.5 = bf16[256,1536]{1,0:T(8,128)(2,1)S(1)} copy-done((bf16[256,1536]{1,0:T(8,128)(2,1)S(1)}, bf16[256,1536]{1,0:T(8,128)(2,1)}, u32[]{:S(2)}) %copy-start.5) | copy-done | bytes 786456
  11.3 0.0 copy-start.7
  11.3 0.9 %copy-done.7 = bf16[128,768]{1,0:T(8,128)(2,1)S(1)} copy-done((bf16[128,768]{1,0:T(8,128)(2,1)S(1)}, bf16[128,768]{1,0:T(8,128)(2,1)}, u32[]{:S(2)}) %copy-start.7) | copy-done | bytes 196632
  12.3 0.0 copy-start.4
  12.3 0.0 copy-start.6
  12.3 6.9 %shard_map.104 = (bf16[8,256,1536]{2,1,0:T(8,128)(2,1)S(1)}, f8e5m2[8,256,1536]{2,1,0:T(32,128)(4,1)S(1)}) custom-call(s32[3,256]{1,0:T(4,128)S(1)} %copy-done.2, s32[3,256]{1,0:T(4,128)S(1)} %copy-done.3, bf16[256,1536]{1,0:T(8,128)(2,1)S(1)} %copy-done.5, bf16[128,768]{1,0:T(8,128)(2,1)S(1)} %copy-done.7), custom_call_target="tpu_custom_call" | custom-call | flops 2000000000 | bytes 14000000 | tf_op jit(solution)/shard_map/pallas_call | solution.py:129
  19.2 0.0 collective-permute-done.3.refs_4_
  19.2 0.0 collective-permute-done.1.refs_2_
  19.2 0.0 collective-permute-done.4.refs_5_
  19.2 0.0 collective-permute-done.2.refs_3_
  19.2 0.0 collective-permute-done.refs_1_
  19.2 1.7 %collective-permute-start.5 = (bf16[416,256]{1,0:T(8,128)(2,1)S(1)}, bf16[416,256]{1,0:T(8,128)(2,1)S(1)}, u32[]{:S(2)}, u32[]{:S(2)}) collective-permute-start(bf16[416,256]{1,0:T(8,128)(2,1)S(1)} %collective-permute-done.1.refs_2_), channel_id=1, source_target_pairs={{0,16},{4,20},{8,24},{12,28},{16,0},{20,4},{24,8},{28,12},{1,17},{... | collective-permute-start | bytes 638984 | tf_op jit(solution)/shard_map/ppermute | solution.py:387
  20.9 1.5 %collective-permute-start.6 = (bf16[416,256]{1,0:T(8,128)(2,1)S(1)}, bf16[416,256]{1,0:T(8,128)(2,1)S(1)}, u32[]{:S(2)}, u32[]{:S(2)}) collective-permute-start(bf16[416,256]{1,0:T(8,128)(2,1)S(1)} %collective-permute-done.4.refs_5_), channel_id=1, source_target_pairs={{0,8},{4,12},{8,0},{12,4},{16,24},{20,28},{24,16},{28,20},{1,9},{5... | collective-permute-start | bytes 638984 | tf_op jit(solution)/shard_map/ppermute | solution.py:387
  22.4 0.0 copy-done
  22.4 0.0 copy-done.1
  22.4 0.0 copy-done.4
  22.4 0.0 copy-done.6
  22.4 13.3 %shard_map.106.refs_12_ = bf16[9,512,256]{2,1,0:T(8,128)(2,1)S(1)} custom-call(s32[8]{0:T(128)S(1)} %copy-done, bf16[416,256]{1,0:T(8,128)(2,1)S(1)} %copy-done.1, bf16[416,256]{1,0:T(8,128)(2,1)S(1)} %collective-permute-done.refs_1_, bf16[416,256]{1,0:T(8,128)(2,1)S(1)} %collective-permute-done.1.refs_2_, ...), custom_call_target="tpu_custom_call" | custom-call | flops 10240000000 | bytes 24000000 | tf_op jit(solution)/shard_map/pallas_call | solution.py:433
  35.8 0.0 collective-permute-done.5.refs_6_
  35.8 0.0 collective-permute-done.6.refs_7_
  35.8 28.8 %shard_map.107 = (f32[520,1024]{1,0:T(8,128)S(1)}, bf16[528,1024]{1,0:T(8,128)(2,1)S(1)}) custom-call(s32[8]{0:T(128)S(1)} %copy-done, bf16[416,256]{1,0:T(8,128)(2,1)S(1)} %copy-done.1, bf16[416,256]{1,0:T(8,128)(2,1)S(1)} %collective-permute-done.refs_1_, bf16[416,256]{1,0:T(8,128)(2,1)S(1)} %collective-permute-done.1.refs_2_, ...), custom_call_target="tpu_custom_call" | custom-call | flops 20480000000 | bytes 24000000 | tf_op jit(solution)/shard_map/pallas_call | solution.py:433
  64.6 0.0 collective-permute-start.7
  64.6 2.7 %collective-permute-done.7 = bf16[528,1024]{1,0:T(8,128)(2,1)S(1)} collective-permute-done((bf16[528,1024]{1,0:T(8,128)(2,1)S(1)}, bf16[528,1024]{1,0:T(8,128)(2,1)S(1)}, u32[]{:S(2)}, u32[]{:S(2)}) %collective-permute-start.7) | collective-permute-done | bytes 1081376 | tf_op jit(solution)/shard_map/ppermute | solution.py:387
  67.3 0.6 fusion.1
  67.9 1.7 %add_multiply_fusion = f32[512,1024]{1,0:T(8,128)} fusion(f32[520,1024]{1,0:T(8,128)S(1)} %get-tuple-element.26, bf16[528,1024]{1,0:T(8,128)(2,1)S(1)} %collective-permute-done.7), kind=kLoop, calls=%fused_computation | loop fusion | flops 1572864 | bytes 5242880 | tf_op jit(solution)/shard_map/mul | solution.py:448
Async XLA Ops:
  3.7 15.5 %collective-permute-start.3 = (bf16[416,256]{1,0:T(8,128)(2,1)}, bf16[416,256]{1,0:T(8,128)(2,1)S(1)}, u32[]{:S(2)}, u32[]{:S(2)}) collective-permute-start(bf16[416,256]{1,0:T(8,128)(2,1)} %get-tuple-element.18.refs_0_), channel_id=1, source_target_pairs={{0,16},{4,20},{8,24},{12,28},{16,0},{20,4},{24,8},{28,12},{1,17},{... | collective-permute-start | bytes 638984 | tf_op jit(solution)/shard_map/ppermute | solution.py:387
  6.7 12.5 %collective-permute-start.1 = (bf16[416,256]{1,0:T(8,128)(2,1)}, bf16[416,256]{1,0:T(8,128)(2,1)S(1)}, u32[]{:S(2)}, u32[]{:S(2)}) collective-permute-start(bf16[416,256]{1,0:T(8,128)(2,1)} %get-tuple-element.18.refs_0_), channel_id=1, source_target_pairs={{0,8},{4,12},{8,0},{12,4},{16,24},{20,28},{24,16},{28,20},{1,9},{5... | collective-permute-start | bytes 638984 | tf_op jit(solution)/shard_map/ppermute | solution.py:387
  8.2 14.2 %copy-start = (s32[8]{0:T(128)S(1)}, s32[8]{0:T(128)}, u32[]{:S(2)}) copy-start(s32[8]{0:T(128)} %counts_ref.5) | copy-start | bytes 100
  8.2 14.2 %copy-start.1 = (bf16[416,256]{1,0:T(8,128)(2,1)S(1)}, bf16[416,256]{1,0:T(8,128)(2,1)}, u32[]{:S(2)}) copy-start(bf16[416,256]{1,0:T(8,128)(2,1)} %get-tuple-element.18.refs_0_) | copy-start | bytes 638980
  8.2 11.0 %collective-permute-start.4 = (bf16[416,256]{1,0:T(8,128)(2,1)}, bf16[416,256]{1,0:T(8,128)(2,1)S(1)}, u32[]{:S(2)}, u32[]{:S(2)}) collective-permute-start(bf16[416,256]{1,0:T(8,128)(2,1)} %get-tuple-element.17), channel_id=1, source_target_pairs={{0,20},{4,16},{8,28},{12,24},{16,4},{20,0},{24,12},{28,8},{1,21},{... | collective-permute-start | bytes 638984 | tf_op jit(solution)/shard_map/ppermute | solution.py:387
  8.2 11.0 %collective-permute-start.2 = (bf16[416,256]{1,0:T(8,128)(2,1)}, bf16[416,256]{1,0:T(8,128)(2,1)S(1)}, u32[]{:S(2)}, u32[]{:S(2)}) collective-permute-start(bf16[416,256]{1,0:T(8,128)(2,1)} %get-tuple-element.17), channel_id=1, source_target_pairs={{0,12},{4,8},{8,4},{12,0},{16,28},{20,24},{24,20},{28,16},{1,13},{... | collective-permute-start | bytes 638984 | tf_op jit(solution)/shard_map/ppermute | solution.py:387
  8.4 10.8 %collective-permute-start = (bf16[416,256]{1,0:T(8,128)(2,1)}, bf16[416,256]{1,0:T(8,128)(2,1)S(1)}, u32[]{:S(2)}, u32[]{:S(2)}) collective-permute-start(bf16[416,256]{1,0:T(8,128)(2,1)} %get-tuple-element.17), channel_id=1, source_target_pairs={{0,4},{4,0},{8,12},{12,8},{16,20},{20,16},{24,28},{28,24},{1,5},{5... | collective-permute-start | bytes 638984 | tf_op jit(solution)/shard_map/ppermute | solution.py:387
  8.8 0.7 copy-start.2
  9.5 0.7 copy-start.3
  10.2 1.1 %copy-start.5 = (bf16[256,1536]{1,0:T(8,128)(2,1)S(1)}, bf16[256,1536]{1,0:T(8,128)(2,1)}, u32[]{:S(2)}) copy-start(bf16[256,1536]{1,0:T(8,128)(2,1)} %constant.12.clone.low_turns_ref) | copy-start | bytes 2359300
  11.3 0.9 %copy-start.7 = (bf16[128,768]{1,0:T(8,128)(2,1)S(1)}, bf16[128,768]{1,0:T(8,128)(2,1)}, u32[]{:S(2)}) copy-start(bf16[128,768]{1,0:T(8,128)(2,1)} %constant.13.clone.high_turns_ref) | copy-start | bytes 589828
  12.3 10.1 %copy-start.4 = (bf16[7,512,512]{2,1,0:T(8,128)(2,1)S(1)}, bf16[7,512,512]{2,1,0:T(8,128)(2,1)}, u32[]{:S(2)}) copy-start(bf16[7,512,512]{2,1,0:T(8,128)(2,1)} %constant.15.clone.refs_9_.refs_11_) | copy-start | bytes 11010052
  12.3 10.1 %copy-start.6 = (bf16[256,512]{1,0:T(8,128)(2,1)S(1)}, bf16[256,512]{1,0:T(8,128)(2,1)}, u32[]{:S(2)}) copy-start(bf16[256,512]{1,0:T(8,128)(2,1)} %constant.14.clone.refs_8_.refs_10_) | copy-start | bytes 786436
  19.2 16.5 %collective-permute-start.5 = (bf16[416,256]{1,0:T(8,128)(2,1)S(1)}, bf16[416,256]{1,0:T(8,128)(2,1)S(1)}, u32[]{:S(2)}, u32[]{:S(2)}) collective-permute-start(bf16[416,256]{1,0:T(8,128)(2,1)S(1)} %collective-permute-done.1.refs_2_), channel_id=1, source_target_pairs={{0,16},{4,20},{8,24},{12,28},{16,0},{20,4},{24,8},{28,12},{1,17},{... | collective-permute-start | bytes 638984 | tf_op jit(solution)/shard_map/ppermute | solution.py:387
  20.9 14.9 %collective-permute-start.6 = (bf16[416,256]{1,0:T(8,128)(2,1)S(1)}, bf16[416,256]{1,0:T(8,128)(2,1)S(1)}, u32[]{:S(2)}, u32[]{:S(2)}) collective-permute-start(bf16[416,256]{1,0:T(8,128)(2,1)S(1)} %collective-permute-done.4.refs_5_), channel_id=1, source_target_pairs={{0,8},{4,12},{8,0},{12,4},{16,24},{20,28},{24,16},{28,20},{1,9},{5... | collective-permute-start | bytes 638984 | tf_op jit(solution)/shard_map/ppermute | solution.py:387
  64.6 2.7 %collective-permute-start.7 = (bf16[528,1024]{1,0:T(8,128)(2,1)S(1)}, bf16[528,1024]{1,0:T(8,128)(2,1)S(1)}, u32[]{:S(2)}, u32[]{:S(2)}) collective-permute-start(bf16[528,1024]{1,0:T(8,128)(2,1)S(1)} %get-tuple-element.27), channel_id=1, source_target_pairs={{0,4},{4,0},{8,12},{12,8},{16,20},{20,16},{24,28},{28,24},{1,5},{5... | collective-permute-start | bytes 3244040 | tf_op jit(solution)/shard_map/ppermute | solution.py:387

commit v6 on v5

--- a/solution.py
+++ b/solution.py
@@ -173,7 +173,7 @@
         start = start + jnp.where(j < device, counts_ref[j], 0)
     cut = (start + counts_ref[device] + 1) // 2 - (start + 1) // 2
     late = window_start(cut, slots)
-    lines = [targets_ref[:, i * width : (i + 1) * width] for i in range(slots // width)]
+    lines = [targets_ref[i * width : (i + 1) * width].reshape(1, width) for i in range(slots // width)]
     lines.append(jnp.zeros((TAIL - len(lines), width), jnp.bfloat16))
     tail = jnp.concatenate(lines, axis=0)
     for target, is_late in ((own_ref, core), (other_ref, 1 - core)):
@@ -366,6 +366,12 @@
         send_ref[each * WIDE :, at] = jnp.concatenate([line, line], axis=0).astype(send_ref.dtype)
 
 
+def merge_kernel(total, mine_ref, theirs_ref, mine_line_ref, theirs_line_ref, gram_ref, zty_ref):
+    gram_ref[...] = (mine_ref[...] + theirs_ref[...].astype(jnp.float32)) * (1.0 / total)
+    line = mine_line_ref[...] + theirs_line_ref[...].astype(jnp.float32)[:8]
+    zty_ref[...] = line[:1] * total ** (-0.5)
+
+
 def body(samples, targets, counts, bucket_ids, sign_bits):
     n_dp, n_feat = lax.axis_size("dp"), lax.axis_size("feat")
     slots, width = samples.shape
@@ -381,7 +387,8 @@
         out_shape=(message, message),
         in_specs=scalars + [vector] * 2,
         out_specs=(vector, vector),
-    )(counts, samples, targets.reshape(1, slots))
+        compiler_params=pltpu.CompilerParams(vmem_limit_bytes=VMEM_BYTES // 6),
+    )(counts, samples, targets)
 
     def swap(block, bit):
         return lax.ppermute(block, "dp", [(i, i ^ bit) for i in range(n_dp)])
@@ -445,9 +452,29 @@
     early = (transform(near, 0, first, False, ()),) if first else ()
     mine, send = transform(near + far, first, rows, True, early)
     theirs = swap(send, 1)
-    gram = (mine[:own_columns] + theirs[:own_columns].astype(jnp.float32)) * (1.0 / total)
-    zty = (mine[own_columns] + theirs[own_columns].astype(jnp.float32)) * total ** (-0.5)
-    return gram, zty
+    blocks_in = min(own_columns, 2 * HALF)
+    parts = own_columns // blocks_in
+    rest = own_columns // 16
+    gram, zty = pl.pallas_call(
+        functools.partial(merge_kernel, total),
+        grid=(parts,),
+        out_shape=(
+            jax.ShapeDtypeStruct((own_columns, panel_columns), jnp.float32),
+            jax.ShapeDtypeStruct((1, panel_columns), jnp.float32),
+        ),
+        in_specs=[
+            pl.BlockSpec((blocks_in, panel_columns), lambda i: (i, 0)),
+            pl.BlockSpec((blocks_in, panel_columns), lambda i: (i, 0)),
+            pl.BlockSpec((8, panel_columns), lambda i: (2 * rest, 0)),
+            pl.BlockSpec((16, panel_columns), lambda i: (rest, 0)),
+        ],
+        out_specs=(
+            pl.BlockSpec((blocks_in, panel_columns), lambda i: (i, 0)),
+            pl.BlockSpec((1, panel_columns), lambda i: (0, 0)),
+        ),
+        compiler_params=pltpu.CompilerParams(vmem_limit_bytes=VMEM_BYTES // 2),
+    )(mine, theirs, mine, theirs)
+    return gram, zty.reshape(panel_columns)
 
 
 def solution(mesh):

time: 69.9 us -> 69 us (0.987)
  other arithmetic: 2.29 us -> 0 us
  local copies, waits for them, and re-layouts: 4.71 us -> 5.77 us
    unnamed x16 -> x20, local copies, waits for them, and re-layouts: 3.45 us -> 5.77 us
    mul x2 -> x0, other arithmetic: 2.29 us -> none  [the longest x1 1.69 us: body(): (mine[:own_columns] + theirs[:own_columns].astype(jnp.float32)) * (1.0 /...]
    pallas_call x0 -> x1, Pallas kernels: none -> 1.45 us  [body(): pl.pallas_call(functools.partial(merge_kernel, total), grid=(parts,), out...]
    reshape x1 -> x0, local copies, waits for them, and re-layouts: 1.26 us -> none  [body(): targets.reshape(1, slots)]
    pallas_call x1, Pallas kernels: 1.83 us -> 0.6 us  [body(): pl.pallas_call(prepare_kernel, out_shape=(message, message), in_specs=sca...]
where the time goes in v6:
time: 69 us; the launch traced here: 68.7 us
  Pallas kernels  51.1 us (74%)
  starting transfers between devices  8.37 us (12%)
  local copies, waits for them, and re-layouts  5.77 us (8%)
  waiting for transfers between devices  2.74 us (4%)
  between operations  0.73 us (1%)
    pallas_call x2, Pallas kernels, transform(): pl.pallas_call(functools.partial(main_kernel, deltas, begin, final), out_...  42.1 us
    ppermute x8, starting transfers between devices, swap(): return lax.ppermute(block, 'dp', [(i, i ^ bit) for i in range(n_dp)])  8.37 us
    pallas_call x1, Pallas kernels, forward_tables(): pl.pallas_call(table_kernel, out_shape=(jax.ShapeDtypeStruct(shape, jnp.b...  6.88 us
    unnamed x20, local copies, waits for them, and re-layouts  5.77 us
    ppermute x8, waiting for transfers between devices, swap(): return lax.ppermute(block, 'dp', [(i, i ^ bit) for i in range(n_dp)])  2.74 us
    pallas_call x1, Pallas kernels, body(): pl.pallas_call(functools.partial(merge_kernel, total), grid=(parts,), out...  1.45 us
  transfers between devices with their start and end apart: 8, of which 1 were waited for; matrix products, arithmetic and copies ran while one was open for 0% of the time, Pallas kernels for 29%

profile of v6, /device:TPU:0, one launch (start us, length us, event | category | flops | bytes accessed | tf_op | source)
XLA Modules:
  0.0 68.7 jit_solution(14313132932044343647)
XLA Ops:
  0.6 0.0 copy-start
  0.6 1.0 %copy-done = bf16[768,256]{1,0:T(8,128)(2,1)S(1)} copy-done((bf16[768,256]{1,0:T(8,128)(2,1)S(1)}, bf16[768,256]{1,0:T(8,128)(2,1)}, u32[]{:S(2)}) %copy-start) | copy-done | bytes 393240
  1.6 0.0 copy-start.1
  1.6 0.7 copy-done.1
  2.3 0.0 copy-start.2
  2.3 0.7 copy-done.2
  3.0 0.6 shard_map.105
  3.6 3.0 %collective-permute-start.3 = (bf16[416,256]{1,0:T(8,128)(2,1)S(1)}, bf16[416,256]{1,0:T(8,128)(2,1)S(1)}, u32[]{:S(2)}, u32[]{:S(2)}) collective-permute-start(bf16[416,256]{1,0:T(8,128)(2,1)S(1)} %get-tuple-element.20.refs_0_), channel_id=1, source_target_pairs={{0,16},{4,20},{8,24},{12,28},{16,0},{20,4},{24,8},{28,12},{1,17},{... | collective-permute-start | bytes 638984 | tf_op jit(solution)/shard_map/ppermute | solution.py:394
  6.6 1.5 %collective-permute-start.1 = (bf16[416,256]{1,0:T(8,128)(2,1)S(1)}, bf16[416,256]{1,0:T(8,128)(2,1)S(1)}, u32[]{:S(2)}, u32[]{:S(2)}) collective-permute-start(bf16[416,256]{1,0:T(8,128)(2,1)S(1)} %get-tuple-element.20.refs_0_), channel_id=1, source_target_pairs={{0,8},{4,12},{8,0},{12,4},{16,24},{20,28},{24,16},{28,20},{1,9},{5... | collective-permute-start | bytes 638984 | tf_op jit(solution)/shard_map/ppermute | solution.py:394
  8.1 0.0 copy-start.3
  8.1 0.0 collective-permute-start.4
  8.1 0.3 collective-permute-start.2
  8.4 0.3 collective-permute-start
  8.8 0.0 copy-start.4
  8.8 0.7 copy-done.4
  9.4 0.0 copy-start.5
  9.4 0.7 copy-done.5
  10.1 0.0 copy-start.7
  10.1 1.1 %copy-done.7 = bf16[256,1536]{1,0:T(8,128)(2,1)S(1)} copy-done((bf16[256,1536]{1,0:T(8,128)(2,1)S(1)}, bf16[256,1536]{1,0:T(8,128)(2,1)}, u32[]{:S(2)}) %copy-start.7) | copy-done | bytes 786456
  11.3 0.0 copy-start.9
  11.3 0.9 %copy-done.9 = bf16[128,768]{1,0:T(8,128)(2,1)S(1)} copy-done((bf16[128,768]{1,0:T(8,128)(2,1)S(1)}, bf16[128,768]{1,0:T(8,128)(2,1)}, u32[]{:S(2)}) %copy-start.9) | copy-done | bytes 196632
  12.2 0.0 copy-start.6
  12.2 0.0 copy-start.8
  12.2 6.9 %shard_map.104 = (bf16[8,256,1536]{2,1,0:T(8,128)(2,1)S(1)}, f8e5m2[8,256,1536]{2,1,0:T(32,128)(4,1)S(1)}) custom-call(s32[3,256]{1,0:T(4,128)S(1)} %copy-done.4, s32[3,256]{1,0:T(4,128)S(1)} %copy-done.5, bf16[256,1536]{1,0:T(8,128)(2,1)S(1)} %copy-done.7, bf16[128,768]{1,0:T(8,128)(2,1)S(1)} %copy-done.9), custom_call_target="tpu_custom_call" | custom-call | flops 2000000000 | bytes 14000000 | tf_op jit(solution)/shard_map/pallas_call | solution.py:129
  19.1 0.0 collective-permute-done.3.refs_4_
  19.1 0.0 collective-permute-done.1.refs_2_
  19.1 0.0 collective-permute-done.4.refs_5_
  19.1 0.0 collective-permute-done.2.refs_3_
  19.1 0.0 collective-permute-done.refs_1_
  19.1 1.7 %collective-permute-start.5 = (bf16[416,256]{1,0:T(8,128)(2,1)S(1)}, bf16[416,256]{1,0:T(8,128)(2,1)S(1)}, u32[]{:S(2)}, u32[]{:S(2)}) collective-permute-start(bf16[416,256]{1,0:T(8,128)(2,1)S(1)} %collective-permute-done.1.refs_2_), channel_id=1, source_target_pairs={{0,16},{4,20},{8,24},{12,28},{16,0},{20,4},{24,8},{28,12},{1,17},{... | collective-permute-start | bytes 638984 | tf_op jit(solution)/shard_map/ppermute | solution.py:394
  20.8 1.5 %collective-permute-start.6 = (bf16[416,256]{1,0:T(8,128)(2,1)S(1)}, bf16[416,256]{1,0:T(8,128)(2,1)S(1)}, u32[]{:S(2)}, u32[]{:S(2)}) collective-permute-start(bf16[416,256]{1,0:T(8,128)(2,1)S(1)} %collective-permute-done.4.refs_5_), channel_id=1, source_target_pairs={{0,8},{4,12},{8,0},{12,4},{16,24},{20,28},{24,16},{28,20},{1,9},{5... | collective-permute-start | bytes 638984 | tf_op jit(solution)/shard_map/ppermute | solution.py:394
  22.3 0.0 copy-done.3
  22.3 0.0 copy-done.6
  22.3 0.0 copy-done.8
  22.3 13.3 %shard_map.106.refs_12_ = bf16[9,512,256]{2,1,0:T(8,128)(2,1)S(1)} custom-call(s32[8]{0:T(128)S(1)} %copy-done.3, bf16[416,256]{1,0:T(8,128)(2,1)S(1)} %get-tuple-element.20.refs_0_, bf16[416,256]{1,0:T(8,128)(2,1)S(1)} %collective-permute-done.refs_1_, bf16[416,256]{1,0:T(8,128)(2,1)S(1)} %collective-permute-done.1.refs_2_, ...), custom_call_target="tpu_custom_call" | custom-call | flops 10240000000 | bytes 24000000 | tf_op jit(solution)/shard_map/pallas_call | solution.py:440
  35.7 0.0 collective-permute-done.5.refs_6_
  35.7 0.0 collective-permute-done.6.refs_7_
  35.7 28.8 %shard_map.107 = (f32[520,1024]{1,0:T(8,128)S(1)}, bf16[528,1024]{1,0:T(8,128)(2,1)S(1)}) custom-call(s32[8]{0:T(128)S(1)} %copy-done.3, bf16[416,256]{1,0:T(8,128)(2,1)S(1)} %get-tuple-element.20.refs_0_, bf16[416,256]{1,0:T(8,128)(2,1)S(1)} %collective-permute-done.refs_1_, bf16[416,256]{1,0:T(8,128)(2,1)S(1)} %collective-permute-done.1.refs_2_, ...), custom_call_target="tpu_custom_call" | custom-call | flops 20480000000 | bytes 24000000 | tf_op jit(solution)/shard_map/pallas_call | solution.py:440
  64.5 0.0 collective-permute-start.7
  64.5 2.7 %collective-permute-done.7.theirs_ref.theirs_line_ref = bf16[528,1024]{1,0:T(8,128)(2,1)S(1)} collective-permute-done((bf16[528,1024]{1,0:T(8,128)(2,1)S(1)}, bf16[528,1024]{1,0:T(8,128)(2,1)S(1)}, u32[]{:S(2)}, u32[]{:S(2)}) %collective-permute-start.7) | collective-permute-done | bytes 1081376 | tf_op jit(solution)/shard_map/ppermute | solution.py:394
  67.2 1.5 %shard_map.108 = (f32[512,1024]{1,0:T(8,128)}, f32[1,1024]{1,0:T(1,128)}) custom-call(f32[520,1024]{1,0:T(8,128)S(1)} %get-tuple-element.28.mine_ref.mine_line_ref, bf16[528,1024]{1,0:T(8,128)(2,1)S(1)} %collective-permute-done.7.theirs_ref.theirs_line_ref, f32[520,1024]{1,0:T(8,128)S(1)} %get-tuple-element.28.mine_ref.mine_line_ref, ...), custom_call_target="tpu_custom_call" | custom-call | tf_op jit(solution)/shard_map/pallas_call | solution.py:458
Async XLA Ops:
  0.6 1.0 %copy-start = (bf16[768,256]{1,0:T(8,128)(2,1)S(1)}, bf16[768,256]{1,0:T(8,128)(2,1)}, u32[]{:S(2)}) copy-start(bf16[768,256]{1,0:T(8,128)(2,1)} %samples_ref.1) | copy-start | bytes 1179652
  1.6 0.7 copy-start.1
  2.3 0.7 copy-start.2
  3.6 15.5 %collective-permute-start.3 = (bf16[416,256]{1,0:T(8,128)(2,1)S(1)}, bf16[416,256]{1,0:T(8,128)(2,1)S(1)}, u32[]{:S(2)}, u32[]{:S(2)}) collective-permute-start(bf16[416,256]{1,0:T(8,128)(2,1)S(1)} %get-tuple-element.20.refs_0_), channel_id=1, source_target_pairs={{0,16},{4,20},{8,24},{12,28},{16,0},{20,4},{24,8},{28,12},{1,17},{... | collective-permute-start | bytes 638984 | tf_op jit(solution)/shard_map/ppermute | solution.py:394
  6.6 12.5 %collective-permute-start.1 = (bf16[416,256]{1,0:T(8,128)(2,1)S(1)}, bf16[416,256]{1,0:T(8,128)(2,1)S(1)}, u32[]{:S(2)}, u32[]{:S(2)}) collective-permute-start(bf16[416,256]{1,0:T(8,128)(2,1)S(1)} %get-tuple-element.20.refs_0_), channel_id=1, source_target_pairs={{0,8},{4,12},{8,0},{12,4},{16,24},{20,28},{24,16},{28,20},{1,9},{5... | collective-permute-start | bytes 638984 | tf_op jit(solution)/shard_map/ppermute | solution.py:394
  8.1 14.2 %copy-start.3 = (s32[8]{0:T(128)S(1)}, s32[8]{0:T(128)}, u32[]{:S(2)}) copy-start(s32[8]{0:T(128)} %counts_ref.5) | copy-start | bytes 100
  8.1 11.0 %collective-permute-start.4 = (bf16[416,256]{1,0:T(8,128)(2,1)S(1)}, bf16[416,256]{1,0:T(8,128)(2,1)S(1)}, u32[]{:S(2)}, u32[]{:S(2)}) collective-permute-start(bf16[416,256]{1,0:T(8,128)(2,1)S(1)} %get-tuple-element.19), channel_id=1, source_target_pairs={{0,20},{4,16},{8,28},{12,24},{16,4},{20,0},{24,12},{28,8},{1,21},{... | collective-permute-start | bytes 638984 | tf_op jit(solution)/shard_map/ppermute | solution.py:394
  8.1 11.0 %collective-permute-start.2 = (bf16[416,256]{1,0:T(8,128)(2,1)S(1)}, bf16[416,256]{1,0:T(8,128)(2,1)S(1)}, u32[]{:S(2)}, u32[]{:S(2)}) collective-permute-start(bf16[416,256]{1,0:T(8,128)(2,1)S(1)} %get-tuple-element.19), channel_id=1, source_target_pairs={{0,12},{4,8},{8,4},{12,0},{16,28},{20,24},{24,20},{28,16},{1,13},{... | collective-permute-start | bytes 638984 | tf_op jit(solution)/shard_map/ppermute | solution.py:394
  8.4 10.7 %collective-permute-start = (bf16[416,256]{1,0:T(8,128)(2,1)S(1)}, bf16[416,256]{1,0:T(8,128)(2,1)S(1)}, u32[]{:S(2)}, u32[]{:S(2)}) collective-permute-start(bf16[416,256]{1,0:T(8,128)(2,1)S(1)} %get-tuple-element.19), channel_id=1, source_target_pairs={{0,4},{4,0},{8,12},{12,8},{16,20},{20,16},{24,28},{28,24},{1,5},{5... | collective-permute-start | bytes 638984 | tf_op jit(solution)/shard_map/ppermute | solution.py:394
  8.8 0.7 %copy-start.4 = (s32[3,256]{1,0:T(4,128)S(1)}, s32[3,256]{1,0:T(4,128)}, u32[]{:S(2)}) copy-start(s32[3,256]{1,0:T(4,128)} %bucket_ref.1) | copy-start | bytes 9220
  9.4 0.7 %copy-start.5 = (s32[3,256]{1,0:T(4,128)S(1)}, s32[3,256]{1,0:T(4,128)}, u32[]{:S(2)}) copy-start(s32[3,256]{1,0:T(4,128)} %sign_ref.1) | copy-start | bytes 9220
  10.1 1.1 %copy-start.7 = (bf16[256,1536]{1,0:T(8,128)(2,1)S(1)}, bf16[256,1536]{1,0:T(8,128)(2,1)}, u32[]{:S(2)}) copy-start(bf16[256,1536]{1,0:T(8,128)(2,1)} %constant.8.clone.low_turns_ref) | copy-start | bytes 2359300
  11.3 0.9 %copy-start.9 = (bf16[128,768]{1,0:T(8,128)(2,1)S(1)}, bf16[128,768]{1,0:T(8,128)(2,1)}, u32[]{:S(2)}) copy-start(bf16[128,768]{1,0:T(8,128)(2,1)} %constant.9.clone.high_turns_ref) | copy-start | bytes 589828
  12.2 10.1 %copy-start.6 = (bf16[7,512,512]{2,1,0:T(8,128)(2,1)S(1)}, bf16[7,512,512]{2,1,0:T(8,128)(2,1)}, u32[]{:S(2)}) copy-start(bf16[7,512,512]{2,1,0:T(8,128)(2,1)} %constant.11.clone.refs_9_.refs_11_) | copy-start | bytes 11010052
  12.2 10.1 %copy-start.8 = (bf16[256,512]{1,0:T(8,128)(2,1)S(1)}, bf16[256,512]{1,0:T(8,128)(2,1)}, u32[]{:S(2)}) copy-start(bf16[256,512]{1,0:T(8,128)(2,1)} %constant.10.clone.refs_8_.refs_10_) | copy-start | bytes 786436
  19.1 16.5 %collective-permute-start.5 = (bf16[416,256]{1,0:T(8,128)(2,1)S(1)}, bf16[416,256]{1,0:T(8,128)(2,1)S(1)}, u32[]{:S(2)}, u32[]{:S(2)}) collective-permute-start(bf16[416,256]{1,0:T(8,128)(2,1)S(1)} %collective-permute-done.1.refs_2_), channel_id=1, source_target_pairs={{0,16},{4,20},{8,24},{12,28},{16,0},{20,4},{24,8},{28,12},{1,17},{... | collective-permute-start | bytes 638984 | tf_op jit(solution)/shard_map/ppermute | solution.py:394
  20.8 14.8 %collective-permute-start.6 = (bf16[416,256]{1,0:T(8,128)(2,1)S(1)}, bf16[416,256]{1,0:T(8,128)(2,1)S(1)}, u32[]{:S(2)}, u32[]{:S(2)}) collective-permute-start(bf16[416,256]{1,0:T(8,128)(2,1)S(1)} %collective-permute-done.4.refs_5_), channel_id=1, source_target_pairs={{0,8},{4,12},{8,0},{12,4},{16,24},{20,28},{24,16},{28,20},{1,9},{5... | collective-permute-start | bytes 638984 | tf_op jit(solution)/shard_map/ppermute | solution.py:394
  64.5 2.7 %collective-permute-start.7 = (bf16[528,1024]{1,0:T(8,128)(2,1)S(1)}, bf16[528,1024]{1,0:T(8,128)(2,1)S(1)}, u32[]{:S(2)}, u32[]{:S(2)}) collective-permute-start(bf16[528,1024]{1,0:T(8,128)(2,1)S(1)} %get-tuple-element.29), channel_id=1, source_target_pairs={{0,4},{4,0},{8,12},{12,8},{16,20},{20,16},{24,28},{28,24},{1,5},{5... | collective-permute-start | bytes 3244040 | tf_op jit(solution)/shard_map/ppermute | solution.py:394

commit v7 on v6

--- a/solution.py
+++ b/solution.py
@@ -44,7 +44,8 @@
         high * starts[None, :] % RADIX * (2.0 * np.pi / RADIX),
     ]
     pairs = [three_terms([np.cos(angle), -np.sin(angle)]) for angle in angles]
-    return np.concatenate(pairs[:2], axis=1), pairs[2]
+    high_part = np.pad(pairs[2], ((0, 0), (0, 6 * HALF)))
+    return np.concatenate([np.concatenate(pairs[:2], axis=1), high_part], axis=0)
 
 
 def inverse_tables():
@@ -76,28 +77,27 @@
     return ends.astype(jnp.bfloat16), np.stack(groups).astype(jnp.bfloat16)
 
 
-def table_kernel(bucket_ref, sign_ref, low_turns_ref, high_turns_ref, high_ref, low_ref):
-    sketches, features_in = bucket_ref.shape
+def table_kernel(packed_ref, turns_ref, high_ref, low_ref):
+    sketches, features_in = packed_ref.shape
     groups = RADIX // 2
-    blank = jnp.zeros((8 - 2 * sketches, features_in), jnp.float32)
-    columns = jnp.concatenate(
-        [bucket_ref[...].astype(jnp.float32), sign_ref[...].astype(jnp.float32), blank], axis=0
-    ).T
+    blank = jnp.zeros((8 - sketches, features_in), jnp.float32)
+    columns = jnp.concatenate([packed_ref[...].astype(jnp.float32), blank], axis=0).T
 
     def three(full, at):
         return full[:, at : at + HALF] + full[:, at + HALF : at + 2 * HALF] + full[:, at + 2 * HALF : at + 3 * HALF]
 
     chunk = 64
     for k in range(sketches):
-        bucket = columns[:, k : k + 1].astype(jnp.int32)
-        sign = 2.0 * columns[:, sketches + k : sketches + k + 1] - 1.0
+        packed = columns[:, k : k + 1].astype(jnp.int32)
+        bucket = packed // 2
+        sign = (2 * (packed % 2) - 1).astype(jnp.float32)
         lane = lax.broadcasted_iota(jnp.int32, (features_in, WIDE), 1)
         chosen = jnp.where(bucket % WIDE == lane, 1.0, 0.0).astype(jnp.bfloat16)
-        full = jnp.dot(chosen, low_turns_ref[...], preferred_element_type=jnp.float32)
+        full = jnp.dot(chosen, turns_ref[:WIDE, :], preferred_element_type=jnp.float32)
         base_re, base_im, fine_re, fine_im = [three(full, 3 * i * HALF) for i in range(4)]
         lane = lax.broadcasted_iota(jnp.int32, (features_in, HALF), 1)
         chosen = jnp.where(bucket // WIDE == lane, 1.0, 0.0).astype(jnp.bfloat16)
-        full = jnp.dot(chosen, high_turns_ref[...], preferred_element_type=jnp.float32)
+        full = jnp.dot(chosen, turns_ref[WIDE:, : 6 * HALF], preferred_element_type=jnp.float32)
         wide_re, wide_im = three(full, 0), three(full, 3 * HALF)
         turns_re = (fine_re * wide_re - fine_im * wide_im) * sign
         turns_im = (fine_re * wide_im + fine_im * wide_re) * sign
@@ -124,16 +124,16 @@
 
 def forward_tables(bucket_ids, sign_bits):
     shape = (RADIX // 2, bucket_ids.shape[1], 6 * WIDE)
-    low_turns, high_turns = turn_tables()
+    packed = 2 * bucket_ids + sign_bits
     vector = pl.BlockSpec(memory_space=pltpu.VMEM)
     return pl.pallas_call(
         table_kernel,
         out_shape=(jax.ShapeDtypeStruct(shape, jnp.bfloat16), jax.ShapeDtypeStruct(shape, LOW)),
-        in_specs=[vector] * 4,
+        in_specs=[vector] * 2,
         out_specs=(vector, vector),
         compiler_params=pltpu.CompilerParams(vmem_limit_bytes=VMEM_BYTES // 2),
         cost_estimate=pl.CostEstimate(flops=2 * 10**9, bytes_accessed=14 * 10**6, transcendentals=0),
-    )(bucket_ids, sign_bits, jnp.asarray(low_turns), jnp.asarray(high_turns))
+    )(packed, jnp.asarray(turn_tables()))
 
 
 def combine(load):
@@ -387,7 +387,6 @@
         out_shape=(message, message),
         in_specs=scalars + [vector] * 2,
         out_specs=(vector, vector),
-        compiler_params=pltpu.CompilerParams(vmem_limit_bytes=VMEM_BYTES // 6),
     )(counts, samples, targets)
 
     def swap(block, bit):

time: 69 us -> 66.5 us (0.964)
  local copies, waits for them, and re-layouts: 5.77 us -> 1.28 us
  Pallas kernels: 51.1 us -> 52.5 us
  other arithmetic: 0 us -> 0.71 us
    unnamed x20 -> x10, local copies, waits for them, and re-layouts: 5.77 us -> 1.28 us
    pallas_call x1, Pallas kernels: 0.6 us -> 1.82 us  [body(): pl.pallas_call(prepare_kernel, out_shape=(message, message), in_specs=sca...]
    add x0 -> x1, other arithmetic: none -> 0.71 us  [forward_tables(): packed = 2 * bucket_ids + sign_bits]
  transfers between devices with their start and end apart: 8 -> 8, of which waited for: 1 -> 1; matrix products, arithmetic and copies ran while one was open for 0% -> 1% of each run, Pallas kernels for 29% -> 31%
where the time goes in v7:
time: 66.5 us; the launch traced here: 66.2 us
  Pallas kernels  52.5 us (79%)
  starting transfers between devices  8.3 us (12%)
  waiting for transfers between devices  2.74 us (4%)
  local copies, waits for them, and re-layouts  1.28 us (2%)
  between operations  0.72 us (1%)
  other arithmetic  0.71 us (1%)
    pallas_call x2, Pallas kernels, transform(): pl.pallas_call(functools.partial(main_kernel, deltas, begin, final), out_...  42.1 us
    ppermute x8, starting transfers between devices, swap(): return lax.ppermute(block, 'dp', [(i, i ^ bit) for i in range(n_dp)])  8.3 us
    pallas_call x1, Pallas kernels, forward_tables(): pl.pallas_call(table_kernel, out_shape=(jax.ShapeDtypeStruct(shape, jnp.b...  7.1 us
    ppermute x8, waiting for transfers between devices, swap(): return lax.ppermute(block, 'dp', [(i, i ^ bit) for i in range(n_dp)])  2.74 us
    pallas_call x1, Pallas kernels, body(): pl.pallas_call(prepare_kernel, out_shape=(message, message), in_specs=sca...  1.82 us
    pallas_call x1, Pallas kernels, body(): pl.pallas_call(functools.partial(merge_kernel, total), grid=(parts,), out...  1.45 us
  transfers between devices with their start and end apart: 8, of which 1 were waited for; matrix products, arithmetic and copies ran while one was open for 1% of the time, Pallas kernels for 31%

profile of v7, /device:TPU:0, one launch (start us, length us, event | category | flops | bytes accessed | tf_op | source)
XLA Modules:
  0.0 66.2 jit_solution(831225248343518914)
XLA Ops:
  0.6 1.8 %shard_map.96 = (bf16[416,256]{1,0:T(8,128)(2,1)}, bf16[416,256]{1,0:T(8,128)(2,1)}) custom-call(s32[8]{0:T(128)} %counts_ref.5, bf16[768,256]{1,0:T(8,128)(2,1)} %samples_ref.1, bf16[768]{0:T(1024)(128)(2,1)} %targets_ref.1), custom_call_target="tpu_custom_call" | custom-call | tf_op jit(solution)/shard_map/pallas_call | solution.py:385
  2.4 3.0 %collective-permute-start.3 = (bf16[416,256]{1,0:T(8,128)(2,1)}, bf16[416,256]{1,0:T(8,128)(2,1)S(1)}, u32[]{:S(2)}, u32[]{:S(2)}) collective-permute-start(bf16[416,256]{1,0:T(8,128)(2,1)} %get-tuple-element.20.refs_0_), channel_id=1, source_target_pairs={{0,16},{4,20},{8,24},{12,28},{16,0},{20,4},{24,8},{28,12},{1,17},{... | collective-permute-start | bytes 638984 | tf_op jit(solution)/shard_map/ppermute | solution.py:393
  5.4 1.5 %collective-permute-start.1 = (bf16[416,256]{1,0:T(8,128)(2,1)}, bf16[416,256]{1,0:T(8,128)(2,1)S(1)}, u32[]{:S(2)}, u32[]{:S(2)}) collective-permute-start(bf16[416,256]{1,0:T(8,128)(2,1)} %get-tuple-element.20.refs_0_), channel_id=1, source_target_pairs={{0,8},{4,12},{8,0},{12,4},{16,24},{20,28},{24,16},{28,20},{1,9},{5... | collective-permute-start | bytes 638984 | tf_op jit(solution)/shard_map/ppermute | solution.py:393
  6.9 0.0 collective-permute-start.4
  6.9 0.3 collective-permute-start.2
  7.2 0.4 collective-permute-start
  7.6 0.7 %multiply_add_fusion.packed_ref = s32[3,256]{1,0:T(4,128)S(1)} fusion(s32[3,256]{1,0:T(4,128)} %param.12, s32[3,256]{1,0:T(4,128)} %param.11), kind=kLoop, calls=%fused_computation | loop fusion | flops 1536 | bytes 9216 | tf_op jit(solution)/shard_map/add | solution.py:127
  8.3 0.0 copy-start.3
  8.3 1.3 %copy-done.3 = bf16[384,1536]{1,0:T(8,128)(2,1)S(1)} copy-done((bf16[384,1536]{1,0:T(8,128)(2,1)S(1)}, bf16[384,1536]{1,0:T(8,128)(2,1)}, u32[]{:S(2)}) %copy-start.3) | copy-done | bytes 1179672
  9.5 0.0 copy-start
  9.5 0.0 copy-start.1
  9.5 0.0 copy-start.2
  9.5 0.0 copy-start.4
  9.6 7.1 %shard_map.95 = (bf16[8,256,1536]{2,1,0:T(8,128)(2,1)S(1)}, f8e5m2[8,256,1536]{2,1,0:T(32,128)(4,1)S(1)}) custom-call(s32[3,256]{1,0:T(4,128)S(1)} %multiply_add_fusion.packed_ref, bf16[384,1536]{1,0:T(8,128)(2,1)S(1)} %copy-done.3), custom_call_target="tpu_custom_call" | custom-call | flops 2000000000 | bytes 14000000 | tf_op jit(solution)/shard_map/pallas_call | solution.py:129
  16.7 0.0 collective-permute-done.3.refs_4_
  16.7 0.0 collective-permute-done.1.refs_2_
  16.7 0.0 collective-permute-done.4.refs_5_
  16.7 0.0 collective-permute-done.2.refs_3_
  16.7 0.0 collective-permute-done.refs_1_
  16.7 1.7 %collective-permute-start.5 = (bf16[416,256]{1,0:T(8,128)(2,1)S(1)}, bf16[416,256]{1,0:T(8,128)(2,1)S(1)}, u32[]{:S(2)}, u32[]{:S(2)}) collective-permute-start(bf16[416,256]{1,0:T(8,128)(2,1)S(1)} %collective-permute-done.1.refs_2_), channel_id=1, source_target_pairs={{0,16},{4,20},{8,24},{12,28},{16,0},{20,4},{24,8},{28,12},{1,17},{... | collective-permute-start | bytes 638984 | tf_op jit(solution)/shard_map/ppermute | solution.py:393
  18.4 1.5 %collective-permute-start.6 = (bf16[416,256]{1,0:T(8,128)(2,1)S(1)}, bf16[416,256]{1,0:T(8,128)(2,1)S(1)}, u32[]{:S(2)}, u32[]{:S(2)}) collective-permute-start(bf16[416,256]{1,0:T(8,128)(2,1)S(1)} %collective-permute-done.4.refs_5_), channel_id=1, source_target_pairs={{0,8},{4,12},{8,0},{12,4},{16,24},{20,28},{24,16},{28,20},{1,9},{5... | collective-permute-start | bytes 638984 | tf_op jit(solution)/shard_map/ppermute | solution.py:393
  19.9 0.0 copy-done
  19.9 0.0 copy-done.1
  19.9 0.0 copy-done.2
  19.9 0.0 copy-done.4
  19.9 13.3 %shard_map.97.refs_12_ = bf16[9,512,256]{2,1,0:T(8,128)(2,1)S(1)} custom-call(s32[8]{0:T(128)S(1)} %copy-done, bf16[416,256]{1,0:T(8,128)(2,1)S(1)} %copy-done.1, bf16[416,256]{1,0:T(8,128)(2,1)S(1)} %collective-permute-done.refs_1_, bf16[416,256]{1,0:T(8,128)(2,1)S(1)} %collective-permute-done.1.refs_2_, ...), custom_call_target="tpu_custom_call" | custom-call | flops 10240000000 | bytes 24000000 | tf_op jit(solution)/shard_map/pallas_call | solution.py:439
  33.2 0.0 collective-permute-done.5.refs_6_
  33.2 0.0 collective-permute-done.6.refs_7_
  33.2 28.8 %shard_map.98 = (f32[520,1024]{1,0:T(8,128)S(1)}, bf16[528,1024]{1,0:T(8,128)(2,1)S(1)}) custom-call(s32[8]{0:T(128)S(1)} %copy-done, bf16[416,256]{1,0:T(8,128)(2,1)S(1)} %copy-done.1, bf16[416,256]{1,0:T(8,128)(2,1)S(1)} %collective-permute-done.refs_1_, bf16[416,256]{1,0:T(8,128)(2,1)S(1)} %collective-permute-done.1.refs_2_, ...), custom_call_target="tpu_custom_call" | custom-call | flops 20480000000 | bytes 24000000 | tf_op jit(solution)/shard_map/pallas_call | solution.py:439
  62.1 0.0 collective-permute-start.7
  62.1 2.7 %collective-permute-done.7.theirs_ref.theirs_line_ref = bf16[528,1024]{1,0:T(8,128)(2,1)S(1)} collective-permute-done((bf16[528,1024]{1,0:T(8,128)(2,1)S(1)}, bf16[528,1024]{1,0:T(8,128)(2,1)S(1)}, u32[]{:S(2)}, u32[]{:S(2)}) %collective-permute-start.7) | collective-permute-done | bytes 1081376 | tf_op jit(solution)/shard_map/ppermute | solution.py:393
  64.8 1.5 %shard_map.99 = (f32[512,1024]{1,0:T(8,128)}, f32[1,1024]{1,0:T(1,128)}) custom-call(f32[520,1024]{1,0:T(8,128)S(1)} %get-tuple-element.28.mine_ref.mine_line_ref, bf16[528,1024]{1,0:T(8,128)(2,1)S(1)} %collective-permute-done.7.theirs_ref.theirs_line_ref, f32[520,1024]{1,0:T(8,128)S(1)} %get-tuple-element.28.mine_ref.mine_line_ref, ...), custom_call_target="tpu_custom_call" | custom-call | tf_op jit(solution)/shard_map/pallas_call | solution.py:457
Async XLA Ops:
  2.4 14.2 %collective-permute-start.3 = (bf16[416,256]{1,0:T(8,128)(2,1)}, bf16[416,256]{1,0:T(8,128)(2,1)S(1)}, u32[]{:S(2)}, u32[]{:S(2)}) collective-permute-start(bf16[416,256]{1,0:T(8,128)(2,1)} %get-tuple-element.20.refs_0_), channel_id=1, source_target_pairs={{0,16},{4,20},{8,24},{12,28},{16,0},{20,4},{24,8},{28,12},{1,17},{... | collective-permute-start | bytes 638984 | tf_op jit(solution)/shard_map/ppermute | solution.py:393
  5.4 11.3 %collective-permute-start.1 = (bf16[416,256]{1,0:T(8,128)(2,1)}, bf16[416,256]{1,0:T(8,128)(2,1)S(1)}, u32[]{:S(2)}, u32[]{:S(2)}) collective-permute-start(bf16[416,256]{1,0:T(8,128)(2,1)} %get-tuple-element.20.refs_0_), channel_id=1, source_target_pairs={{0,8},{4,12},{8,0},{12,4},{16,24},{20,28},{24,16},{28,20},{1,9},{5... | collective-permute-start | bytes 638984 | tf_op jit(solution)/shard_map/ppermute | solution.py:393
  6.9 9.8 %collective-permute-start.4 = (bf16[416,256]{1,0:T(8,128)(2,1)}, bf16[416,256]{1,0:T(8,128)(2,1)S(1)}, u32[]{:S(2)}, u32[]{:S(2)}) collective-permute-start(bf16[416,256]{1,0:T(8,128)(2,1)} %get-tuple-element.19), channel_id=1, source_target_pairs={{0,20},{4,16},{8,28},{12,24},{16,4},{20,0},{24,12},{28,8},{1,21},{... | collective-permute-start | bytes 638984 | tf_op jit(solution)/shard_map/ppermute | solution.py:393
  6.9 9.8 %collective-permute-start.2 = (bf16[416,256]{1,0:T(8,128)(2,1)}, bf16[416,256]{1,0:T(8,128)(2,1)S(1)}, u32[]{:S(2)}, u32[]{:S(2)}) collective-permute-start(bf16[416,256]{1,0:T(8,128)(2,1)} %get-tuple-element.19), channel_id=1, source_target_pairs={{0,12},{4,8},{8,4},{12,0},{16,28},{20,24},{24,20},{28,16},{1,13},{... | collective-permute-start | bytes 638984 | tf_op jit(solution)/shard_map/ppermute | solution.py:393
  7.2 9.5 %collective-permute-start = (bf16[416,256]{1,0:T(8,128)(2,1)}, bf16[416,256]{1,0:T(8,128)(2,1)S(1)}, u32[]{:S(2)}, u32[]{:S(2)}) collective-permute-start(bf16[416,256]{1,0:T(8,128)(2,1)} %get-tuple-element.19), channel_id=1, source_target_pairs={{0,4},{4,0},{8,12},{12,8},{16,20},{20,16},{24,28},{28,24},{1,5},{5... | collective-permute-start | bytes 638984 | tf_op jit(solution)/shard_map/ppermute | solution.py:393
  8.3 1.3 %copy-start.3 = (bf16[384,1536]{1,0:T(8,128)(2,1)S(1)}, bf16[384,1536]{1,0:T(8,128)(2,1)}, u32[]{:S(2)}) copy-start(bf16[384,1536]{1,0:T(8,128)(2,1)} %constant.8.clone.turns_ref) | copy-start | bytes 3538948
  9.5 10.4 %copy-start = (s32[8]{0:T(128)S(1)}, s32[8]{0:T(128)}, u32[]{:S(2)}) copy-start(s32[8]{0:T(128)} %counts_ref.5) | copy-start | bytes 100
  9.5 10.4 %copy-start.1 = (bf16[416,256]{1,0:T(8,128)(2,1)S(1)}, bf16[416,256]{1,0:T(8,128)(2,1)}, u32[]{:S(2)}) copy-start(bf16[416,256]{1,0:T(8,128)(2,1)} %get-tuple-element.20.refs_0_) | copy-start | bytes 638980
  9.5 10.4 %copy-start.2 = (bf16[7,512,512]{2,1,0:T(8,128)(2,1)S(1)}, bf16[7,512,512]{2,1,0:T(8,128)(2,1)}, u32[]{:S(2)}) copy-start(bf16[7,512,512]{2,1,0:T(8,128)(2,1)} %constant.10.clone.refs_9_.refs_11_) | copy-start | bytes 11010052
  9.5 10.4 %copy-start.4 = (bf16[256,512]{1,0:T(8,128)(2,1)S(1)}, bf16[256,512]{1,0:T(8,128)(2,1)}, u32[]{:S(2)}) copy-start(bf16[256,512]{1,0:T(8,128)(2,1)} %constant.9.clone.refs_8_.refs_10_) | copy-start | bytes 786436
  16.7 16.5 %collective-permute-start.5 = (bf16[416,256]{1,0:T(8,128)(2,1)S(1)}, bf16[416,256]{1,0:T(8,128)(2,1)S(1)}, u32[]{:S(2)}, u32[]{:S(2)}) collective-permute-start(bf16[416,256]{1,0:T(8,128)(2,1)S(1)} %collective-permute-done.1.refs_2_), channel_id=1, source_target_pairs={{0,16},{4,20},{8,24},{12,28},{16,0},{20,4},{24,8},{28,12},{1,17},{... | collective-permute-start | bytes 638984 | tf_op jit(solution)/shard_map/ppermute | solution.py:393
  18.4 14.8 %collective-permute-start.6 = (bf16[416,256]{1,0:T(8,128)(2,1)S(1)}, bf16[416,256]{1,0:T(8,128)(2,1)S(1)}, u32[]{:S(2)}, u32[]{:S(2)}) collective-permute-start(bf16[416,256]{1,0:T(8,128)(2,1)S(1)} %collective-permute-done.4.refs_5_), channel_id=1, source_target_pairs={{0,8},{4,12},{8,0},{12,4},{16,24},{20,28},{24,16},{28,20},{1,9},{5... | collective-permute-start | bytes 638984 | tf_op jit(solution)/shard_map/ppermute | solution.py:393
  62.1 2.7 %collective-permute-start.7 = (bf16[528,1024]{1,0:T(8,128)(2,1)S(1)}, bf16[528,1024]{1,0:T(8,128)(2,1)S(1)}, u32[]{:S(2)}, u32[]{:S(2)}) collective-permute-start(bf16[528,1024]{1,0:T(8,128)(2,1)S(1)} %get-tuple-element.29), channel_id=1, source_target_pairs={{0,4},{4,0},{8,12},{12,8},{16,20},{20,16},{24,28},{28,24},{1,5},{5... | collective-permute-start | bytes 3244040 | tf_op jit(solution)/shard_map/ppermute | solution.py:393

commit v8 on v7

--- a/solution.py
+++ b/solution.py
@@ -20,11 +20,11 @@
 VMEM_BYTES = 25 * 1024 * 1024
 
 
-def three_terms(tables):
+def two_terms(tables):
     terms = []
     for table in tables:
         rest = table.astype(np.float32)
-        for _ in range(3):
+        for _ in range(2):
             part = rest.astype(jnp.bfloat16)
             terms.append(part)
             rest = rest - part.astype(np.float32)
@@ -43,8 +43,8 @@
         low * starts[None, :] % SK * (2.0 * np.pi / SK),
         high * starts[None, :] % RADIX * (2.0 * np.pi / RADIX),
     ]
-    pairs = [three_terms([np.cos(angle), -np.sin(angle)]) for angle in angles]
-    high_part = np.pad(pairs[2], ((0, 0), (0, 6 * HALF)))
+    pairs = [two_terms([np.cos(angle), -np.sin(angle)]) for angle in angles]
+    high_part = np.pad(pairs[2], ((0, 0), (0, 4 * HALF)))
     return np.concatenate([np.concatenate(pairs[:2], axis=1), high_part], axis=0)
 
 
@@ -83,8 +83,8 @@
     blank = jnp.zeros((8 - sketches, features_in), jnp.float32)
     columns = jnp.concatenate([packed_ref[...].astype(jnp.float32), blank], axis=0).T
 
-    def three(full, at):
-        return full[:, at : at + HALF] + full[:, at + HALF : at + 2 * HALF] + full[:, at + 2 * HALF : at + 3 * HALF]
+    def join(full, at):
+        return full[:, at : at + HALF] + full[:, at + HALF : at + 2 * HALF]
 
     chunk = 64
     for k in range(sketches):
@@ -94,11 +94,11 @@
         lane = lax.broadcasted_iota(jnp.int32, (features_in, WIDE), 1)
         chosen = jnp.where(bucket % WIDE == lane, 1.0, 0.0).astype(jnp.bfloat16)
         full = jnp.dot(chosen, turns_ref[:WIDE, :], preferred_element_type=jnp.float32)
-        base_re, base_im, fine_re, fine_im = [three(full, 3 * i * HALF) for i in range(4)]
+        base_re, base_im, fine_re, fine_im = [join(full, 2 * i * HALF) for i in range(4)]
         lane = lax.broadcasted_iota(jnp.int32, (features_in, HALF), 1)
         chosen = jnp.where(bucket // WIDE == lane, 1.0, 0.0).astype(jnp.bfloat16)
-        full = jnp.dot(chosen, turns_ref[WIDE:, : 6 * HALF], preferred_element_type=jnp.float32)
-        wide_re, wide_im = three(full, 0), three(full, 3 * HALF)
+        full = jnp.dot(chosen, turns_ref[WIDE:, : 4 * HALF], preferred_element_type=jnp.float32)
+        wide_re, wide_im = join(full, 0), join(full, 2 * HALF)
         turns_re = (fine_re * wide_re - fine_im * wide_im) * sign
         turns_im = (fine_re * wide_im + fine_im * wide_re) * sign
         middle = sign * (1 - 2 * (bucket % 2)).astype(jnp.float32)

time: 66.5 us -> 66 us (level)
  transfers between devices with their start and end apart: 8 -> 8, of which waited for: 1 -> 1; matrix products, arithmetic and copies ran while one was open for 1% -> 1% of each run, Pallas kernels for 31% -> 30%
where the time goes in v8:
time: 66 us; the launch traced here: 65.8 us
  Pallas kernels  52.2 us (79%)
  starting transfers between devices  8.3 us (13%)
  waiting for transfers between devices  2.74 us (4%)
  local copies, waits for them, and re-layouts  1.15 us (2%)
  between operations  0.72 us (1%)
  other arithmetic  0.71 us (1%)
    pallas_call x2, Pallas kernels, transform(): pl.pallas_call(functools.partial(main_kernel, deltas, begin, final), out_...  42.2 us
    ppermute x8, starting transfers between devices, swap(): return lax.ppermute(block, 'dp', [(i, i ^ bit) for i in range(n_dp)])  8.3 us
    pallas_call x1, Pallas kernels, forward_tables(): pl.pallas_call(table_kernel, out_shape=(jax.ShapeDtypeStruct(shape, jnp.b...  6.72 us
    ppermute x8, waiting for transfers between devices, swap(): return lax.ppermute(block, 'dp', [(i, i ^ bit) for i in range(n_dp)])  2.74 us
    pallas_call x1, Pallas kernels, body(): pl.pallas_call(prepare_kernel, out_shape=(message, message), in_specs=sca...  1.82 us
    pallas_call x1, Pallas kernels, body(): pl.pallas_call(functools.partial(merge_kernel, total), grid=(parts,), out...  1.45 us
  transfers between devices with their start and end apart: 8, of which 1 were waited for; matrix products, arithmetic and copies ran while one was open for 1% of the time, Pallas kernels for 30%

profile of v8, /device:TPU:0, one launch (start us, length us, event | category | flops | bytes accessed | tf_op | source)
XLA Modules:
  0.0 65.8 jit_solution(11139050453960424646)
XLA Ops:
  0.6 1.8 %shard_map.96 = (bf16[416,256]{1,0:T(8,128)(2,1)}, bf16[416,256]{1,0:T(8,128)(2,1)}) custom-call(s32[8]{0:T(128)} %counts_ref.5, bf16[768,256]{1,0:T(8,128)(2,1)} %samples_ref.1, bf16[768]{0:T(1024)(128)(2,1)} %targets_ref.1), custom_call_target="tpu_custom_call" | custom-call | tf_op jit(solution)/shard_map/pallas_call | solution.py:385
  2.4 3.0 %collective-permute-start.3 = (bf16[416,256]{1,0:T(8,128)(2,1)}, bf16[416,256]{1,0:T(8,128)(2,1)S(1)}, u32[]{:S(2)}, u32[]{:S(2)}) collective-permute-start(bf16[416,256]{1,0:T(8,128)(2,1)} %get-tuple-element.20.refs_0_), channel_id=1, source_target_pairs={{0,16},{4,20},{8,24},{12,28},{16,0},{20,4},{24,8},{28,12},{1,17},{... | collective-permute-start | bytes 638984 | tf_op jit(solution)/shard_map/ppermute | solution.py:393
  5.4 1.5 %collective-permute-start.1 = (bf16[416,256]{1,0:T(8,128)(2,1)}, bf16[416,256]{1,0:T(8,128)(2,1)S(1)}, u32[]{:S(2)}, u32[]{:S(2)}) collective-permute-start(bf16[416,256]{1,0:T(8,128)(2,1)} %get-tuple-element.20.refs_0_), channel_id=1, source_target_pairs={{0,8},{4,12},{8,0},{12,4},{16,24},{20,28},{24,16},{28,20},{1,9},{5... | collective-permute-start | bytes 638984 | tf_op jit(solution)/shard_map/ppermute | solution.py:393
  6.9 0.0 collective-permute-start.4
  6.9 0.3 collective-permute-start.2
  7.2 0.4 collective-permute-start
  7.6 0.7 %multiply_add_fusion.packed_ref = s32[3,256]{1,0:T(4,128)S(1)} fusion(s32[3,256]{1,0:T(4,128)} %param.12, s32[3,256]{1,0:T(4,128)} %param.11), kind=kLoop, calls=%fused_computation | loop fusion | flops 1536 | bytes 9216 | tf_op jit(solution)/shard_map/add | solution.py:127
  8.3 0.0 copy-start.3
  8.3 1.1 %copy-done.3 = bf16[384,1024]{1,0:T(8,128)(2,1)S(1)} copy-done((bf16[384,1024]{1,0:T(8,128)(2,1)S(1)}, bf16[384,1024]{1,0:T(8,128)(2,1)}, u32[]{:S(2)}) %copy-start.3) | copy-done | bytes 786456
  9.4 0.0 copy-start
  9.4 0.0 copy-start.1
  9.4 0.0 copy-start.2
  9.4 0.0 copy-start.4
  9.4 6.7 %shard_map.95 = (bf16[8,256,1536]{2,1,0:T(8,128)(2,1)S(1)}, f8e5m2[8,256,1536]{2,1,0:T(32,128)(4,1)S(1)}) custom-call(s32[3,256]{1,0:T(4,128)S(1)} %multiply_add_fusion.packed_ref, bf16[384,1024]{1,0:T(8,128)(2,1)S(1)} %copy-done.3), custom_call_target="tpu_custom_call" | custom-call | flops 2000000000 | bytes 14000000 | tf_op jit(solution)/shard_map/pallas_call | solution.py:129
  16.1 0.0 collective-permute-done.3.refs_4_
  16.2 0.0 collective-permute-done.1.refs_2_
  16.2 0.0 collective-permute-done.4.refs_5_
  16.2 0.0 collective-permute-done.2.refs_3_
  16.2 0.0 collective-permute-done.refs_1_
  16.2 1.7 %collective-permute-start.5 = (bf16[416,256]{1,0:T(8,128)(2,1)S(1)}, bf16[416,256]{1,0:T(8,128)(2,1)S(1)}, u32[]{:S(2)}, u32[]{:S(2)}) collective-permute-start(bf16[416,256]{1,0:T(8,128)(2,1)S(1)} %collective-permute-done.1.refs_2_), channel_id=1, source_target_pairs={{0,16},{4,20},{8,24},{12,28},{16,0},{20,4},{24,8},{28,12},{1,17},{... | collective-permute-start | bytes 638984 | tf_op jit(solution)/shard_map/ppermute | solution.py:393
  17.9 1.5 %collective-permute-start.6 = (bf16[416,256]{1,0:T(8,128)(2,1)S(1)}, bf16[416,256]{1,0:T(8,128)(2,1)S(1)}, u32[]{:S(2)}, u32[]{:S(2)}) collective-permute-start(bf16[416,256]{1,0:T(8,128)(2,1)S(1)} %collective-permute-done.4.refs_5_), channel_id=1, source_target_pairs={{0,8},{4,12},{8,0},{12,4},{16,24},{20,28},{24,16},{28,20},{1,9},{5... | collective-permute-start | bytes 638984 | tf_op jit(solution)/shard_map/ppermute | solution.py:393
  19.4 0.0 copy-done
  19.4 0.0 copy-done.1
  19.4 0.0 copy-done.2
  19.4 0.0 copy-done.4
  19.4 13.3 %shard_map.97.refs_12_ = bf16[9,512,256]{2,1,0:T(8,128)(2,1)S(1)} custom-call(s32[8]{0:T(128)S(1)} %copy-done, bf16[416,256]{1,0:T(8,128)(2,1)S(1)} %copy-done.1, bf16[416,256]{1,0:T(8,128)(2,1)S(1)} %collective-permute-done.refs_1_, bf16[416,256]{1,0:T(8,128)(2,1)S(1)} %collective-permute-done.1.refs_2_, ...), custom_call_target="tpu_custom_call" | custom-call | flops 10240000000 | bytes 24000000 | tf_op jit(solution)/shard_map/pallas_call | solution.py:439
  32.7 0.0 collective-permute-done.5.refs_6_
  32.8 0.0 collective-permute-done.6.refs_7_
  32.8 28.8 %shard_map.98 = (f32[520,1024]{1,0:T(8,128)S(1)}, bf16[528,1024]{1,0:T(8,128)(2,1)S(1)}) custom-call(s32[8]{0:T(128)S(1)} %copy-done, bf16[416,256]{1,0:T(8,128)(2,1)S(1)} %copy-done.1, bf16[416,256]{1,0:T(8,128)(2,1)S(1)} %collective-permute-done.refs_1_, bf16[416,256]{1,0:T(8,128)(2,1)S(1)} %collective-permute-done.1.refs_2_, ...), custom_call_target="tpu_custom_call" | custom-call | flops 20480000000 | bytes 24000000 | tf_op jit(solution)/shard_map/pallas_call | solution.py:439
  61.6 0.0 collective-permute-start.7
  61.6 2.7 %collective-permute-done.7.theirs_ref.theirs_line_ref = bf16[528,1024]{1,0:T(8,128)(2,1)S(1)} collective-permute-done((bf16[528,1024]{1,0:T(8,128)(2,1)S(1)}, bf16[528,1024]{1,0:T(8,128)(2,1)S(1)}, u32[]{:S(2)}, u32[]{:S(2)}) %collective-permute-start.7) | collective-permute-done | bytes 1081376 | tf_op jit(solution)/shard_map/ppermute | solution.py:393
  64.3 1.5 %shard_map.99 = (f32[512,1024]{1,0:T(8,128)}, f32[1,1024]{1,0:T(1,128)}) custom-call(f32[520,1024]{1,0:T(8,128)S(1)} %get-tuple-element.28.mine_ref.mine_line_ref, bf16[528,1024]{1,0:T(8,128)(2,1)S(1)} %collective-permute-done.7.theirs_ref.theirs_line_ref, f32[520,1024]{1,0:T(8,128)S(1)} %get-tuple-element.28.mine_ref.mine_line_ref, ...), custom_call_target="tpu_custom_call" | custom-call | tf_op jit(solution)/shard_map/pallas_call | solution.py:457
Async XLA Ops:
  2.4 13.7 %collective-permute-start.3 = (bf16[416,256]{1,0:T(8,128)(2,1)}, bf16[416,256]{1,0:T(8,128)(2,1)S(1)}, u32[]{:S(2)}, u32[]{:S(2)}) collective-permute-start(bf16[416,256]{1,0:T(8,128)(2,1)} %get-tuple-element.20.refs_0_), channel_id=1, source_target_pairs={{0,16},{4,20},{8,24},{12,28},{16,0},{20,4},{24,8},{28,12},{1,17},{... | collective-permute-start | bytes 638984 | tf_op jit(solution)/shard_map/ppermute | solution.py:393
  5.4 10.7 %collective-permute-start.1 = (bf16[416,256]{1,0:T(8,128)(2,1)}, bf16[416,256]{1,0:T(8,128)(2,1)S(1)}, u32[]{:S(2)}, u32[]{:S(2)}) collective-permute-start(bf16[416,256]{1,0:T(8,128)(2,1)} %get-tuple-element.20.refs_0_), channel_id=1, source_target_pairs={{0,8},{4,12},{8,0},{12,4},{16,24},{20,28},{24,16},{28,20},{1,9},{5... | collective-permute-start | bytes 638984 | tf_op jit(solution)/shard_map/ppermute | solution.py:393
  6.9 9.3 %collective-permute-start.4 = (bf16[416,256]{1,0:T(8,128)(2,1)}, bf16[416,256]{1,0:T(8,128)(2,1)S(1)}, u32[]{:S(2)}, u32[]{:S(2)}) collective-permute-start(bf16[416,256]{1,0:T(8,128)(2,1)} %get-tuple-element.19), channel_id=1, source_target_pairs={{0,20},{4,16},{8,28},{12,24},{16,4},{20,0},{24,12},{28,8},{1,21},{... | collective-permute-start | bytes 638984 | tf_op jit(solution)/shard_map/ppermute | solution.py:393
  6.9 9.3 %collective-permute-start.2 = (bf16[416,256]{1,0:T(8,128)(2,1)}, bf16[416,256]{1,0:T(8,128)(2,1)S(1)}, u32[]{:S(2)}, u32[]{:S(2)}) collective-permute-start(bf16[416,256]{1,0:T(8,128)(2,1)} %get-tuple-element.19), channel_id=1, source_target_pairs={{0,12},{4,8},{8,4},{12,0},{16,28},{20,24},{24,20},{28,16},{1,13},{... | collective-permute-start | bytes 638984 | tf_op jit(solution)/shard_map/ppermute | solution.py:393
  7.2 9.0 %collective-permute-start = (bf16[416,256]{1,0:T(8,128)(2,1)}, bf16[416,256]{1,0:T(8,128)(2,1)S(1)}, u32[]{:S(2)}, u32[]{:S(2)}) collective-permute-start(bf16[416,256]{1,0:T(8,128)(2,1)} %get-tuple-element.19), channel_id=1, source_target_pairs={{0,4},{4,0},{8,12},{12,8},{16,20},{20,16},{24,28},{28,24},{1,5},{5... | collective-permute-start | bytes 638984 | tf_op jit(solution)/shard_map/ppermute | solution.py:393
  8.3 1.1 %copy-start.3 = (bf16[384,1024]{1,0:T(8,128)(2,1)S(1)}, bf16[384,1024]{1,0:T(8,128)(2,1)}, u32[]{:S(2)}) copy-start(bf16[384,1024]{1,0:T(8,128)(2,1)} %constant.8.clone.turns_ref) | copy-start | bytes 2359300
  9.4 10.0 %copy-start = (s32[8]{0:T(128)S(1)}, s32[8]{0:T(128)}, u32[]{:S(2)}) copy-start(s32[8]{0:T(128)} %counts_ref.5) | copy-start | bytes 100
  9.4 10.0 %copy-start.1 = (bf16[416,256]{1,0:T(8,128)(2,1)S(1)}, bf16[416,256]{1,0:T(8,128)(2,1)}, u32[]{:S(2)}) copy-start(bf16[416,256]{1,0:T(8,128)(2,1)} %get-tuple-element.20.refs_0_) | copy-start | bytes 638980
  9.4 10.0 %copy-start.2 = (bf16[7,512,512]{2,1,0:T(8,128)(2,1)S(1)}, bf16[7,512,512]{2,1,0:T(8,128)(2,1)}, u32[]{:S(2)}) copy-start(bf16[7,512,512]{2,1,0:T(8,128)(2,1)} %constant.10.clone.refs_9_.refs_11_) | copy-start | bytes 11010052
  9.4 10.0 %copy-start.4 = (bf16[256,512]{1,0:T(8,128)(2,1)S(1)}, bf16[256,512]{1,0:T(8,128)(2,1)}, u32[]{:S(2)}) copy-start(bf16[256,512]{1,0:T(8,128)(2,1)} %constant.9.clone.refs_8_.refs_10_) | copy-start | bytes 786436
  16.2 16.6 %collective-permute-start.5 = (bf16[416,256]{1,0:T(8,128)(2,1)S(1)}, bf16[416,256]{1,0:T(8,128)(2,1)S(1)}, u32[]{:S(2)}, u32[]{:S(2)}) collective-permute-start(bf16[416,256]{1,0:T(8,128)(2,1)S(1)} %collective-permute-done.1.refs_2_), channel_id=1, source_target_pairs={{0,16},{4,20},{8,24},{12,28},{16,0},{20,4},{24,8},{28,12},{1,17},{... | collective-permute-start | bytes 638984 | tf_op jit(solution)/shard_map/ppermute | solution.py:393
  17.9 14.9 %collective-permute-start.6 = (bf16[416,256]{1,0:T(8,128)(2,1)S(1)}, bf16[416,256]{1,0:T(8,128)(2,1)S(1)}, u32[]{:S(2)}, u32[]{:S(2)}) collective-permute-start(bf16[416,256]{1,0:T(8,128)(2,1)S(1)} %collective-permute-done.4.refs_5_), channel_id=1, source_target_pairs={{0,8},{4,12},{8,0},{12,4},{16,24},{20,28},{24,16},{28,20},{1,9},{5... | collective-permute-start | bytes 638984 | tf_op jit(solution)/shard_map/ppermute | solution.py:393
  61.6 2.7 %collective-permute-start.7 = (bf16[528,1024]{1,0:T(8,128)(2,1)S(1)}, bf16[528,1024]{1,0:T(8,128)(2,1)S(1)}, u32[]{:S(2)}, u32[]{:S(2)}) collective-permute-start(bf16[528,1024]{1,0:T(8,128)(2,1)S(1)} %get-tuple-element.29), channel_id=1, source_target_pairs={{0,4},{4,0},{8,12},{12,8},{16,20},{20,16},{24,28},{28,24},{1,5},{5... | collective-permute-start | bytes 3244040 | tf_op jit(solution)/shard_map/ppermute | solution.py:393
